TPU v7x, 256 devices: a whole 4x4x8 slice. The times are simulated.
256 devices in a mesh: doc: 16 (over z_hi, x, core), seq: 16 (over z_lo, y).
Axes of the slice: x: 4, y: 4, z: 8 (z_hi: 2, z_lo: 4; z = z_hi * 4 + z_lo), core: 2. Of those that a mesh axis runs over, the one named last changes fastest.
Arguments:
- queries: bfloat16 [16, 2048, 2048], P('doc', 'seq'), may hold values from -6 to 6
- keys: bfloat16 [16, 2048, 512], P('doc', 'seq'), may hold values from -6 to 6
- values: bfloat16 [16, 2048, 512], P('doc', 'seq'), may hold values from -6 to 6
- outputs: bfloat16 [16, 2048, 2048], P('doc', 'seq'), may hold values from -1.5 to 1.5
- out_grads: bfloat16 [16, 2048, 2048], P('doc', 'seq'), may hold values from -6 to 6
- lengths: int32 [16, 16, 16], P('doc', 'seq'), may hold values from 1 to 16, 128 in all within a row
- owners: int32 [16, 16, 16], P('doc', 'seq'), may hold values from 0 to 15, each once within a row
Outputs:
- returned: bfloat16 [16, 16, 16, 16, 3072], P('doc', 'seq')
Inputs may be any that keep to these rules, and one draw needn't show every extreme that they name: Within each block of 128 positions the 16 lengths sum to 128, and the longest is exactly 16. Within each block the 16 child summaries have 16 different owners.
All inputs are finite; a program needn't handle non-finite values.
Results may differ from a plain program's by a relative error of at most 0.0095.
Values may be sent and summed in bfloat16 or wider, within the bound.
No kernel may reach another device: no remote copies, remote signals or barrier semaphores. Data moves between devices by JAX's collectives and lax.ppermute only.
A program may use at most 64 MiB of HBM per device.

v0:
```python
import jax
import jax.numpy as jnp
import numpy as np
from jax import lax
from jax.sharding import PartitionSpec as P

HD = 128
QH = 16
KVH = 4


def head_grads(query_rows, key_rows, value_rows, grad_out, row_terms):
    length = query_rows.shape[0]
    head_dim = query_rows.shape[1]
    blocks = 1
    while blocks < 8 and length // (blocks * 2) >= 512:
        blocks = blocks * 2
    block_rows = length // blocks
    factor = head_dim ** (-0.5)
    key_acc = jnp.zeros((length, head_dim), jnp.float32)
    value_acc = jnp.zeros((length, head_dim), jnp.float32)
    pieces = []
    for block_id in range(blocks):
        first = block_id * block_rows
        key_end = first + block_rows
        query_blk = query_rows[first:key_end]
        grad_blk = grad_out[first:key_end]
        key_seen = key_rows[:key_end]
        value_seen = value_rows[:key_end]
        score = (
            lax.dot_general(
                query_blk, key_seen, (((1,), (1,)), ((), ())), preferred_element_type=jnp.float32
            )
            * factor
        )
        causal = jnp.arange(key_end)[None, :] <= (first + jnp.arange(block_rows))[:, None]
        score = jnp.where(causal, score, -jnp.inf)
        row_max = jnp.max(score, axis=1, keepdims=True)
        weight = jnp.exp(score - row_max)
        attn_prob = weight / jnp.sum(weight, axis=1, keepdims=True)
        attn_low = attn_prob.astype(jnp.bfloat16)
        grad_prob = lax.dot_general(
            grad_blk, value_seen, (((1,), (1,)), ((), ())), preferred_element_type=jnp.float32
        )
        grad_score = (attn_prob * (grad_prob - row_terms[first:key_end][:, None])).astype(
            jnp.bfloat16
        )
        pieces.append(
            (jnp.dot(grad_score, key_seen, preferred_element_type=jnp.float32) * factor).astype(
                jnp.bfloat16
            )
        )
        key_part = lax.dot_general(
            grad_score, query_blk, (((0,), (0,)), ((), ())), preferred_element_type=jnp.float32
        )
        value_part = lax.dot_general(
            attn_low, grad_blk, (((0,), (0,)), ((), ())), preferred_element_type=jnp.float32
        )
        missing = length - key_end
        key_acc = key_acc + jnp.pad(key_part, ((0, missing), (0, 0)))
        value_acc = value_acc + jnp.pad(value_part, ((0, missing), (0, 0)))
    return (
        jnp.concatenate(pieces, axis=0),
        (key_acc * factor).astype(jnp.bfloat16),
        value_acc.astype(jnp.bfloat16),
    )


def route(grad_rows, child_lens, child_owner, doc_devs, capacity):
    child_start = jnp.cumsum(child_lens) - child_lens
    owned = child_owner[None, :] == jnp.arange(doc_devs, dtype=jnp.int32)[:, None]
    start_of = jnp.sum(jnp.where(owned, child_start[None, :], 0), axis=1)
    len_of = jnp.sum(jnp.where(owned, child_lens[None, :], 0), axis=1)
    slot_ids = jnp.arange(capacity, dtype=jnp.int32)
    filled = slot_ids[None, :] < len_of[:, None]
    row_ids = jnp.where(filled, start_of[:, None] + slot_ids[None, :], 0)
    picked = jnp.take(grad_rows, row_ids.reshape(-1), axis=0).reshape(
        doc_devs, capacity, grad_rows.shape[1]
    )
    return jnp.where(filled[:, :, None], picked, jnp.zeros_like(picked))


def body(queries, keys, values, outputs, out_grads, lengths, owners):
    seq_devs = lax.axis_size("seq")
    doc_devs = lax.axis_size("doc")
    tok_rows = queries.shape[1]
    heads_here = QH // seq_devs
    group = QH // KVH
    capacity = 2 * tok_rows // doc_devs
    slots = np.arange(QH) // group
    query_split = queries[0].reshape(tok_rows, seq_devs, heads_here, HD)
    key_split = (
        keys[0].reshape(tok_rows, KVH, HD)[:, slots].reshape(tok_rows, seq_devs, heads_here, HD)
    )
    value_split = (
        values[0].reshape(tok_rows, KVH, HD)[:, slots].reshape(tok_rows, seq_devs, heads_here, HD)
    )
    grad_split = out_grads[0].reshape(tok_rows, seq_devs, heads_here, HD)
    output_split = outputs[0].reshape(tok_rows, seq_devs, heads_here, HD)
    query_in, key_in, value_in, grad_in, output_in = (
        lax.all_to_all(query_split, "seq", split_axis=1, concat_axis=0, tiled=True),
        lax.all_to_all(key_split, "seq", split_axis=1, concat_axis=0, tiled=True),
        lax.all_to_all(value_split, "seq", split_axis=1, concat_axis=0, tiled=True),
        lax.all_to_all(grad_split, "seq", split_axis=1, concat_axis=0, tiled=True),
        lax.all_to_all(output_split, "seq", split_axis=1, concat_axis=0, tiled=True),
    )
    row_terms = jnp.sum(grad_in.astype(jnp.float32) * output_in.astype(jnp.float32), axis=3)[:, 0]
    results = [
        head_grads(
            query_in[:, 0, 0], key_in[:, 0, 0], value_in[:, 0, 0], grad_in[:, 0, 0], row_terms[:, 0]
        )
    ]
    query_grad = jnp.stack([item[0] for item in results], axis=1)
    key_parts = jnp.stack([item[1] for item in results], axis=1)
    value_parts = jnp.stack([item[2] for item in results], axis=1)
    back_query, back_key, back_value = (
        lax.all_to_all(query_grad[:, None], "seq", split_axis=0, concat_axis=1, tiled=True),
        lax.all_to_all(key_parts[:, None], "seq", split_axis=0, concat_axis=1, tiled=True),
        lax.all_to_all(value_parts[:, None], "seq", split_axis=0, concat_axis=1, tiled=True),
    )
    key_grad = jnp.sum(
        back_key.reshape(tok_rows, KVH, group, HD).astype(jnp.float32), axis=2
    ).astype(jnp.bfloat16)
    value_grad = jnp.sum(
        back_value.reshape(tok_rows, KVH, group, HD).astype(jnp.float32), axis=2
    ).astype(jnp.bfloat16)
    grad_rows = jnp.concatenate(
        [
            back_query.reshape(tok_rows, QH * HD),
            key_grad.reshape(tok_rows, KVH * HD),
            value_grad.reshape(tok_rows, KVH * HD),
        ],
        axis=1,
    )
    outgoing = route(grad_rows, lengths[0, 0], owners[0, 0], doc_devs, capacity)
    incoming = lax.all_to_all(outgoing, "doc", split_axis=0, concat_axis=0, tiled=True)
    return incoming[None, None]


def solution(mesh):
    return jax.shard_map(
        body,
        mesh=mesh,
        in_specs=(
            P("doc", "seq", None),
            P("doc", "seq", None),
            P("doc", "seq", None),
            P("doc", "seq", None),
            P("doc", "seq", None),
            P("doc", "seq", None),
            P("doc", "seq", None),
        ),
        out_specs=P("doc", "seq", None, None, None),
        check_vma=False,
    )
```

profile of v0, /device:TPU:32, one launch (start us, length us, event | category | flops | bytes accessed | tf_op | source)
XLA Modules:
  0.0 227.0 jit_solution(8832470394665084416)
XLA Ops:
  1.9 1.4 gather_fusion.1
  3.3 8.8 %all-to-all-start.2 = ((bf16[128,16,1,128]{3,0,2,1:T(8,128)(2,1)}), bf16[128,16,1,128]{3,0,2,1:T(8,128)(2,1)S(1)}, u32[]{:S(2)}, u32[]{:S(2)}) async-start(bf16[128,16,1,128]{3,0,2,1:T(8,128)(2,1)} %bitcast.19), calls=%async_computation.2 | async-start | bytes 1048576 | tf_op jit(solution)/shard_map/all_to_all | solution.py:103
  12.3 1.4 gather_fusion
  13.7 13.1 %all-to-all-done.2 = bf16[128,16,1,128]{3,0,2,1:T(8,128)(2,1)S(1)} async-done(((bf16[128,16,1,128]{3,0,2,1:T(8,128)(2,1)}), bf16[128,16,1,128]{3,0,2,1:T(8,128)(2,1)S(1)}, u32[]{:S(2)}, u32[]{:S(2)}) %all-to-all-start.2) | async-done | bytes 524320 | tf_op jit(solution)/shard_map/all_to_all | solution.py:103
  26.8 5.1 %all-to-all-start = ((bf16[128,16,1,128]{3,0,2,1:T(8,128)(2,1)}), bf16[128,16,1,128]{3,0,2,1:T(8,128)(2,1)S(1)}, u32[]{:S(2)}, u32[]{:S(2)}) async-start(bf16[128,16,1,128]{3,0,2,1:T(8,128)(2,1)} %bitcast.6), calls=%async_computation | async-start | bytes 1048576 | tf_op jit(solution)/shard_map/all_to_all | solution.py:102
  33.0 12.9 %all-to-all-done = bf16[128,16,1,128]{3,0,2,1:T(8,128)(2,1)S(1)} async-done(((bf16[128,16,1,128]{3,0,2,1:T(8,128)(2,1)}), bf16[128,16,1,128]{3,0,2,1:T(8,128)(2,1)S(1)}, u32[]{:S(2)}, u32[]{:S(2)}) %all-to-all-start) | async-done | bytes 524320 | tf_op jit(solution)/shard_map/all_to_all | solution.py:102
  45.9 5.1 %all-to-all-start.1 = ((bf16[128,16,1,128]{0,3,2,1:T(8,128)(2,1)}), bf16[128,16,1,128]{0,3,2,1:T(8,128)(2,1)S(1)}, u32[]{:S(2)}, u32[]{:S(2)}) async-start(bf16[128,16,1,128]{0,3,2,1:T(8,128)(2,1)} %bitcast.11), calls=%async_computation.1 | async-start | bytes 1048576 | tf_op jit(solution)/shard_map/all_to_all | solution.py:101
  52.0 12.6 %all-to-all-done.1 = bf16[128,16,1,128]{0,3,2,1:T(8,128)(2,1)S(1)} async-done(((bf16[128,16,1,128]{0,3,2,1:T(8,128)(2,1)}), bf16[128,16,1,128]{0,3,2,1:T(8,128)(2,1)S(1)}, u32[]{:S(2)}, u32[]{:S(2)}) %all-to-all-start.1) | async-done | bytes 524320 | tf_op jit(solution)/shard_map/all_to_all | solution.py:101
  64.6 5.1 %all-to-all-start.4 = ((bf16[128,16,1,128]{0,3,2,1:T(8,128)(2,1)}), bf16[128,16,1,128]{0,3,2,1:T(8,128)(2,1)S(1)}, u32[]{:S(2)}, u32[]{:S(2)}) async-start(bf16[128,16,1,128]{0,3,2,1:T(8,128)(2,1)} %bitcast.30), calls=%async_computation.4 | async-start | bytes 1048576 | tf_op jit(solution)/shard_map/all_to_all | solution.py:105
  70.7 12.3 %all-to-all-done.4 = bf16[128,16,1,128]{0,3,2,1:T(8,128)(2,1)S(1)} async-done(((bf16[128,16,1,128]{0,3,2,1:T(8,128)(2,1)}), bf16[128,16,1,128]{0,3,2,1:T(8,128)(2,1)S(1)}, u32[]{:S(2)}, u32[]{:S(2)}) %all-to-all-start.4) | async-done | bytes 524320 | tf_op jit(solution)/shard_map/all_to_all | solution.py:105
  83.1 5.1 %all-to-all-start.3 = ((bf16[128,16,1,128]{0,3,2,1:T(8,128)(2,1)}), bf16[128,16,1,128]{0,3,2,1:T(8,128)(2,1)S(1)}, u32[]{:S(2)}, u32[]{:S(2)}) async-start(bf16[128,16,1,128]{0,3,2,1:T(8,128)(2,1)} %bitcast.24), calls=%async_computation.3 | async-start | bytes 1048576 | tf_op jit(solution)/shard_map/all_to_all | solution.py:104
  95.1 6.5 %all-to-all-done.3 = bf16[128,16,1,128]{0,3,2,1:T(8,128)(2,1)S(1)} async-done(((bf16[128,16,1,128]{0,3,2,1:T(8,128)(2,1)}), bf16[128,16,1,128]{0,3,2,1:T(8,128)(2,1)S(1)}, u32[]{:S(2)}, u32[]{:S(2)}) %all-to-all-start.3) | async-done | bytes 524320 | tf_op jit(solution)/shard_map/all_to_all | solution.py:104
  111.8 1.3 copy-done
  116.6 5.1 %all-to-all-start.7 = ((bf16[16,2,8192]{2,1,0:T(2,128)(2,1)}), bf16[16,2,8192]{2,1,0:T(2,128)(2,1)S(1)}, u32[]{:S(2)}, u32[]{:S(2)}) async-start(bf16[16,2,8192]{2,1,0:T(2,128)(2,1)} %reshape.258), calls=%async_computation.7 | async-start | bytes 1048576 | tf_op jit(solution)/shard_map/all_to_all | solution.py:119
  121.8 1.8 fusion.25
  124.9 1.9 copy-done.1
  131.8 3.3 %all-to-all-done.7 = bf16[16,2,8192]{2,1,0:T(2,128)(2,1)S(1)} async-done(((bf16[16,2,8192]{2,1,0:T(2,128)(2,1)}), bf16[16,2,8192]{2,1,0:T(2,128)(2,1)S(1)}, u32[]{:S(2)}, u32[]{:S(2)}) %all-to-all-start.7) | async-done | bytes 524320 | tf_op jit(solution)/shard_map/all_to_all | solution.py:119
  135.1 5.1 %all-to-all-start.5 = ((bf16[16,2,8192]{2,1,0:T(2,128)(2,1)}), bf16[16,2,8192]{2,1,0:T(2,128)(2,1)S(1)}, u32[]{:S(2)}, u32[]{:S(2)}) async-start(bf16[16,2,8192]{2,1,0:T(2,128)(2,1)} %reshape.262), calls=%async_computation.5 | async-start | bytes 1048576 | tf_op jit(solution)/shard_map/all_to_all | solution.py:117
  145.1 8.5 %all-to-all-done.5 = bf16[16,2,8192]{2,1,0:T(2,128)(2,1)S(1)} async-done(((bf16[16,2,8192]{2,1,0:T(2,128)(2,1)}), bf16[16,2,8192]{2,1,0:T(2,128)(2,1)S(1)}, u32[]{:S(2)}, u32[]{:S(2)}) %all-to-all-start.5) | async-done | bytes 524320 | tf_op jit(solution)/shard_map/all_to_all | solution.py:117
  153.6 5.1 %all-to-all-start.6 = ((bf16[16,2,8192]{2,1,0:T(2,128)(2,1)}), bf16[16,2,8192]{2,1,0:T(2,128)(2,1)S(1)}, u32[]{:S(2)}, u32[]{:S(2)}) async-start(bf16[16,2,8192]{2,1,0:T(2,128)(2,1)} %reshape.260), calls=%async_computation.6 | async-start | bytes 1048576 | tf_op jit(solution)/shard_map/all_to_all | solution.py:118
  160.9 11.3 %all-to-all-done.6 = bf16[16,2,8192]{2,1,0:T(2,128)(2,1)S(1)} async-done(((bf16[16,2,8192]{2,1,0:T(2,128)(2,1)}), bf16[16,2,8192]{2,1,0:T(2,128)(2,1)S(1)}, u32[]{:S(2)}, u32[]{:S(2)}) %all-to-all-start.6) | async-done | bytes 524320 | tf_op jit(solution)/shard_map/all_to_all | solution.py:118
  173.0 1.6 gather_fusion.2
  174.9 51.0 %all_to_all.119 = bf16[16,16,3072]{2,1,0:T(8,128)(2,1)S(1)} all-to-all(bf16[16,16,3072]{2,1,0:T(8,128)(2,1)S(1)} %select_select_fusion), channel_id=1, replica_groups=mesh['doc'=16,'seq'=16] {'doc'}, dimensions={0} | all-to-all | bytes 3145728 | tf_op jit(solution)/shard_map/all_to_all | solution.py:136
  225.9 1.1 copy.90
  (160 shorter events, 39.8 us)
Async XLA Ops:
  0.0 12.1 %copy-start.25 = (bf16[1,128,512]{2,1,0:T(8,128)(2,1)S(1)}, bf16[1,128,512]{2,1,0:T(8,128)(2,1)}, u32[]{:S(2)}) copy-start(bf16[1,128,512]{2,1,0:T(8,128)(2,1)} %param.11) | copy-start | bytes 393220
  3.3 28.7 %copy-start.9 = (bf16[1,128,2048]{2,1,0:T(8,128)(2,1)S(1)}, bf16[1,128,2048]{2,1,0:T(8,128)(2,1)}, u32[]{:S(2)}) copy-start(bf16[1,128,2048]{2,1,0:T(8,128)(2,1)} %param.10) | copy-start | bytes 1572868
  3.3 23.6 %all-to-all-start.2 = ((bf16[128,16,1,128]{3,0,2,1:T(8,128)(2,1)}), bf16[128,16,1,128]{3,0,2,1:T(8,128)(2,1)S(1)}, u32[]{:S(2)}, u32[]{:S(2)}) async-start(bf16[128,16,1,128]{3,0,2,1:T(8,128)(2,1)} %bitcast.19), calls=%async_computation.2 | async-start | bytes 1048576 | tf_op jit(solution)/shard_map/all_to_all | solution.py:103
  12.3 38.7 %copy-start.10 = (bf16[1,128,2048]{2,1,0:T(8,128)(2,1)S(1)}, bf16[1,128,2048]{2,1,0:T(8,128)(2,1)}, u32[]{:S(2)}) copy-start(bf16[1,128,2048]{2,1,0:T(8,128)(2,1)} %param.13) | copy-start | bytes 1572868
  26.8 19.1 %all-to-all-start = ((bf16[128,16,1,128]{3,0,2,1:T(8,128)(2,1)}), bf16[128,16,1,128]{3,0,2,1:T(8,128)(2,1)S(1)}, u32[]{:S(2)}, u32[]{:S(2)}) async-start(bf16[128,16,1,128]{3,0,2,1:T(8,128)(2,1)} %bitcast.6), calls=%async_computation | async-start | bytes 1048576 | tf_op jit(solution)/shard_map/all_to_all | solution.py:102
  32.0 37.7 %copy-start.11 = (bf16[1,128,2048]{2,1,0:T(8,128)(2,1)S(1)}, bf16[1,128,2048]{2,1,0:T(8,128)(2,1)}, u32[]{:S(2)}) copy-start(bf16[1,128,2048]{2,1,0:T(8,128)(2,1)} %param.14) | copy-start | bytes 1572868
  45.9 18.7 %all-to-all-start.1 = ((bf16[128,16,1,128]{0,3,2,1:T(8,128)(2,1)}), bf16[128,16,1,128]{0,3,2,1:T(8,128)(2,1)S(1)}, u32[]{:S(2)}, u32[]{:S(2)}) async-start(bf16[128,16,1,128]{0,3,2,1:T(8,128)(2,1)} %bitcast.11), calls=%async_computation.1 | async-start | bytes 1048576 | tf_op jit(solution)/shard_map/all_to_all | solution.py:101
  51.0 37.1 %copy-start.35 = (s32[1,1,16]{2,1,0:T(1,128)S(1)}, s32[1,1,16]{2,1,0:T(1,128)}, u32[]{:S(2)}) copy-start(s32[1,1,16]{2,1,0:T(1,128)} %param.15) | copy-start | bytes 196
  64.6 18.5 %all-to-all-start.4 = ((bf16[128,16,1,128]{0,3,2,1:T(8,128)(2,1)}), bf16[128,16,1,128]{0,3,2,1:T(8,128)(2,1)S(1)}, u32[]{:S(2)}, u32[]{:S(2)}) async-start(bf16[128,16,1,128]{0,3,2,1:T(8,128)(2,1)} %bitcast.30), calls=%async_computation.4 | async-start | bytes 1048576 | tf_op jit(solution)/shard_map/all_to_all | solution.py:105
  83.1 18.5 %all-to-all-start.3 = ((bf16[128,16,1,128]{0,3,2,1:T(8,128)(2,1)}), bf16[128,16,1,128]{0,3,2,1:T(8,128)(2,1)S(1)}, u32[]{:S(2)}, u32[]{:S(2)}) async-start(bf16[128,16,1,128]{0,3,2,1:T(8,128)(2,1)} %bitcast.24), calls=%async_computation.3 | async-start | bytes 1048576 | tf_op jit(solution)/shard_map/all_to_all | solution.py:104
  95.1 8.4 %copy-start.18 = (bf16[4,128,1,1,128]{4,1,0,3,2:T(8,128)(2,1)}, bf16[4,128,1,1,128]{4,1,0,3,2:T(8,128)(2,1)S(1)}, u32[]{:S(2)}) copy-start(bf16[4,128,1,1,128]{4,1,0,3,2:T(8,128)(2,1)S(1)} %get-tuple-element.10) | copy-start | bytes 393220
  95.1 11.4 %copy-start.16 = (bf16[4,128,1,1,128]{4,1,0,3,2:T(8,128)(2,1)}, bf16[4,128,1,1,128]{4,1,0,3,2:T(8,128)(2,1)S(1)}, u32[]{:S(2)}) copy-start(bf16[4,128,1,1,128]{4,1,0,3,2:T(8,128)(2,1)S(1)} %get-tuple-element.7) | copy-start | bytes 393220
  95.1 12.6 %copy-start.14 = (bf16[4,128,1,1,128]{4,1,0,3,2:T(8,128)(2,1)}, bf16[4,128,1,1,128]{4,1,0,3,2:T(8,128)(2,1)S(1)}, u32[]{:S(2)}) copy-start(bf16[4,128,1,1,128]{4,1,0,3,2:T(8,128)(2,1)S(1)} %get-tuple-element.9) | copy-start | bytes 393220
  95.1 15.3 %copy-start.12 = (bf16[4,128,1,1,128]{4,1,0,3,2:T(8,128)(2,1)}, bf16[4,128,1,1,128]{4,1,0,3,2:T(8,128)(2,1)S(1)}, u32[]{:S(2)}) copy-start(bf16[4,128,1,1,128]{4,1,0,3,2:T(8,128)(2,1)S(1)} %get-tuple-element.8) | copy-start | bytes 393220
  102.3 9.6 %copy-start.27 = (bf16[4,128,1,1,128]{4,1,0,3,2:T(8,128)(2,1)}, bf16[4,128,1,1,128]{4,1,0,3,2:T(8,128)(2,1)S(1)}, u32[]{:S(2)}) copy-start(bf16[4,128,1,1,128]{4,1,0,3,2:T(8,128)(2,1)S(1)} %get-tuple-element.14) | copy-start | bytes 393220
  116.6 18.5 %all-to-all-start.7 = ((bf16[16,2,8192]{2,1,0:T(2,128)(2,1)}), bf16[16,2,8192]{2,1,0:T(2,128)(2,1)S(1)}, u32[]{:S(2)}, u32[]{:S(2)}) async-start(bf16[16,2,8192]{2,1,0:T(2,128)(2,1)} %reshape.258), calls=%async_computation.7 | async-start | bytes 1048576 | tf_op jit(solution)/shard_map/all_to_all | solution.py:119
  129.8 10.4 %copy-start.17 = (bf16[4,128,1,1,128]{4,1,0,3,2:T(8,128)(2,1)S(1)}, bf16[4,128,1,1,128]{4,1,0,3,2:T(8,128)(2,1)}, u32[]{:S(2)}) copy-start(bf16[4,128,1,1,128]{4,1,0,3,2:T(8,128)(2,1)} %copy-done.16) | copy-start | bytes 393220
  129.8 10.7 %copy-start.19 = (bf16[4,128,1,1,128]{4,1,0,3,2:T(8,128)(2,1)S(1)}, bf16[4,128,1,1,128]{4,1,0,3,2:T(8,128)(2,1)}, u32[]{:S(2)}) copy-start(bf16[4,128,1,1,128]{4,1,0,3,2:T(8,128)(2,1)} %copy-done.18) | copy-start | bytes 393220
  130.9 10.1 %copy-start.15 = (bf16[4,128,1,1,128]{4,1,0,3,2:T(8,128)(2,1)S(1)}, bf16[4,128,1,1,128]{4,1,0,3,2:T(8,128)(2,1)}, u32[]{:S(2)}) copy-start(bf16[4,128,1,1,128]{4,1,0,3,2:T(8,128)(2,1)} %copy-done.14) | copy-start | bytes 393220
  135.1 18.5 %all-to-all-start.5 = ((bf16[16,2,8192]{2,1,0:T(2,128)(2,1)}), bf16[16,2,8192]{2,1,0:T(2,128)(2,1)S(1)}, u32[]{:S(2)}, u32[]{:S(2)}) async-start(bf16[16,2,8192]{2,1,0:T(2,128)(2,1)} %reshape.262), calls=%async_computation.5 | async-start | bytes 1048576 | tf_op jit(solution)/shard_map/all_to_all | solution.py:117
  143.1 15.7 %copy-start.36 = (s32[1,1,16]{2,1,0:T(1,128)S(1)}, s32[1,1,16]{2,1,0:T(1,128)}, u32[]{:S(2)}) copy-start(s32[1,1,16]{2,1,0:T(1,128)} %param.15) | copy-start | bytes 196
  143.1 15.6 %copy-start.41 = (s32[16]{0:T(128)S(1)}, s32[16]{0:T(128)}, u32[]{:S(2)}) copy-start(s32[16]{0:T(128)} %reduce.4) | copy-start | bytes 196
  143.1 15.7 %copy-start.40 = (s32[1,1,16]{2,1,0:T(1,128)S(1)}, s32[1,1,16]{2,1,0:T(1,128)}, u32[]{:S(2)}) copy-start(s32[1,1,16]{2,1,0:T(1,128)} %param.16) | copy-start | bytes 196
  153.6 18.5 %all-to-all-start.6 = ((bf16[16,2,8192]{2,1,0:T(2,128)(2,1)}), bf16[16,2,8192]{2,1,0:T(2,128)(2,1)S(1)}, u32[]{:S(2)}, u32[]{:S(2)}) async-start(bf16[16,2,8192]{2,1,0:T(2,128)(2,1)} %reshape.260), calls=%async_computation.6 | async-start | bytes 1048576 | tf_op jit(solution)/shard_map/all_to_all | solution.py:118
  (26 other events, 63.8 us)
where the time goes:
time: 228 us; the launch traced here: 227 us
  waiting for transfers between devices  80.5 us (35%)
  blocking collectives  51 us (22%)
  starting transfers between devices  44.5 us (20%)
  local copies, waits for them, and re-layouts  28.8 us (13%)
  matrix products  13.5 us (6%)
  other arithmetic  8.03 us (4%)
    all_to_all x1, blocking collectives, body(): lax.all_to_all(outgoing, 'doc', split_axis=0, concat_axis=0, tiled=True)  51 us
    unnamed x100, local copies, waits for them, and re-layouts  16.6 us
    all_to_all x1, waiting for transfers between devices, body(): lax.all_to_all(value_split, 'seq', split_axis=1, concat_axis=0, tiled=True)  13.1 us
    all_to_all x1, waiting for transfers between devices, body(): lax.all_to_all(key_split, 'seq', split_axis=1, concat_axis=0, tiled=True)  12.9 us
    all_to_all x1, waiting for transfers between devices, body(): lax.all_to_all(query_split, 'seq', split_axis=1, concat_axis=0, tiled=True)  12.6 us
    all_to_all x1, waiting for transfers between devices, body(): lax.all_to_all(output_split, 'seq', split_axis=1, concat_axis=0, tiled=True)  12.3 us
    all_to_all x1, waiting for transfers between devices, body(): lax.all_to_all(key_parts[:, None], 'seq', split_axis=0, concat_axis=1, ti...  11.3 us
    all_to_all x1, starting transfers between devices, body(): lax.all_to_all(value_split, 'seq', split_axis=1, concat_axis=0, tiled=True)  8.78 us
  transfers between devices with their start and end apart: 8, of which 8 were waited for; matrix products, arithmetic and copies ran while one was open for 11% of the time, Pallas kernels for 0%

commit v1 on v0

v1 whole, which is shorter than its diff:
```python
import functools

import jax
import jax.numpy as jnp
from jax import lax
from jax.experimental import pallas as pl
from jax.experimental.pallas import tpu as pltpu
from jax.sharding import Mesh, PartitionSpec as P

HD = 128
QH = 16
KVH = 4
GROUP = QH // KVH
TOK = 128
CAP = 16
SLOTS = 4
BLK = SLOTS * TOK
QROWS = GROUP * TOK
QD_ROWS = 2 * QROWS + 16
KV_ROWS = 2 * TOK
FACTOR = HD ** (-0.5)
LOG2E = 1.4426950408889634
f32 = jnp.float32
bf16 = jnp.bfloat16
VMEM = pl.BlockSpec(memory_space=pltpu.VMEM)
SMEM = pl.BlockSpec(memory_space=pltpu.SMEM)
PARAMS = pltpu.CompilerParams(vmem_limit_bytes=56 * 1024 * 1024)


def aligned(index, unit):
    return pl.ds(pl.multiple_of(index * unit, unit), unit)


def split_kv(at_ref, k_ref, v_ref, *outs):
    y = at_ref[0]
    for slot in range(SLOTS):
        head = aligned(lax.rem(y + slot, SLOTS), HD)
        outs[slot][:TOK, :] = k_ref[:, head]
        outs[slot][TOK:, :] = v_ref[:, head]


def split_qd(at_ref, q_ref, o_ref, g_ref, *outs):
    y = at_ref[0]
    lane = lax.broadcasted_iota(jnp.int32, (TOK, HD), 1)
    for slot in range(SLOTS):
        dest = lax.rem(y + slot, SLOTS)
        terms = jnp.zeros((TOK, HD), f32)
        for h in range(GROUP):
            head = aligned(dest * GROUP + h, HD)
            grad = g_ref[:, head]
            outs[slot][h * TOK : (h + 1) * TOK, :] = q_ref[:, head]
            outs[slot][QROWS + h * TOK : QROWS + (h + 1) * TOK, :] = grad
            term = jnp.sum(
                grad.astype(f32) * o_ref[:, head].astype(f32), axis=1, keepdims=True
            )
            terms = jnp.where(lax.rem(lane, GROUP) == h, term, terms)
        high = terms.astype(bf16).astype(f32)
        mid = (terms - high).astype(bf16).astype(f32)
        low = terms - high - mid
        part = lane // GROUP
        packed = jnp.where(
            part == 0, high, jnp.where(part == 1, mid, jnp.where(part == 2, low, 0.0))
        )
        outs[slot][2 * QROWS :, :] = packed.T[:16, :].astype(bf16)


def dot(a, b, dims):
    return lax.dot_general(a, b, (dims, ((), ())), preferred_element_type=f32)


def attention_grads(at_ref, *refs):
    qd_refs, kv_refs = refs[:4], refs[4:8]
    dq_refs, dkv_refs = refs[8:12], refs[12:16]
    qd, kk, vv, score, kacc, vacc, dqs = refs[16:]
    y, z = at_ref[0], at_ref[1]
    for s in range(SLOTS):
        qd[s] = qd_refs[s][...]
    for d in range(SLOTS):
        for s in range(SLOTS):
            kk[d, s * TOK : (s + 1) * TOK, :] = kv_refs[d][s * KV_ROWS : s * KV_ROWS + TOK, :]
            vv[d, s * TOK : (s + 1) * TOK, :] = kv_refs[d][s * KV_ROWS + TOK : (s + 1) * KV_ROWS, :]
    kacc[...] = jnp.zeros_like(kacc)
    vacc[...] = jnp.zeros_like(vacc)

    def tile(slot, carry):
        query = qd[slot, :QROWS, :]
        grad = qd[slot, QROWS : 2 * QROWS, :]
        terms3 = qd[slot, 2 * QROWS :, :].astype(f32)
        term4 = terms3[0:4] + terms3[4:8] + terms3[8:12]
        term = jnp.concatenate([term4[h : h + 1] for h in range(GROUP)], axis=1)
        key_row = lax.broadcasted_iota(jnp.int32, (BLK, QROWS), 0)
        query_col = lax.broadcasted_iota(jnp.int32, (BLK, QROWS), 1)
        key_pos = lax.rem(y + SLOTS - key_row // TOK, SLOTS) * TOK + lax.rem(key_row, TOK)
        query_pos = lax.rem(y + SLOTS - slot, SLOTS) * TOK + lax.rem(query_col, TOK)
        first = dot(kk[0], query, ((1,), (1,)))
        first = jnp.where(key_pos <= query_pos, first, -jnp.inf)
        score[0] = first

        def scores(d, top):
            s = dot(kk[d], query, ((1,), (1,)))
            score[d] = s
            return jnp.maximum(top, jnp.max(s, axis=0, keepdims=True))

        top = lax.fori_loop(1, z + 1, scores, jnp.max(first, axis=0, keepdims=True))

        def weights(d, total):
            e = jnp.exp2((score[d] - top) * (FACTOR * LOG2E))
            score[d] = e
            return total + jnp.sum(e, axis=0, keepdims=True)

        total = lax.fori_loop(0, z + 1, weights, jnp.zeros((1, QROWS), f32))
        inverse = 1.0 / total

        def grads(d, dq):
            attn = score[d] * inverse
            grad_attn = dot(vv[d], grad, ((1,), (1,)))
            low = (attn * (grad_attn - term)).astype(bf16)
            vacc[d] += dot(attn.astype(bf16), grad, ((1,), (0,)))
            kacc[d] += dot(low, query, ((1,), (0,)))
            return dq + dot(low, kk[d], ((0,), (0,)))

        dq = lax.fori_loop(0, z + 1, grads, jnp.zeros((QROWS, HD), f32))
        dqs[slot] = (dq * FACTOR).astype(bf16)
        return carry

    lax.fori_loop(0, SLOTS, tile, 0)
    for s in range(SLOTS):
        dq_refs[s][...] = dqs[s]
    for d in range(SLOTS):
        for s in range(SLOTS):
            rows = slice(s * TOK, (s + 1) * TOK)
            dkv_refs[d][s * KV_ROWS : s * KV_ROWS + TOK, :] = (kacc[d, rows, :] * FACTOR).astype(bf16)
            dkv_refs[d][s * KV_ROWS + TOK : (s + 1) * KV_ROWS, :] = vacc[d, rows, :].astype(bf16)


def pack_query(at_ref, sel_ref, *refs):
    y = at_ref[0]
    parts, outs = refs[:8], refs[8:]
    for doc in range(2):
        sel = sel_ref[doc]
        for slot in range(SLOTS):
            group = lax.rem(y + slot, SLOTS)
            for h in range(GROUP):
                rows = parts[doc * SLOTS + slot][h * TOK : (h + 1) * TOK, :]
                picked = dot(sel, rows, ((1,), (0,))).astype(bf16)
                for dest in range(8):
                    outs[dest][doc, :, aligned(group * GROUP + h, HD)] = picked[
                        dest * CAP : (dest + 1) * CAP
                    ]


def pack_kv(at_ref, sel_ref, *refs):
    y = at_ref[0]
    parts, outs = refs[:2], refs[2:]
    for doc in range(2):
        sel = sel_ref[doc]
        for slot in range(SLOTS):
            head = lax.rem(y + slot, SLOTS)
            for kind in range(2):
                first = slot * KV_ROWS + kind * TOK
                picked = dot(sel, parts[doc][first : first + TOK, :], ((1,), (0,))).astype(bf16)
                for dest in range(8):
                    outs[dest][doc, :, aligned(kind * KVH + head, HD)] = picked[
                        dest * CAP : (dest + 1) * CAP
                    ]


def place(at_ref, *refs):
    queries, kvs, out, sem = refs[:8], refs[8:16], refs[16], refs[17]
    x, c, zh = at_ref[2], at_ref[3], at_ref[4]
    copies = []
    for kx in range(4):
        for cc in range(2):
            piece = kx * 2 + cc
            for dz in range(2):
                doc = lax.rem(zh + dz, 2) * 8 + lax.rem(x + 4 - kx, 4) * 2 + lax.rem(c + cc, 2)
                for source, columns in (
                    (queries[piece], pl.ds(0, QH * HD)),
                    (kvs[piece], pl.ds(QH * HD, 2 * KVH * HD)),
                ):
                    copies.append(
                        pltpu.make_async_copy(
                            source.at[dz], out.at[doc, :, columns], sem.at[len(copies)]
                        )
                    )
    for copy in copies:
        copy.start()
    for copy in copies:
        copy.wait()


def call(kernel, ins, outs, scratch=(), out_specs=None):
    return pl.pallas_call(
        kernel,
        out_shape=outs,
        in_specs=[SMEM] + [VMEM] * ins,
        out_specs=out_specs or [VMEM] * len(outs),
        scratch_shapes=list(scratch),
        compiler_params=PARAMS,
    )


def shaped(*shape, dtype=bf16):
    return jax.ShapeDtypeStruct(shape, dtype)


def selection(lens, owners, targets):
    before = jnp.arange(16)[:, None] < jnp.arange(16)[None, :]
    starts = jnp.sum(jnp.where(before, lens[:, None], 0), axis=0)
    owned = owners[None, :] == targets[:, None]
    start = jnp.sum(jnp.where(owned, starts[None, :], 0), axis=1)
    size = jnp.sum(jnp.where(owned, lens[None, :], 0), axis=1)
    slot = jnp.arange(CAP)
    row = jnp.where(slot[None, :] < size[:, None], start[:, None] + slot[None, :], -1)
    return (row.reshape(-1)[:, None] == jnp.arange(TOK)[None, :]).astype(bf16)


def body(queries, keys, values, outputs, out_grads, lengths, owners):
    y, z = lax.axis_index("y"), lax.axis_index("zl")
    x, c, zh = lax.axis_index("x"), lax.axis_index("c"), lax.axis_index("zh")
    at = jnp.stack([y, z, x, c, zh]).astype(jnp.int32)

    def shift(a, axis, by):
        size = lax.axis_size(axis)
        return lax.ppermute(a, axis, [(i, (i + by) % size) for i in range(size)])

    kv = call(split_kv, 2, [shaped(KV_ROWS, HD)] * 4)(at, keys[0], values[0])
    kv_own = jnp.concatenate([kv[0]] + [shift(kv[k], "y", k) for k in (1, 2, 3)], axis=0)
    kv_all = [kv_own] + [
        lax.ppermute(kv_own, "zl", [(i, i + d) for i in range(4 - d)]) for d in (1, 2, 3)
    ]
    qd = call(split_qd, 3, [shaped(QD_ROWS, HD)] * 4)(at, queries[0], outputs[0], out_grads[0])
    qd_all = [qd[0]] + [shift(qd[k], "y", k) for k in (1, 2, 3)]

    meta = jnp.stack([lengths[0, 0], owners[0, 0]])
    other = shift(meta, "zh", 1)
    near = jnp.arange(8) // 2
    targets = zh * 8 + lax.rem(x + near, 4) * 2 + lax.rem(c + jnp.arange(8) % 2, 2)
    sel = jnp.stack([selection(meta[0], meta[1], targets), selection(other[0], other[1], targets)])

    grads = call(
        attention_grads,
        8,
        [shaped(QROWS, HD)] * 4 + [shaped(4 * KV_ROWS, HD)] * 4,
        [
            pltpu.VMEM((SLOTS, QD_ROWS, HD), bf16),
            pltpu.VMEM((4, BLK, HD), bf16),
            pltpu.VMEM((4, BLK, HD), bf16),
            pltpu.VMEM((4, BLK, QROWS), f32),
            pltpu.VMEM((4, BLK, HD), f32),
            pltpu.VMEM((4, BLK, HD), f32),
            pltpu.VMEM((SLOTS, QROWS, HD), bf16),
        ],
    )(at, *qd_all, *kv_all)
    dq, dkv = grads[:4], grads[4:]

    dq_back = [dq[0]] + [shift(dq[k], "y", 4 - k) for k in (1, 2, 3)]
    dq_far = [shift(a, "zh", 1) for a in dq_back]
    dkv_parts = [dkv[0]] + [
        lax.ppermute(dkv[d], "zl", [(i, i - d) for i in range(d, 4)]) for d in (1, 2, 3)
    ]
    dkv_sum = sum(a.astype(f32) for a in dkv_parts).astype(bf16)
    dkv_slots = [dkv_sum[k * KV_ROWS : (k + 1) * KV_ROWS] for k in range(4)]
    dkv_back = jnp.concatenate(
        [dkv_slots[0]] + [shift(dkv_slots[k], "y", 4 - k) for k in (1, 2, 3)], axis=0
    )
    dkv_far = shift(dkv_back, "zh", 1)

    def spread(pieces):
        out = []
        for kx in range(4):
            for cc in range(2):
                piece = pieces[kx * 2 + cc]
                if kx or cc:
                    pairs = [
                        (i, ((i // 2 + kx) % 4) * 2 + (i % 2 + cc) % 2) for i in range(8)
                    ]
                    piece = lax.ppermute(piece, ("x", "c"), pairs)
                out.append(piece)
        return out

    query_out = spread(
        call(pack_query, 9, [shaped(2, CAP, QH * HD)] * 8)(at, sel, *dq_back, *dq_far)
    )
    kv_out = spread(call(pack_kv, 3, [shaped(2, CAP, 2 * KVH * HD)] * 8)(at, sel, dkv_back, dkv_far))
    returned = call(
        place,
        16,
        shaped(16, CAP, (QH + 2 * KVH) * HD),
        [pltpu.SemaphoreType.DMA((32,))],
        pl.BlockSpec(memory_space=pl.ANY),
    )(at, *query_out, *kv_out)
    return returned[None, None]


def solution(mesh):
    split = Mesh(mesh.devices.reshape(2, 4, 2, 4, 4), ("zh", "x", "c", "zl", "y"))
    rows = P(("zh", "x", "c"), ("zl", "y"), None)
    return jax.shard_map(
        body,
        mesh=split,
        in_specs=(rows,) * 7,
        out_specs=P(("zh", "x", "c"), ("zl", "y"), None, None, None),
        check_vma=False,
    )
```

time: 228 us -> 157 us (0.69)
  the two profiles are of different devices: /device:TPU:32 before, /device:TPU:1 now
where the time goes in v1:
time: 157 us; the launch traced here: 155 us
  starting transfers between devices  67.4 us (43%)
  waiting for transfers between devices  61.6 us (39%)
  Pallas kernels  20.4 us (13%)
  local copies, waits for them, and re-layouts  2.79 us (2%)
  other arithmetic  2.4 us (2%)
    ppermute x18, starting transfers between devices, shift(): return lax.ppermute(a, axis, [(i, (i + by) % size) for i in range(size)])  39.2 us
    ppermute x3, waiting for transfers between devices, body(): lax.ppermute(dkv[d], 'zl', [(i, i - d) for i in range(d, 4)])  31.4 us
    ppermute x14, starting transfers between devices, spread(): piece = lax.ppermute(piece, ('x', 'c'), pairs)  17.2 us
    ppermute x18, waiting for transfers between devices, shift(): return lax.ppermute(a, axis, [(i, (i + by) % size) for i in range(size)])  11.2 us
    ppermute x3, waiting for transfers between devices, body(): lax.ppermute(kv_own, 'zl', [(i, i + d) for i in range(4 - d)])  10.3 us
    ppermute x14, waiting for transfers between devices, spread(): piece = lax.ppermute(piece, ('x', 'c'), pairs)  8.6 us
    pallas_call x1, Pallas kernels, body(): call(attention_grads, 8, [shaped(QROWS, HD)] * 4 + [shaped(4 * KV_ROWS, H...  8.14 us
    ppermute x3, starting transfers between devices, body(): lax.ppermute(kv_own, 'zl', [(i, i + d) for i in range(4 - d)])  7.06 us
  transfers between devices with their start and end apart: 38, of which 15 were waited for; matrix products, arithmetic and copies ran while one was open for 2% of the time, Pallas kernels for 5%

profile of v1, /device:TPU:1, one launch (start us, length us, event | category | flops | bytes accessed | tf_op | source)
XLA Modules:
  0.0 155.2 jit_solution(16082928179600417920)
XLA Ops:
  2.4 2.1 %collective-permute-start.4 = (bf16[256,128]{1,0:T(8,128)(2,1)}, bf16[256,128]{1,0:T(8,128)(2,1)S(1)}, u32[]{:S(2)}, u32[]{:S(2)}) collective-permute-start(bf16[256,128]{1,0:T(8,128)(2,1)} %get-tuple-element.42), channel_id=1, source_target_pairs={{0,1},{1,2},{2,3},{3,0},{4,5},{5,6},{6,7},{7,4},{8,9},{9,10},{10,1... | collective-permute-start | bytes 196616 | tf_op jit(solution)/shard_map/ppermute | solution.py:225
  4.5 2.6 %collective-permute-start.5 = (bf16[256,128]{1,0:T(8,128)(2,1)}, bf16[256,128]{1,0:T(8,128)(2,1)S(1)}, u32[]{:S(2)}, u32[]{:S(2)}) collective-permute-start(bf16[256,128]{1,0:T(8,128)(2,1)} %get-tuple-element.43), channel_id=1, source_target_pairs={{0,2},{1,3},{2,0},{3,1},{4,6},{5,7},{6,4},{7,5},{8,10},{9,11},{10,... | collective-permute-start | bytes 196616 | tf_op jit(solution)/shard_map/ppermute | solution.py:225
  8.2 2.8 %shard_map.73 = (bf16[1040,128]{1,0:T(8,128)(2,1)}, bf16[1040,128]{1,0:T(8,128)(2,1)}, bf16[1040,128]{1,0:T(8,128)(2,1)}, bf16[1040,128]{1,0:T(8,128)(2,1)}) custom-call(s32[5]{0:T(128)} %stack.33.at_ref, bf16[128,2048]{1,0:T(8,128)(2,1)} %bitcast.19, bf16[128,2048]{1,0:T(8,128)(2,1)} %bitcast.20, bf16[128,2048]{1,0:T(8,128)(2,1)} %bitcast.21), custom_call_target="tpu_custom_call" | custom-call | tf_op jit(solution)/shard_map/pallas_call | solution.py:232
  14.1 7.0 %collective-permute-start = (s32[2,16]{1,0:T(2,128)S(1)}, s32[2,16]{1,0:T(2,128)S(1)}, u32[]{:S(2)}, u32[]{:S(2)}) collective-permute-start(s32[2,16]{1,0:T(2,128)S(1)} %pad_add_fusion), channel_id=1, source_target_pairs={{0,128},{128,0},{1,129},{129,1},{2,130},{130,2},{3,131},{131,3},{4... | collective-permute-start | bytes 392 | tf_op jit(solution)/shard_map/ppermute | solution.py:225
  21.1 2.7 %collective-permute-start.7 = (bf16[1024,128]{1,0:T(8,128)(2,1)S(1)}, bf16[1024,128]{1,0:T(8,128)(2,1)S(1)}, u32[]{:S(2)}, u32[]{:S(2)}) collective-permute-start(bf16[1024,128]{1,0:T(8,128)(2,1)S(1)} %constant_dynamic-update-slice_fusion.refs_4_), channel_id=1, source_target_pairs={{0,4},{4,8},{8,12},{1,5},{5,9},{9,13},{2,6},{6,10},{10,14},{3,7},{... | collective-permute-start | bytes 786440 | tf_op jit(solution)/shard_map/ppermute | solution.py:230
  23.8 3.1 %collective-permute-start.8 = (bf16[1024,128]{1,0:T(8,128)(2,1)S(1)}, bf16[1024,128]{1,0:T(8,128)(2,1)S(1)}, u32[]{:S(2)}, u32[]{:S(2)}) collective-permute-start(bf16[1024,128]{1,0:T(8,128)(2,1)S(1)} %constant_dynamic-update-slice_fusion.refs_4_), channel_id=1, source_target_pairs={{0,8},{4,12},{1,9},{5,13},{2,10},{6,14},{3,11},{7,15},{16,24},{20,... | collective-permute-start | bytes 786440 | tf_op jit(solution)/shard_map/ppermute | solution.py:230
  28.4 4.6 %collective-permute-done.8.refs_6_ = bf16[1024,128]{1,0:T(8,128)(2,1)S(1)} collective-permute-done((bf16[1024,128]{1,0:T(8,128)(2,1)S(1)}, bf16[1024,128]{1,0:T(8,128)(2,1)S(1)}, u32[]{:S(2)}, u32[]{:S(2)}) %collective-permute-start.8) | collective-permute-done | bytes 262176 | tf_op jit(solution)/shard_map/ppermute | solution.py:230
  33.0 5.7 %collective-permute-done.9.refs_7_ = bf16[1024,128]{1,0:T(8,128)(2,1)S(1)} collective-permute-done((bf16[1024,128]{1,0:T(8,128)(2,1)S(1)}, bf16[1024,128]{1,0:T(8,128)(2,1)S(1)}, u32[]{:S(2)}, u32[]{:S(2)}) %collective-permute-start.9) | collective-permute-done | bytes 262176 | tf_op jit(solution)/shard_map/ppermute | solution.py:230
  39.4 8.1 %shard_map.75 = (bf16[512,128]{1,0:T(8,128)(2,1)}, bf16[512,128]{1,0:T(8,128)(2,1)}, bf16[512,128]{1,0:T(8,128)(2,1)}, bf16[512,128]{1,0:T(8,128)(2,1)}, bf16[10...) custom-call(s32[5]{0:T(128)} %stack.33.at_ref, ...), custom_call_target="tpu_custom_call" | custom-call | tf_op jit(solution)/shard_map/pallas_call | solution.py:241
  54.3 10.1 %collective-permute-done.24 = bf16[1024,128]{1,0:T(8,128)(2,1)S(1)} collective-permute-done((bf16[1024,128]{1,0:T(8,128)(2,1)}, bf16[1024,128]{1,0:T(8,128)(2,1)S(1)}, u32[]{:S(2)}, u32[]{:S(2)}) %collective-permute-start.24) | collective-permute-done | bytes 262176 | tf_op jit(solution)/shard_map/ppermute | solution.py:260
  64.9 3.6 %collective-permute-done.25 = bf16[1024,128]{1,0:T(8,128)(2,1)S(1)} collective-permute-done((bf16[1024,128]{1,0:T(8,128)(2,1)}, bf16[1024,128]{1,0:T(8,128)(2,1)S(1)}, u32[]{:S(2)}, u32[]{:S(2)}) %collective-permute-start.25) | collective-permute-done | bytes 262176 | tf_op jit(solution)/shard_map/ppermute | solution.py:260
  68.5 17.7 %collective-permute-done.26 = bf16[1024,128]{1,0:T(8,128)(2,1)S(1)} collective-permute-done((bf16[1024,128]{1,0:T(8,128)(2,1)}, bf16[1024,128]{1,0:T(8,128)(2,1)S(1)}, u32[]{:S(2)}, u32[]{:S(2)}) %collective-permute-start.26) | collective-permute-done | bytes 262176 | tf_op jit(solution)/shard_map/ppermute | solution.py:260
  90.1 7.2 %collective-permute-start.13 = (bf16[512,128]{1,0:T(8,128)(2,1)S(1)}, bf16[512,128]{1,0:T(8,128)(2,1)S(1)}, u32[]{:S(2)}, u32[]{:S(2)}) collective-permute-start(bf16[512,128]{1,0:T(8,128)(2,1)S(1)} %copy-done.9), channel_id=1, source_target_pairs={{0,128},{128,0},{1,129},{129,1},{2,130},{130,2},{3,131},{131,3},{4... | collective-permute-start | bytes 393224 | tf_op jit(solution)/shard_map/ppermute | solution.py:225
  97.5 5.3 %collective-permute-start.15 = (bf16[512,128]{1,0:T(8,128)(2,1)S(1)}, bf16[512,128]{1,0:T(8,128)(2,1)S(1)}, u32[]{:S(2)}, u32[]{:S(2)}) collective-permute-start(bf16[512,128]{1,0:T(8,128)(2,1)S(1)} %collective-permute-done.11.refs_2_), channel_id=1, source_target_pairs={{0,128},{128,0},{1,129},{129,1},{2,130},{130,2},{3,131},{131,3},{4... | collective-permute-start | bytes 393224 | tf_op jit(solution)/shard_map/ppermute | solution.py:225
  102.9 5.3 %collective-permute-start.30 = (bf16[1024,128]{1,0:T(8,128)(2,1)S(1)}, bf16[1024,128]{1,0:T(8,128)(2,1)S(1)}, u32[]{:S(2)}, u32[]{:S(2)}) collective-permute-start(bf16[1024,128]{1,0:T(8,128)(2,1)S(1)} %pad_maximum_fusion.refs_0_), channel_id=1, source_target_pairs={{0,128},{128,0},{1,129},{129,1},{2,130},{130,2},{3,131},{131,3},{4... | collective-permute-start | bytes 786440 | tf_op jit(solution)/shard_map/ppermute | solution.py:225
  109.0 2.2 %collective-permute-done.13.refs_4_ = bf16[512,128]{1,0:T(8,128)(2,1)S(1)} collective-permute-done((bf16[512,128]{1,0:T(8,128)(2,1)S(1)}, bf16[512,128]{1,0:T(8,128)(2,1)S(1)}, u32[]{:S(2)}, u32[]{:S(2)}) %collective-permute-start.13) | collective-permute-done | bytes 131104 | tf_op jit(solution)/shard_map/ppermute | solution.py:225
  111.2 3.3 %collective-permute-done.14.refs_5_ = bf16[512,128]{1,0:T(8,128)(2,1)S(1)} collective-permute-done((bf16[512,128]{1,0:T(8,128)(2,1)S(1)}, bf16[512,128]{1,0:T(8,128)(2,1)S(1)}, u32[]{:S(2)}, u32[]{:S(2)}) %collective-permute-start.14) | collective-permute-done | bytes 131104 | tf_op jit(solution)/shard_map/ppermute | solution.py:225
  114.6 2.8 %collective-permute-done.15.refs_6_ = bf16[512,128]{1,0:T(8,128)(2,1)S(1)} collective-permute-done((bf16[512,128]{1,0:T(8,128)(2,1)S(1)}, bf16[512,128]{1,0:T(8,128)(2,1)S(1)}, u32[]{:S(2)}, u32[]{:S(2)}) %collective-permute-start.15) | collective-permute-done | bytes 131104 | tf_op jit(solution)/shard_map/ppermute | solution.py:225
  117.4 2.8 %collective-permute-done.16.refs_7_ = bf16[512,128]{1,0:T(8,128)(2,1)S(1)} collective-permute-done((bf16[512,128]{1,0:T(8,128)(2,1)S(1)}, bf16[512,128]{1,0:T(8,128)(2,1)S(1)}, u32[]{:S(2)}, u32[]{:S(2)}) %collective-permute-start.16) | collective-permute-done | bytes 131104 | tf_op jit(solution)/shard_map/ppermute | solution.py:225
  120.9 2.7 %shard_map.76 = (bf16[2,16,2048]{2,1,0:T(8,128)(2,1)}, bf16[2,16,2048]{2,1,0:T(8,128)(2,1)}, bf16[2,16,2048]{2,1,0:T(8,128)(2,1)}, bf16[2,16,2048]{2,1,0:T(8,128...) custom-call(s32[5]{0:T(128)} %stack.33.at_ref, ...), custom_call_target="tpu_custom_call" | custom-call | tf_op jit(solution)/shard_map/pallas_call | solution.py:283
  134.7 2.2 %shard_map.77 = (bf16[2,16,1024]{2,1,0:T(8,128)(2,1)}, bf16[2,16,1024]{2,1,0:T(8,128)(2,1)}, bf16[2,16,1024]{2,1,0:T(8,128)(2,1)}, bf16[2,16,1024]{2,1,0:T(8,128...) custom-call(s32[5]{0:T(128)} %stack.33.at_ref, ...), custom_call_target="tpu_custom_call" | custom-call | tf_op jit(solution)/shard_map/pallas_call | solution.py:285
  138.0 3.4 %collective-permute-done.21.refs_5_ = bf16[2,16,2048]{2,1,0:T(8,128)(2,1)S(1)} collective-permute-done((bf16[2,16,2048]{2,1,0:T(8,128)(2,1)}, bf16[2,16,2048]{2,1,0:T(8,128)(2,1)S(1)}, u32[]{:S(2)}, u32[]{:S(2)}) %collective-permute-start.21) | collective-permute-done | bytes 131104 | tf_op jit(solution)/shard_map/ppermute | solution.py:278
  144.5 3.1 %collective-permute-start.36 = (bf16[2,16,1024]{2,1,0:T(8,128)(2,1)}, bf16[2,16,1024]{2,1,0:T(8,128)(2,1)S(1)}, u32[]{:S(2)}, u32[]{:S(2)}) collective-permute-start(bf16[2,16,1024]{2,1,0:T(8,128)(2,1)} %get-tuple-element.67), channel_id=1, source_target_pairs={{0,96},{16,112},{32,0},{48,16},{64,32},{80,48},{96,64},{112,80},{1... | collective-permute-start | bytes 196616 | tf_op jit(solution)/shard_map/ppermute | solution.py:278
  152.2 2.8 %shard_map.78 = bf16[16,16,3072]{2,1,0:T(8,128)(2,1)} custom-call(s32[5]{0:T(128)} %stack.33.at_ref, bf16[2,16,2048]{2,1,0:T(8,128)(2,1)} %get-tuple-element.49.refs_0_, bf16[2,16,2048]{2,1,0:T(8,128)(2,1)} %copy-done.17, bf16[2,16,2048]{2,1,0:T(8,128)(2,1)} %copy-done.18, bf16[2,16,2048]{2,1,0:T(8,128)(2,1)} %copy-done.19, bf16[2,16,2048]{2,1,0:T(8,128)(2,1)} %copy-done.20, ...), custom_call_target="tpu_custom_call" | custom-call | tf_op jit(solution)/shard_map/pallas_call | solution.py:286
  (146 shorter events, 41.1 us)
Async XLA Ops:
  7.1 14.0 %collective-permute-start.6 = (bf16[256,128]{1,0:T(8,128)(2,1)}, bf16[256,128]{1,0:T(8,128)(2,1)S(1)}, u32[]{:S(2)}, u32[]{:S(2)}) collective-permute-start(bf16[256,128]{1,0:T(8,128)(2,1)} %get-tuple-element.44), channel_id=1, source_target_pairs={{0,3},{1,0},{2,1},{3,2},{4,7},{5,4},{6,5},{7,6},{8,11},{9,8},{10,9... | collective-permute-start | bytes 196616 | tf_op jit(solution)/shard_map/ppermute | solution.py:225
  11.0 15.9 %collective-permute-start.1 = (bf16[1040,128]{1,0:T(8,128)(2,1)}, bf16[1040,128]{1,0:T(8,128)(2,1)S(1)}, u32[]{:S(2)}, u32[]{:S(2)}) collective-permute-start(bf16[1040,128]{1,0:T(8,128)(2,1)} %get-tuple-element.38), channel_id=1, source_target_pairs={{0,1},{1,2},{2,3},{3,0},{4,5},{5,6},{6,7},{7,4},{8,9},{9,10},{10,1... | collective-permute-start | bytes 798728 | tf_op jit(solution)/shard_map/ppermute | solution.py:225
  11.4 16.9 %collective-permute-start.2 = (bf16[1040,128]{1,0:T(8,128)(2,1)}, bf16[1040,128]{1,0:T(8,128)(2,1)S(1)}, u32[]{:S(2)}, u32[]{:S(2)}) collective-permute-start(bf16[1040,128]{1,0:T(8,128)(2,1)} %get-tuple-element.39), channel_id=1, source_target_pairs={{0,2},{1,3},{2,0},{3,1},{4,6},{5,7},{6,4},{7,5},{8,10},{9,11},{10,... | collective-permute-start | bytes 798728 | tf_op jit(solution)/shard_map/ppermute | solution.py:225
  12.4 16.0 %collective-permute-start.3 = (bf16[1040,128]{1,0:T(8,128)(2,1)}, bf16[1040,128]{1,0:T(8,128)(2,1)S(1)}, u32[]{:S(2)}, u32[]{:S(2)}) collective-permute-start(bf16[1040,128]{1,0:T(8,128)(2,1)} %get-tuple-element.40), channel_id=1, source_target_pairs={{0,3},{1,0},{2,1},{3,2},{4,7},{5,4},{6,5},{7,6},{8,11},{9,8},{10,9... | collective-permute-start | bytes 798728 | tf_op jit(solution)/shard_map/ppermute | solution.py:225
  26.9 11.7 %collective-permute-start.9 = (bf16[1024,128]{1,0:T(8,128)(2,1)S(1)}, bf16[1024,128]{1,0:T(8,128)(2,1)S(1)}, u32[]{:S(2)}, u32[]{:S(2)}) collective-permute-start(bf16[1024,128]{1,0:T(8,128)(2,1)S(1)} %constant_dynamic-update-slice_fusion.refs_4_), channel_id=1, source_target_pairs={{0,12},{1,13},{2,14},{3,15},{16,28},{17,29},{18,30},{19,31},{32,44... | collective-permute-start | bytes 786440 | tf_op jit(solution)/shard_map/ppermute | solution.py:230
  47.5 16.9 %collective-permute-start.24 = (bf16[1024,128]{1,0:T(8,128)(2,1)}, bf16[1024,128]{1,0:T(8,128)(2,1)S(1)}, u32[]{:S(2)}, u32[]{:S(2)}) collective-permute-start(bf16[1024,128]{1,0:T(8,128)(2,1)} %get-tuple-element.58), channel_id=1, source_target_pairs={{4,0},{8,4},{12,8},{5,1},{9,5},{13,9},{6,2},{10,6},{14,10},{7,3},{... | collective-permute-start | bytes 786440 | tf_op jit(solution)/shard_map/ppermute | solution.py:260
  48.9 19.5 %collective-permute-start.25 = (bf16[1024,128]{1,0:T(8,128)(2,1)}, bf16[1024,128]{1,0:T(8,128)(2,1)S(1)}, u32[]{:S(2)}, u32[]{:S(2)}) collective-permute-start(bf16[1024,128]{1,0:T(8,128)(2,1)} %get-tuple-element.59), channel_id=1, source_target_pairs={{8,0},{12,4},{9,1},{13,5},{10,2},{14,6},{11,3},{15,7},{24,16},{28,... | collective-permute-start | bytes 786440 | tf_op jit(solution)/shard_map/ppermute | solution.py:260
  50.2 36.0 %collective-permute-start.26 = (bf16[1024,128]{1,0:T(8,128)(2,1)}, bf16[1024,128]{1,0:T(8,128)(2,1)S(1)}, u32[]{:S(2)}, u32[]{:S(2)}) collective-permute-start(bf16[1024,128]{1,0:T(8,128)(2,1)} %get-tuple-element.60), channel_id=1, source_target_pairs={{12,0},{13,1},{14,2},{15,3},{28,16},{29,17},{30,18},{31,19},{44,32... | collective-permute-start | bytes 786440 | tf_op jit(solution)/shard_map/ppermute | solution.py:260
  51.9 37.8 %collective-permute-start.10 = (bf16[512,128]{1,0:T(8,128)(2,1)}, bf16[512,128]{1,0:T(8,128)(2,1)S(1)}, u32[]{:S(2)}, u32[]{:S(2)}) collective-permute-start(bf16[512,128]{1,0:T(8,128)(2,1)} %get-tuple-element.46), channel_id=1, source_target_pairs={{0,3},{1,0},{2,1},{3,2},{4,7},{5,4},{6,5},{7,6},{8,11},{9,8},{10,9... | collective-permute-start | bytes 393224 | tf_op jit(solution)/shard_map/ppermute | solution.py:225
  52.8 37.3 %collective-permute-start.11 = (bf16[512,128]{1,0:T(8,128)(2,1)}, bf16[512,128]{1,0:T(8,128)(2,1)S(1)}, u32[]{:S(2)}, u32[]{:S(2)}) collective-permute-start(bf16[512,128]{1,0:T(8,128)(2,1)} %get-tuple-element.47), channel_id=1, source_target_pairs={{0,2},{1,3},{2,0},{3,1},{4,6},{5,7},{6,4},{7,5},{8,10},{9,11},{10,... | collective-permute-start | bytes 393224 | tf_op jit(solution)/shard_map/ppermute | solution.py:225
  64.4 33.0 %collective-permute-start.12 = (bf16[512,128]{1,0:T(8,128)(2,1)}, bf16[512,128]{1,0:T(8,128)(2,1)S(1)}, u32[]{:S(2)}, u32[]{:S(2)}) collective-permute-start(bf16[512,128]{1,0:T(8,128)(2,1)} %get-tuple-element.48), channel_id=1, source_target_pairs={{0,1},{1,2},{2,3},{3,0},{4,5},{5,6},{6,7},{7,4},{8,9},{9,10},{10,1... | collective-permute-start | bytes 393224 | tf_op jit(solution)/shard_map/ppermute | solution.py:225
  87.3 10.1 %collective-permute-start.27 = (bf16[256,128]{1,0:T(8,128)(2,1)S(1)}, bf16[256,128]{1,0:T(8,128)(2,1)S(1)}, u32[]{:S(2)}, u32[]{:S(2)}) collective-permute-start(bf16[256,128]{1,0:T(8,128)(2,1)S(1)} %get-tuple-element.78), channel_id=1, source_target_pairs={{0,3},{1,0},{2,1},{3,2},{4,7},{5,4},{6,5},{7,6},{8,11},{9,8},{10,9... | collective-permute-start | bytes 196616 | tf_op jit(solution)/shard_map/ppermute | solution.py:225
  87.7 15.0 %collective-permute-start.28 = (bf16[256,128]{1,0:T(8,128)(2,1)S(1)}, bf16[256,128]{1,0:T(8,128)(2,1)S(1)}, u32[]{:S(2)}, u32[]{:S(2)}) collective-permute-start(bf16[256,128]{1,0:T(8,128)(2,1)S(1)} %get-tuple-element.77), channel_id=1, source_target_pairs={{0,2},{1,3},{2,0},{3,1},{4,6},{5,7},{6,4},{7,5},{8,10},{9,11},{10,... | collective-permute-start | bytes 196616 | tf_op jit(solution)/shard_map/ppermute | solution.py:225
  89.7 13.2 %collective-permute-start.29 = (bf16[256,128]{1,0:T(8,128)(2,1)S(1)}, bf16[256,128]{1,0:T(8,128)(2,1)S(1)}, u32[]{:S(2)}, u32[]{:S(2)}) collective-permute-start(bf16[256,128]{1,0:T(8,128)(2,1)S(1)} %get-tuple-element.76), channel_id=1, source_target_pairs={{0,1},{1,2},{2,3},{3,0},{4,5},{5,6},{6,7},{7,4},{8,9},{9,10},{10,1... | collective-permute-start | bytes 196616 | tf_op jit(solution)/shard_map/ppermute | solution.py:225
  90.1 21.1 %collective-permute-start.13 = (bf16[512,128]{1,0:T(8,128)(2,1)S(1)}, bf16[512,128]{1,0:T(8,128)(2,1)S(1)}, u32[]{:S(2)}, u32[]{:S(2)}) collective-permute-start(bf16[512,128]{1,0:T(8,128)(2,1)S(1)} %copy-done.9), channel_id=1, source_target_pairs={{0,128},{128,0},{1,129},{129,1},{2,130},{130,2},{3,131},{131,3},{4... | collective-permute-start | bytes 393224 | tf_op jit(solution)/shard_map/ppermute | solution.py:225
  97.3 17.2 %collective-permute-start.14 = (bf16[512,128]{1,0:T(8,128)(2,1)S(1)}, bf16[512,128]{1,0:T(8,128)(2,1)S(1)}, u32[]{:S(2)}, u32[]{:S(2)}) collective-permute-start(bf16[512,128]{1,0:T(8,128)(2,1)S(1)} %collective-permute-done.10.refs_1_), channel_id=1, source_target_pairs={{0,128},{128,0},{1,129},{129,1},{2,130},{130,2},{3,131},{131,3},{4... | collective-permute-start | bytes 393224 | tf_op jit(solution)/shard_map/ppermute | solution.py:225
  97.5 19.9 %collective-permute-start.15 = (bf16[512,128]{1,0:T(8,128)(2,1)S(1)}, bf16[512,128]{1,0:T(8,128)(2,1)S(1)}, u32[]{:S(2)}, u32[]{:S(2)}) collective-permute-start(bf16[512,128]{1,0:T(8,128)(2,1)S(1)} %collective-permute-done.11.refs_2_), channel_id=1, source_target_pairs={{0,128},{128,0},{1,129},{129,1},{2,130},{130,2},{3,131},{131,3},{4... | collective-permute-start | bytes 393224 | tf_op jit(solution)/shard_map/ppermute | solution.py:225
  102.7 17.4 %collective-permute-start.16 = (bf16[512,128]{1,0:T(8,128)(2,1)S(1)}, bf16[512,128]{1,0:T(8,128)(2,1)S(1)}, u32[]{:S(2)}, u32[]{:S(2)}) collective-permute-start(bf16[512,128]{1,0:T(8,128)(2,1)S(1)} %collective-permute-done.12.refs_3_), channel_id=1, source_target_pairs={{0,128},{128,0},{1,129},{129,1},{2,130},{130,2},{3,131},{131,3},{4... | collective-permute-start | bytes 393224 | tf_op jit(solution)/shard_map/ppermute | solution.py:225
  102.9 29.8 %collective-permute-start.30 = (bf16[1024,128]{1,0:T(8,128)(2,1)S(1)}, bf16[1024,128]{1,0:T(8,128)(2,1)S(1)}, u32[]{:S(2)}, u32[]{:S(2)}) collective-permute-start(bf16[1024,128]{1,0:T(8,128)(2,1)S(1)} %pad_maximum_fusion.refs_0_), channel_id=1, source_target_pairs={{0,128},{128,0},{1,129},{129,1},{2,130},{130,2},{3,131},{131,3},{4... | collective-permute-start | bytes 786440 | tf_op jit(solution)/shard_map/ppermute | solution.py:225
  126.1 10.7 %collective-permute-start.19 = (bf16[2,16,2048]{2,1,0:T(8,128)(2,1)}, bf16[2,16,2048]{2,1,0:T(8,128)(2,1)S(1)}, u32[]{:S(2)}, u32[]{:S(2)}) collective-permute-start(bf16[2,16,2048]{2,1,0:T(8,128)(2,1)} %get-tuple-element.52), channel_id=1, source_target_pairs={{0,48},{16,32},{32,80},{48,64},{64,112},{80,96},{96,16},{112,0},{1... | collective-permute-start | bytes 393224 | tf_op jit(solution)/shard_map/ppermute | solution.py:278
  127.6 10.4 %collective-permute-start.20 = (bf16[2,16,2048]{2,1,0:T(8,128)(2,1)}, bf16[2,16,2048]{2,1,0:T(8,128)(2,1)S(1)}, u32[]{:S(2)}, u32[]{:S(2)}) collective-permute-start(bf16[2,16,2048]{2,1,0:T(8,128)(2,1)} %get-tuple-element.53), channel_id=1, source_target_pairs={{0,64},{16,80},{32,96},{48,112},{64,0},{80,16},{96,32},{112,48},{1... | collective-permute-start | bytes 393224 | tf_op jit(solution)/shard_map/ppermute | solution.py:278
  129.0 12.4 %collective-permute-start.21 = (bf16[2,16,2048]{2,1,0:T(8,128)(2,1)}, bf16[2,16,2048]{2,1,0:T(8,128)(2,1)S(1)}, u32[]{:S(2)}, u32[]{:S(2)}) collective-permute-start(bf16[2,16,2048]{2,1,0:T(8,128)(2,1)} %get-tuple-element.54), channel_id=1, source_target_pairs={{0,80},{16,64},{32,112},{48,96},{64,16},{80,0},{96,48},{112,32},{1... | collective-permute-start | bytes 393224 | tf_op jit(solution)/shard_map/ppermute | solution.py:278
  131.4 10.1 %collective-permute-start.22 = (bf16[2,16,2048]{2,1,0:T(8,128)(2,1)}, bf16[2,16,2048]{2,1,0:T(8,128)(2,1)S(1)}, u32[]{:S(2)}, u32[]{:S(2)}) collective-permute-start(bf16[2,16,2048]{2,1,0:T(8,128)(2,1)} %get-tuple-element.55), channel_id=1, source_target_pairs={{0,96},{16,112},{32,0},{48,16},{64,32},{80,48},{96,64},{112,80},{1... | collective-permute-start | bytes 393224 | tf_op jit(solution)/shard_map/ppermute | solution.py:278
  132.7 10.7 %collective-permute-start.23 = (bf16[2,16,2048]{2,1,0:T(8,128)(2,1)}, bf16[2,16,2048]{2,1,0:T(8,128)(2,1)S(1)}, u32[]{:S(2)}, u32[]{:S(2)}) collective-permute-start(bf16[2,16,2048]{2,1,0:T(8,128)(2,1)} %get-tuple-element.56), channel_id=1, source_target_pairs={{0,112},{16,96},{32,16},{48,0},{64,48},{80,32},{96,80},{112,64},{1... | collective-permute-start | bytes 393224 | tf_op jit(solution)/shard_map/ppermute | solution.py:278
  (48 other events, 505.2 us)

commit v2 on v1

v2 whole, which is shorter than its diff:
```python
import functools

import jax
import jax.numpy as jnp
from jax import lax
from jax.experimental import pallas as pl
from jax.experimental.pallas import tpu as pltpu
from jax.sharding import Mesh, PartitionSpec as P

HD = 128
QH = 16
KVH = 4
GROUP = QH // KVH
TOK = 128
CAP = 16
SLOTS = 4
BLK = SLOTS * TOK
QROWS = GROUP * TOK
QD_ROWS = 2 * QROWS + 16
KV_ROWS = 2 * TOK
FACTOR = HD ** (-0.5)
LOG2E = 1.4426950408889634
f32 = jnp.float32
bf16 = jnp.bfloat16
VMEM = pl.BlockSpec(memory_space=pltpu.VMEM)
SMEM = pl.BlockSpec(memory_space=pltpu.SMEM)
SMALL, LARGE = 12 * 2**20, 28 * 2**20


def aligned(index, unit):
    return pl.ds(pl.multiple_of(index * unit, unit), unit)


def split_kv(at_ref, k_ref, v_ref, *outs):
    y = at_ref[0]
    for slot in range(SLOTS):
        head = aligned(lax.rem(y + slot, SLOTS), HD)
        outs[slot][:TOK, :] = k_ref[:, head]
        outs[slot][TOK:, :] = v_ref[:, head]


def split_qd(at_ref, q_ref, o_ref, g_ref, after_ref, *outs):
    y = at_ref[0]
    lane = lax.broadcasted_iota(jnp.int32, (TOK, HD), 1)
    for slot in range(SLOTS):
        dest = lax.rem(y + slot, SLOTS)
        terms = jnp.zeros((TOK, HD), f32)
        for h in range(GROUP):
            head = aligned(dest * GROUP + h, HD)
            grad = g_ref[:, head]
            outs[slot][h * TOK : (h + 1) * TOK, :] = q_ref[:, head]
            outs[slot][QROWS + h * TOK : QROWS + (h + 1) * TOK, :] = grad
            term = jnp.sum(
                grad.astype(f32) * o_ref[:, head].astype(f32), axis=1, keepdims=True
            )
            terms = jnp.where(lax.rem(lane, GROUP) == h, term, terms)
        high = terms.astype(bf16).astype(f32)
        mid = (terms - high).astype(bf16).astype(f32)
        low = terms - high - mid
        part = lane // GROUP
        packed = jnp.where(
            part == 0, high, jnp.where(part == 1, mid, jnp.where(part == 2, low, 0.0))
        )
        outs[slot][2 * QROWS :, :] = packed.T[:16, :].astype(bf16)


def dot(a, b, dims):
    return lax.dot_general(a, b, (dims, ((), ())), preferred_element_type=f32)


def attention_grads(at_ref, *refs):
    qd_refs, kv_refs = refs[:4], refs[4:8]
    dq_refs, dkv_refs = refs[8:12], refs[12:16]
    qd, kk, vv, kacc, vacc, dqs, delta = refs[16:]
    y, z = at_ref[0], at_ref[1]
    natural = [lax.rem(y + SLOTS - s, SLOTS) for s in range(SLOTS)]
    for s in range(SLOTS):
        qd[natural[s]] = qd_refs[s][...]
    key_at = lax.broadcasted_iota(jnp.int32, (TOK, QROWS), 0)
    query_at = lax.rem(lax.broadcasted_iota(jnp.int32, (TOK, QROWS), 1), TOK)
    delta[...] = key_at - query_at

    def tile(blocks, part):
        query = qd[part, :QROWS, :]
        grad = qd[part, QROWS : 2 * QROWS, :]
        terms3 = qd[part, 2 * QROWS :, :].astype(f32)
        term4 = terms3[0:4] + terms3[4:8] + terms3[8:12]
        term = jnp.concatenate([term4[h : h + 1] for h in range(GROUP)], axis=1)
        scores, tops = [], []
        for d in range(blocks):
            score = dot(kk[d], query, ((1,), (1,)))
            if d == 0:
                score = jnp.concatenate(
                    [
                        jnp.where(
                            delta[...] <= (part - other) * TOK,
                            score[other * TOK : (other + 1) * TOK],
                            -jnp.inf,
                        )
                        for other in range(SLOTS)
                    ],
                    axis=0,
                )
            scores.append(score)
            tops.append(jnp.max(score, axis=0, keepdims=True))
        top = functools.reduce(jnp.maximum, tops)
        weights = [jnp.exp2((score - top) * (FACTOR * LOG2E)) for score in scores]
        inverse = 1.0 / sum(jnp.sum(weight, axis=0, keepdims=True) for weight in weights)
        dq = jnp.zeros((QROWS, HD), f32)
        for d in range(blocks):
            attn = weights[d] * inverse
            grad_attn = dot(vv[d], grad, ((1,), (1,)))
            low = (attn * (grad_attn - term)).astype(bf16)
            vacc[d] += dot(attn.astype(bf16), grad, ((1,), (0,)))
            kacc[d] += dot(low, query, ((1,), (0,)))
            dq = dq + dot(low, kk[d], ((0,), (0,)))
        dqs[part] = (dq * FACTOR).astype(bf16)

    def case(blocks):
        for d in range(blocks):
            for s in range(SLOTS):
                rows = aligned(natural[s], TOK)
                kk[d, rows, :] = kv_refs[d][s * KV_ROWS : s * KV_ROWS + TOK, :]
                vv[d, rows, :] = kv_refs[d][s * KV_ROWS + TOK : (s + 1) * KV_ROWS, :]
            kacc[d] = jnp.zeros((BLK, HD), f32)
            vacc[d] = jnp.zeros((BLK, HD), f32)

        def step(part, carry):
            tile(blocks, part)
            return carry

        lax.fori_loop(0, SLOTS, step, 0)
        for d in range(blocks):
            for s in range(SLOTS):
                rows = aligned(natural[s], TOK)
                dkv_refs[d][s * KV_ROWS : s * KV_ROWS + TOK, :] = (kacc[d, rows, :] * FACTOR).astype(bf16)
                dkv_refs[d][s * KV_ROWS + TOK : (s + 1) * KV_ROWS, :] = vacc[d, rows, :].astype(bf16)

    for ahead in range(4):
        pl.when(z == ahead)(functools.partial(case, ahead + 1))
    for s in range(SLOTS):
        dq_refs[s][...] = dqs[natural[s]]


def sum_kv(at_ref, own_ref, later_ref, *outs):
    total = (own_ref[...].astype(f32) + later_ref[...].astype(f32)).astype(bf16)
    for s in range(SLOTS):
        outs[s][...] = total[s * KV_ROWS : (s + 1) * KV_ROWS]


def pack(heads_of, at_ref, sel_ref, *refs):
    y = at_ref[0]
    parts, near, far = refs[:8], refs[8:12], refs[12:16]
    for doc in range(2):
        sel = sel_ref[doc]
        for slot in range(SLOTS):
            for row, place_of in heads_of(lax.rem(y + slot, SLOTS)):
                rows = parts[doc * SLOTS + slot][row : row + TOK, :]
                picked = dot(sel, rows, ((1,), (0,))).astype(bf16)
                for kx in range(4):
                    for outs, half in ((near, 0), (far, 1)):
                        first = (kx * 2 + half) * CAP
                        outs[kx][doc, :, aligned(place_of, HD)] = picked[first : first + CAP]


def query_heads(group):
    return [(h * TOK, group * GROUP + h) for h in range(GROUP)]


def kv_heads(group):
    return [(0, group), (TOK, KVH + group)]


def put(at_ref, pieces, out, sem, dz, columns):
    x, c, zh = at_ref[2], at_ref[3], at_ref[4]
    copies = []
    for kx in range(4):
        for cc in range(2):
            doc = lax.rem(zh + dz, 2) * 8 + lax.rem(x + 4 - kx, 4) * 2 + lax.rem(c + cc, 2)
            copies.append(
                pltpu.make_async_copy(
                    pieces[kx].at[cc], out.at[doc, :, columns], sem.at[kx * 2 + cc]
                )
            )
    return copies


QUERY_COLS = pl.ds(0, QH * HD)
KV_COLS = pl.ds(QH * HD, 2 * KVH * HD)


def place_first(at_ref, *refs):
    queries, kvs, query_far, out, sem = refs[:4], refs[4:8], refs[8], refs[9], refs[10]
    copies = put(at_ref, queries, out, sem.at[0], 0, QUERY_COLS)
    copies += put(at_ref, kvs, out, sem.at[1], 0, KV_COLS)
    copies += put(at_ref, [query_far.at[k] for k in range(4)], out, sem.at[2], 1, QUERY_COLS)
    for copy in copies:
        copy.start()
    for copy in copies:
        copy.wait()


def place_last(at_ref, kv_far, before, out, sem):
    copies = put(at_ref, [kv_far.at[k] for k in range(4)], out, sem, 1, KV_COLS)
    for copy in copies:
        copy.start()
    for copy in copies:
        copy.wait()


ANY = pl.BlockSpec(memory_space=pl.ANY)


def call(kernel, ins, outs, scratch=(), out_specs=None, aliases=None, limit=SMALL):
    return pl.pallas_call(
        kernel,
        out_shape=outs,
        in_specs=[SMEM] + ([VMEM] * ins if isinstance(ins, int) else ins),
        out_specs=out_specs or [VMEM] * len(outs),
        scratch_shapes=list(scratch),
        input_output_aliases=aliases or {},
        compiler_params=pltpu.CompilerParams(vmem_limit_bytes=limit),
    )


def shaped(*shape, dtype=bf16):
    return jax.ShapeDtypeStruct(shape, dtype)


def selection(lens, owners, targets):
    before = jnp.arange(16)[:, None] < jnp.arange(16)[None, :]
    starts = jnp.sum(jnp.where(before, lens[:, None], 0), axis=0)
    owned = owners[None, :] == targets[:, None]
    start = jnp.sum(jnp.where(owned, starts[None, :], 0), axis=1)
    size = jnp.sum(jnp.where(owned, lens[None, :], 0), axis=1)
    slot = jnp.arange(CAP)
    row = jnp.where(slot[None, :] < size[:, None], start[:, None] + slot[None, :], -1)
    return (row.reshape(-1)[:, None] == jnp.arange(TOK)[None, :]).astype(bf16)


def body(queries, keys, values, outputs, out_grads, lengths, owners):
    y, z = lax.axis_index("y"), lax.axis_index("zl")
    x, c, zh = lax.axis_index("x"), lax.axis_index("c"), lax.axis_index("zh")
    at = jnp.stack([y, z, x, c, zh]).astype(jnp.int32)

    def shift(a, axis, by):
        size = lax.axis_size(axis)
        return lax.ppermute(a, axis, [(i, (i + by) % size) for i in range(size)])

    kv = call(split_kv, 2, [shaped(KV_ROWS, HD)] * 4)(at, keys[0], values[0])
    kv_own = jnp.concatenate([kv[0]] + [shift(kv[k], "y", k) for k in (1, 2, 3)], axis=0)
    kv_all = [kv_own]
    for d in (1, 2, 3):
        kv_all.append(lax.ppermute(kv_all[-1], "zl", [(i, i + 1) for i in range(d - 1, 3)]))
    qd = call(split_qd, [VMEM] * 3 + [ANY], [shaped(QD_ROWS, HD)] * 4)(
        at, queries[0], outputs[0], out_grads[0], kv_own
    )
    qd_all = [qd[0]] + [shift(qd[k], "y", k) for k in (1, 2, 3)]

    meta = jnp.stack([lengths[0, 0], owners[0, 0]])
    meta, *qd_all = lax.optimization_barrier((meta, *qd_all))
    other = shift(meta, "c", 1)
    near = jnp.arange(8)
    targets = lax.rem(zh + near % 2, 2) * 8 + lax.rem(x + near // 2, 4) * 2 + c
    sel = jnp.stack([selection(meta[0], meta[1], targets), selection(other[0], other[1], targets)])

    grads = call(
        attention_grads,
        8,
        [shaped(QROWS, HD)] * 4 + [shaped(4 * KV_ROWS, HD)] * 4,
        [
            pltpu.VMEM((SLOTS, QD_ROWS, HD), bf16),
            pltpu.VMEM((4, BLK, HD), bf16),
            pltpu.VMEM((4, BLK, HD), bf16),
            pltpu.VMEM((4, BLK, HD), f32),
            pltpu.VMEM((4, BLK, HD), f32),
            pltpu.VMEM((SLOTS, QROWS, HD), bf16),
            pltpu.VMEM((TOK, QROWS), jnp.int32),
        ],
        limit=LARGE,
    )(at, *qd_all, *kv_all)
    dq, dkv = grads[:4], grads[4:]
    dkv_part = lax.ppermute(dkv[3], "zl", [(3, 2)])
    for d in (2, 1):
        dkv_part = (dkv[d].astype(f32) + dkv_part.astype(f32)).astype(bf16)
        dkv_part = lax.ppermute(dkv_part, "zl", [(i, i - 1) for i in range(d, 4)])

    def along_x(pieces):
        return [pieces[0]] + [shift(pieces[k], "x", k) for k in (1, 2, 3)]

    def packed(heads_of, parts, others, columns):
        out = call(
            functools.partial(pack, heads_of), 9, [shaped(2, CAP, columns)] * 8
        )(at, sel, *parts, *others)
        return out[:4], out[4:]

    dq_back = [dq[0]] + [shift(dq[k], "y", 4 - k) for k in (1, 2, 3)]
    dq_other = [shift(a, "c", 1) for a in dq_back]
    q_near, q_far = packed(query_heads, dq_back, dq_other, QH * HD)
    q_far = jnp.stack(along_x(q_far))
    q_far_in = shift(q_far, "zh", 1)
    q_near = along_x(q_near)

    slots = call(sum_kv, 2, [shaped(KV_ROWS, HD)] * 4)(at, dkv[0], dkv_part)
    dkv_back = [slots[0]] + [shift(slots[k], "y", 4 - k) for k in (1, 2, 3)]
    dkv_other = [shift(a, "c", 1) for a in dkv_back]
    kv_near, kv_far = packed(kv_heads, dkv_back, dkv_other, 2 * KVH * HD)
    kv_far = jnp.stack(along_x(kv_far))
    kv_far_in = shift(kv_far, "zh", 1)
    kv_near = along_x(kv_near)

    whole = shaped(16, CAP, (QH + 2 * KVH) * HD)
    returned = call(
        place_first, 9, whole, [pltpu.SemaphoreType.DMA((3, 8))], ANY
    )(at, *q_near, *kv_near, q_far_in)
    returned = call(
        place_last, [VMEM, ANY], whole, [pltpu.SemaphoreType.DMA((8,))], ANY, {2: 0}
    )(at, kv_far_in, returned)
    return returned[None, None]


def solution(mesh):
    split = Mesh(mesh.devices.reshape(2, 4, 2, 4, 4), ("zh", "x", "c", "zl", "y"))
    rows = P(("zh", "x", "c"), ("zl", "y"), None)
    return jax.shard_map(
        body,
        mesh=split,
        in_specs=(rows,) * 7,
        out_specs=P(("zh", "x", "c"), ("zl", "y"), None, None, None),
        check_vma=False,
    )
```

time: 157 us -> 138 us (0.88)
  the two profiles are of different devices: /device:TPU:1 before, /device:TPU:119 now
where the time goes in v2:
time: 138 us
  waiting for transfers between devices  53.8 us (39%)
  starting transfers between devices  53.6 us (39%)
  Pallas kernels  23.7 us (17%)
  local copies, waits for them, and re-layouts  5.23 us (4%)
    ppermute x35, starting transfers between devices, shift(): return lax.ppermute(a, axis, [(i, (i + by) % size) for i in range(size)])  42.2 us
    ppermute x35, waiting for transfers between devices, shift(): return lax.ppermute(a, axis, [(i, (i + by) % size) for i in range(size)])  38.7 us
    pallas_call x1, Pallas kernels, body(): call(attention_grads, 8, [shaped(QROWS, HD)] * 4 + [shaped(4 * KV_ROWS, H...  16.3 us
    ppermute x3, waiting for transfers between devices, body(): lax.ppermute(kv_all[-1], 'zl', [(i, i + 1) for i in range(d - 1, 3)])  8.44 us
    ppermute x2, starting transfers between devices, body(): dkv_part = lax.ppermute(dkv_part, 'zl', [(i, i - 1) for i in range(d, 4)])  6.26 us
    unnamed x17, local copies, waits for them, and re-layouts  4.96 us
    ppermute x1, waiting for transfers between devices, body(): dkv_part = lax.ppermute(dkv[3], 'zl', [(3, 2)])  4.8 us
    ppermute x3, starting transfers between devices, body(): lax.ppermute(kv_all[-1], 'zl', [(i, i + 1) for i in range(d - 1, 3)])  3.85 us
  transfers between devices with their start and end apart: 41, of which 21 were waited for; matrix products, arithmetic and copies ran while one was open for 1% of the time, Pallas kernels for 16%

profile of v2, /device:TPU:119, one launch (start us, length us, event | category | flops | bytes accessed | tf_op | source)
XLA Modules:
  0.0 137.7 jit_solution(7202497520356603793)
XLA Ops:
  5.7 2.5 %collective-permute-done.1 = bf16[256,128]{1,0:T(8,128)(2,1)S(1)} collective-permute-done((bf16[256,128]{1,0:T(8,128)(2,1)S(1)}, bf16[256,128]{1,0:T(8,128)(2,1)S(1)}, u32[]{:S(2)}, u32[]{:S(2)}) %collective-permute-start.1) | collective-permute-done | bytes 65568 | tf_op jit(solution)/shard_map/ppermute | solution.py:248
  13.9 2.1 %collective-permute-start.3 = (bf16[1040,128]{1,0:T(8,128)(2,1)S(1)}, bf16[1040,128]{1,0:T(8,128)(2,1)S(1)}, u32[]{:S(2)}, u32[]{:S(2)}) collective-permute-start(bf16[1040,128]{1,0:T(8,128)(2,1)S(1)} %get-tuple-element.51), channel_id=1, source_target_pairs={{0,1},{1,2},{2,3},{3,0},{4,5},{5,6},{6,7},{7,4},{8,9},{9,10},{10,1... | collective-permute-start | bytes 798728 | tf_op jit(solution)/shard_map/ppermute | solution.py:248
  16.0 1.8 %collective-permute-start.5 = (bf16[1040,128]{1,0:T(8,128)(2,1)S(1)}, bf16[1040,128]{1,0:T(8,128)(2,1)S(1)}, u32[]{:S(2)}, u32[]{:S(2)}) collective-permute-start(bf16[1040,128]{1,0:T(8,128)(2,1)S(1)} %get-tuple-element.53), channel_id=1, source_target_pairs={{0,3},{1,0},{2,1},{3,2},{4,7},{5,4},{6,5},{7,6},{8,11},{9,8},{10,9... | collective-permute-start | bytes 798728 | tf_op jit(solution)/shard_map/ppermute | solution.py:248
  19.7 6.1 %collective-permute-done.4.refs_2_ = bf16[1040,128]{1,0:T(8,128)(2,1)S(1)} collective-permute-done((bf16[1040,128]{1,0:T(8,128)(2,1)S(1)}, bf16[1040,128]{1,0:T(8,128)(2,1)S(1)}, u32[]{:S(2)}, u32[]{:S(2)}) %collective-permute-start.4) | collective-permute-done | bytes 266272 | tf_op jit(solution)/shard_map/ppermute | solution.py:248
  25.8 2.3 %collective-permute-done.5.refs_3_ = bf16[1040,128]{1,0:T(8,128)(2,1)S(1)} collective-permute-done((bf16[1040,128]{1,0:T(8,128)(2,1)S(1)}, bf16[1040,128]{1,0:T(8,128)(2,1)S(1)}, u32[]{:S(2)}, u32[]{:S(2)}) %collective-permute-start.5) | collective-permute-done | bytes 266272 | tf_op jit(solution)/shard_map/ppermute | solution.py:248
  28.2 2.1 %collective-permute-start.6 = (s32[2,16]{1,0:T(2,128)S(1)}, s32[2,16]{1,0:T(2,128)S(1)}, u32[]{:S(2)}, u32[]{:S(2)}) collective-permute-start(s32[2,16]{1,0:T(2,128)S(1)} %pad_add_fusion), channel_id=1, source_target_pairs={{0,16},{16,0},{1,17},{17,1},{2,18},{18,2},{3,19},{19,3},{4,20},{20... | collective-permute-start | bytes 392 | tf_op jit(solution)/shard_map/ppermute | solution.py:248
  31.7 8.4 %collective-permute-done.9.refs_7_ = bf16[1024,128]{1,0:T(8,128)(2,1)S(1)} collective-permute-done((bf16[1024,128]{1,0:T(8,128)(2,1)S(1)}, bf16[1024,128]{1,0:T(8,128)(2,1)S(1)}, u32[]{:S(2)}, u32[]{:S(2)}) %collective-permute-start.9) | collective-permute-done | bytes 262176 | tf_op jit(solution)/shard_map/ppermute | solution.py:254
  40.1 16.3 %shard_map.75 = (bf16[512,128]{1,0:T(8,128)(2,1)S(1)}, bf16[512,128]{1,0:T(8,128)(2,1)S(1)}, bf16[512,128]{1,0:T(8,128)(2,1)S(1)}, bf16[512,128]{1,0:T(8,128)(2,...) custom-call(s32[5]{0:T(128)S(1)} %stack.63.at_ref, ...), custom_call_target="tpu_custom_call" | custom-call | tf_op jit(solution)/shard_map/pallas_call | solution.py:267
  58.1 4.8 %collective-permute-done.10 = bf16[1024,128]{1,0:T(8,128)(2,1)S(1)} collective-permute-done((bf16[1024,128]{1,0:T(8,128)(2,1)S(1)}, bf16[1024,128]{1,0:T(8,128)(2,1)S(1)}, u32[]{:S(2)}, u32[]{:S(2)}) %collective-permute-start.10) | collective-permute-done | bytes 262176 | tf_op jit(solution)/shard_map/ppermute | solution.py:283
  63.0 4.1 %collective-permute-start.11 = (bf16[1024,128]{1,0:T(8,128)(2,1)S(1)}, bf16[1024,128]{1,0:T(8,128)(2,1)S(1)}, u32[]{:S(2)}, u32[]{:S(2)}) collective-permute-start(bf16[1024,128]{1,0:T(8,128)(2,1)S(1)} %add_convert_fusion.1), channel_id=1, source_target_pairs={{8,4},{12,8},{9,5},{13,9},{10,6},{14,10},{11,7},{15,11},{24,20},{2... | collective-permute-start | bytes 786440 | tf_op jit(solution)/shard_map/ppermute | solution.py:286
  68.5 2.9 %collective-permute-start.25 = (bf16[512,128]{1,0:T(8,128)(2,1)S(1)}, bf16[512,128]{1,0:T(8,128)(2,1)S(1)}, u32[]{:S(2)}, u32[]{:S(2)}) collective-permute-start(bf16[512,128]{1,0:T(8,128)(2,1)S(1)} %get-tuple-element.73), channel_id=1, source_target_pairs={{0,2},{1,3},{2,0},{3,1},{4,6},{5,7},{6,4},{7,5},{8,10},{9,11},{10,... | collective-permute-start | bytes 393224 | tf_op jit(solution)/shard_map/ppermute | solution.py:248
  71.5 2.3 %collective-permute-start.27 = (bf16[512,128]{1,0:T(8,128)(2,1)S(1)}, bf16[512,128]{1,0:T(8,128)(2,1)S(1)}, u32[]{:S(2)}, u32[]{:S(2)}) collective-permute-start(bf16[512,128]{1,0:T(8,128)(2,1)S(1)} %get-tuple-element.71.refs_0_), channel_id=1, source_target_pairs={{0,16},{16,0},{1,17},{17,1},{2,18},{18,2},{3,19},{19,3},{4,20},{20... | collective-permute-start | bytes 393224 | tf_op jit(solution)/shard_map/ppermute | solution.py:248
  73.8 1.8 %collective-permute-start.28 = (bf16[512,128]{1,0:T(8,128)(2,1)S(1)}, bf16[512,128]{1,0:T(8,128)(2,1)S(1)}, u32[]{:S(2)}, u32[]{:S(2)}) collective-permute-start(bf16[512,128]{1,0:T(8,128)(2,1)S(1)} %collective-permute-done.24.refs_1_), channel_id=1, source_target_pairs={{0,16},{16,0},{1,17},{17,1},{2,18},{18,2},{3,19},{19,3},{4,20},{20... | collective-permute-start | bytes 393224 | tf_op jit(solution)/shard_map/ppermute | solution.py:248
  78.8 2.1 %collective-permute-start.12 = (bf16[1024,128]{1,0:T(8,128)(2,1)S(1)}, bf16[1024,128]{1,0:T(8,128)(2,1)S(1)}, u32[]{:S(2)}, u32[]{:S(2)}) collective-permute-start(bf16[1024,128]{1,0:T(8,128)(2,1)S(1)} %add_convert_fusion), channel_id=1, source_target_pairs={{4,0},{8,4},{12,8},{5,1},{9,5},{13,9},{6,2},{10,6},{14,10},{7,3},{... | collective-permute-start | bytes 786440 | tf_op jit(solution)/shard_map/ppermute | solution.py:286
  82.4 2.1 %collective-permute-start.38 = (bf16[2,16,2048]{2,1,0:T(8,128)(2,1)S(1)}, bf16[2,16,2048]{2,1,0:T(8,128)(2,1)S(1)}, u32[]{:S(2)}, u32[]{:S(2)}) collective-permute-start(bf16[2,16,2048]{2,1,0:T(8,128)(2,1)S(1)} %get-tuple-element.85), channel_id=1, source_target_pairs={{0,64},{32,96},{64,0},{96,32},{1,65},{33,97},{65,1},{97,33},{2,66}... | collective-permute-start | bytes 393224 | tf_op jit(solution)/shard_map/ppermute | solution.py:248
  84.5 1.9 %collective-permute-done.12.later_ref = bf16[1024,128]{1,0:T(8,128)(2,1)S(1)} collective-permute-done((bf16[1024,128]{1,0:T(8,128)(2,1)S(1)}, bf16[1024,128]{1,0:T(8,128)(2,1)S(1)}, u32[]{:S(2)}, u32[]{:S(2)}) %collective-permute-start.12) | collective-permute-done | bytes 262176 | tf_op jit(solution)/shard_map/ppermute | solution.py:286
  87.4 3.0 %collective-permute-start.14 = (bf16[256,128]{1,0:T(8,128)(2,1)S(1)}, bf16[256,128]{1,0:T(8,128)(2,1)S(1)}, u32[]{:S(2)}, u32[]{:S(2)}) collective-permute-start(bf16[256,128]{1,0:T(8,128)(2,1)S(1)} %get-tuple-element.65), channel_id=1, source_target_pairs={{0,2},{1,3},{2,0},{3,1},{4,6},{5,7},{6,4},{7,5},{8,10},{9,11},{10,... | collective-permute-start | bytes 196616 | tf_op jit(solution)/shard_map/ppermute | solution.py:248
  92.0 4.3 %collective-permute-start.40 = (bf16[4,2,16,2048]{3,2,1,0:T(8,128)(2,1)S(1)}, bf16[4,2,16,2048]{3,2,1,0:T(8,128)(2,1)S(1)}, u32[]{:S(2)}, u32[]{:S(2)}) collective-permute-start(bf16[4,2,16,2048]{3,2,1,0:T(8,128)(2,1)S(1)} %pad_maximum_fusion), channel_id=1, source_target_pairs={{0,128},{128,0},{1,129},{129,1},{2,130},{130,2},{3,131},{131,3},{4... | collective-permute-start | bytes 1572872 | tf_op jit(solution)/shard_map/ppermute | solution.py:248
  96.3 1.9 %collective-permute-start.16 = (bf16[256,128]{1,0:T(8,128)(2,1)S(1)}, bf16[256,128]{1,0:T(8,128)(2,1)S(1)}, u32[]{:S(2)}, u32[]{:S(2)}) collective-permute-start(bf16[256,128]{1,0:T(8,128)(2,1)S(1)} %get-tuple-element.63.refs_0_), channel_id=1, source_target_pairs={{0,16},{16,0},{1,17},{17,1},{2,18},{18,2},{3,19},{19,3},{4,20},{20... | collective-permute-start | bytes 196616 | tf_op jit(solution)/shard_map/ppermute | solution.py:248
  104.4 2.5 %collective-permute-done.21 = bf16[2,16,1024]{2,1,0:T(8,128)(2,1)S(1)} collective-permute-done((bf16[2,16,1024]{2,1,0:T(8,128)(2,1)S(1)}, bf16[2,16,1024]{2,1,0:T(8,128)(2,1)S(1)}, u32[]{:S(2)}, u32[]{:S(2)}) %collective-permute-start.21) | collective-permute-done | bytes 65568 | tf_op jit(solution)/shard_map/ppermute | solution.py:248
  111.3 2.2 %collective-permute-done.31.refs_1_ = bf16[2,16,2048]{2,1,0:T(8,128)(2,1)S(1)} collective-permute-done((bf16[2,16,2048]{2,1,0:T(8,128)(2,1)S(1)}, bf16[2,16,2048]{2,1,0:T(8,128)(2,1)S(1)}, u32[]{:S(2)}, u32[]{:S(2)}) %collective-permute-start.31) | collective-permute-done | bytes 131104 | tf_op jit(solution)/shard_map/ppermute | solution.py:248
  118.9 2.0 %collective-permute-done.35.refs_6_ = bf16[2,16,1024]{2,1,0:T(8,128)(2,1)S(1)} collective-permute-done((bf16[2,16,1024]{2,1,0:T(8,128)(2,1)S(1)}, bf16[2,16,1024]{2,1,0:T(8,128)(2,1)S(1)}, u32[]{:S(2)}, u32[]{:S(2)}) %collective-permute-start.35) | collective-permute-done | bytes 65568 | tf_op jit(solution)/shard_map/ppermute | solution.py:248
  122.3 1.8 %shard_map.79.before = bf16[16,16,3072]{2,1,0:T(8,128)(2,1)} custom-call(s32[5]{0:T(128)S(1)} %stack.63.at_ref, bf16[2,16,2048]{2,1,0:T(8,128)(2,1)S(1)} %get-tuple-element.75.refs_0_, bf16[2,16,2048]{2,1,0:T(8,128)(2,1)S(1)} %collective-permute-done.31.refs_1_, bf16[2,16,2048]{2,1,0:T(8,128)(2,1)S(1)} %collective-permute-done.32.refs_2_, ...), custom_call_target="tpu_custom_call" | custom-call | tf_op jit(solution)/shard_map/pallas_call | solution.py:313
  124.2 12.0 %collective-permute-done.23.kv_far = bf16[4,2,16,1024]{3,2,1,0:T(8,128)(2,1)S(1)} collective-permute-done((bf16[4,2,16,1024]{3,2,1,0:T(8,128)(2,1)S(1)}, bf16[4,2,16,1024]{3,2,1,0:T(8,128)(2,1)S(1)}, u32[]{:S(2)}, u32[]{:S(2)}) %collective-permute-start.23) | collective-permute-done | bytes 262176 | tf_op jit(solution)/shard_map/ppermute | solution.py:248
  (102 shorter events, 43.8 us)
Async XLA Ops:
  8.2 9.5 %collective-permute-start.7 = (bf16[1024,128]{1,0:T(8,128)(2,1)S(1)}, bf16[1024,128]{1,0:T(8,128)(2,1)S(1)}, u32[]{:S(2)}, u32[]{:S(2)}) collective-permute-start(bf16[1024,128]{1,0:T(8,128)(2,1)S(1)} %constant_dynamic-update-slice_fusion.after_ref.refs_4_), channel_id=1, source_target_pairs={{0,4},{4,8},{8,12},{1,5},{5,9},{9,13},{2,6},{6,10},{10,14},{3,7},{... | collective-permute-start | bytes 786440 | tf_op jit(solution)/shard_map/ppermute | solution.py:254
  13.9 5.8 %collective-permute-start.3 = (bf16[1040,128]{1,0:T(8,128)(2,1)S(1)}, bf16[1040,128]{1,0:T(8,128)(2,1)S(1)}, u32[]{:S(2)}, u32[]{:S(2)}) collective-permute-start(bf16[1040,128]{1,0:T(8,128)(2,1)S(1)} %get-tuple-element.51), channel_id=1, source_target_pairs={{0,1},{1,2},{2,3},{3,0},{4,5},{5,6},{6,7},{7,4},{8,9},{9,10},{10,1... | collective-permute-start | bytes 798728 | tf_op jit(solution)/shard_map/ppermute | solution.py:248
  16.0 9.9 %collective-permute-start.4 = (bf16[1040,128]{1,0:T(8,128)(2,1)S(1)}, bf16[1040,128]{1,0:T(8,128)(2,1)S(1)}, u32[]{:S(2)}, u32[]{:S(2)}) collective-permute-start(bf16[1040,128]{1,0:T(8,128)(2,1)S(1)} %get-tuple-element.52), channel_id=1, source_target_pairs={{0,2},{1,3},{2,0},{3,1},{4,6},{5,7},{6,4},{7,5},{8,10},{9,11},{10,... | collective-permute-start | bytes 798728 | tf_op jit(solution)/shard_map/ppermute | solution.py:248
  16.0 12.2 %collective-permute-start.5 = (bf16[1040,128]{1,0:T(8,128)(2,1)S(1)}, bf16[1040,128]{1,0:T(8,128)(2,1)S(1)}, u32[]{:S(2)}, u32[]{:S(2)}) collective-permute-start(bf16[1040,128]{1,0:T(8,128)(2,1)S(1)} %get-tuple-element.53), channel_id=1, source_target_pairs={{0,3},{1,0},{2,1},{3,2},{4,7},{5,4},{6,5},{7,6},{8,11},{9,8},{10,9... | collective-permute-start | bytes 798728 | tf_op jit(solution)/shard_map/ppermute | solution.py:248
  17.7 12.5 %collective-permute-start.8 = (bf16[1024,128]{1,0:T(8,128)(2,1)S(1)}, bf16[1024,128]{1,0:T(8,128)(2,1)S(1)}, u32[]{:S(2)}, u32[]{:S(2)}) collective-permute-start(bf16[1024,128]{1,0:T(8,128)(2,1)S(1)} %collective-permute-done.7.refs_5_), channel_id=1, source_target_pairs={{4,8},{8,12},{5,9},{9,13},{6,10},{10,14},{7,11},{11,15},{20,24},{2... | collective-permute-start | bytes 786440 | tf_op jit(solution)/shard_map/ppermute | solution.py:254
  28.2 29.6 %collective-permute-start.6 = (s32[2,16]{1,0:T(2,128)S(1)}, s32[2,16]{1,0:T(2,128)S(1)}, u32[]{:S(2)}, u32[]{:S(2)}) collective-permute-start(s32[2,16]{1,0:T(2,128)S(1)} %pad_add_fusion), channel_id=1, source_target_pairs={{0,16},{16,0},{1,17},{17,1},{2,18},{18,2},{3,19},{19,3},{4,20},{20... | collective-permute-start | bytes 392 | tf_op jit(solution)/shard_map/ppermute | solution.py:248
  30.3 9.8 %collective-permute-start.9 = (bf16[1024,128]{1,0:T(8,128)(2,1)S(1)}, bf16[1024,128]{1,0:T(8,128)(2,1)S(1)}, u32[]{:S(2)}, u32[]{:S(2)}) collective-permute-start(bf16[1024,128]{1,0:T(8,128)(2,1)S(1)} %collective-permute-done.8.refs_6_), channel_id=1, source_target_pairs={{8,12},{9,13},{10,14},{11,15},{24,28},{25,29},{26,30},{27,31},{40,... | collective-permute-start | bytes 786440 | tf_op jit(solution)/shard_map/ppermute | solution.py:254
  56.5 6.4 %collective-permute-start.10 = (bf16[1024,128]{1,0:T(8,128)(2,1)S(1)}, bf16[1024,128]{1,0:T(8,128)(2,1)S(1)}, u32[]{:S(2)}, u32[]{:S(2)}) collective-permute-start(bf16[1024,128]{1,0:T(8,128)(2,1)S(1)} %get-tuple-element.62), channel_id=1, source_target_pairs={{12,8},{13,9},{14,10},{15,11},{28,24},{29,25},{30,26},{31,27},{44,... | collective-permute-start | bytes 786440 | tf_op jit(solution)/shard_map/ppermute | solution.py:283
  63.0 15.8 %collective-permute-start.11 = (bf16[1024,128]{1,0:T(8,128)(2,1)S(1)}, bf16[1024,128]{1,0:T(8,128)(2,1)S(1)}, u32[]{:S(2)}, u32[]{:S(2)}) collective-permute-start(bf16[1024,128]{1,0:T(8,128)(2,1)S(1)} %add_convert_fusion.1), channel_id=1, source_target_pairs={{8,4},{12,8},{9,5},{13,9},{10,6},{14,10},{11,7},{15,11},{24,20},{2... | collective-permute-start | bytes 786440 | tf_op jit(solution)/shard_map/ppermute | solution.py:286
  67.3 6.5 %collective-permute-start.24 = (bf16[512,128]{1,0:T(8,128)(2,1)S(1)}, bf16[512,128]{1,0:T(8,128)(2,1)S(1)}, u32[]{:S(2)}, u32[]{:S(2)}) collective-permute-start(bf16[512,128]{1,0:T(8,128)(2,1)S(1)} %get-tuple-element.72), channel_id=1, source_target_pairs={{0,3},{1,0},{2,1},{3,2},{4,7},{5,4},{6,5},{7,6},{8,11},{9,8},{10,9... | collective-permute-start | bytes 393224 | tf_op jit(solution)/shard_map/ppermute | solution.py:248
  68.5 7.1 %collective-permute-start.25 = (bf16[512,128]{1,0:T(8,128)(2,1)S(1)}, bf16[512,128]{1,0:T(8,128)(2,1)S(1)}, u32[]{:S(2)}, u32[]{:S(2)}) collective-permute-start(bf16[512,128]{1,0:T(8,128)(2,1)S(1)} %get-tuple-element.73), channel_id=1, source_target_pairs={{0,2},{1,3},{2,0},{3,1},{4,6},{5,7},{6,4},{7,5},{8,10},{9,11},{10,... | collective-permute-start | bytes 393224 | tf_op jit(solution)/shard_map/ppermute | solution.py:248
  71.4 5.9 %collective-permute-start.26 = (bf16[512,128]{1,0:T(8,128)(2,1)S(1)}, bf16[512,128]{1,0:T(8,128)(2,1)S(1)}, u32[]{:S(2)}, u32[]{:S(2)}) collective-permute-start(bf16[512,128]{1,0:T(8,128)(2,1)S(1)} %get-tuple-element.74), channel_id=1, source_target_pairs={{0,1},{1,2},{2,3},{3,0},{4,5},{5,6},{6,7},{7,4},{8,9},{9,10},{10,1... | collective-permute-start | bytes 393224 | tf_op jit(solution)/shard_map/ppermute | solution.py:248
  71.5 9.6 %collective-permute-start.27 = (bf16[512,128]{1,0:T(8,128)(2,1)S(1)}, bf16[512,128]{1,0:T(8,128)(2,1)S(1)}, u32[]{:S(2)}, u32[]{:S(2)}) collective-permute-start(bf16[512,128]{1,0:T(8,128)(2,1)S(1)} %get-tuple-element.71.refs_0_), channel_id=1, source_target_pairs={{0,16},{16,0},{1,17},{17,1},{2,18},{18,2},{3,19},{19,3},{4,20},{20... | collective-permute-start | bytes 393224 | tf_op jit(solution)/shard_map/ppermute | solution.py:248
  73.8 7.3 %collective-permute-start.28 = (bf16[512,128]{1,0:T(8,128)(2,1)S(1)}, bf16[512,128]{1,0:T(8,128)(2,1)S(1)}, u32[]{:S(2)}, u32[]{:S(2)}) collective-permute-start(bf16[512,128]{1,0:T(8,128)(2,1)S(1)} %collective-permute-done.24.refs_1_), channel_id=1, source_target_pairs={{0,16},{16,0},{1,17},{17,1},{2,18},{18,2},{3,19},{19,3},{4,20},{20... | collective-permute-start | bytes 393224 | tf_op jit(solution)/shard_map/ppermute | solution.py:248
  78.8 7.6 %collective-permute-start.12 = (bf16[1024,128]{1,0:T(8,128)(2,1)S(1)}, bf16[1024,128]{1,0:T(8,128)(2,1)S(1)}, u32[]{:S(2)}, u32[]{:S(2)}) collective-permute-start(bf16[1024,128]{1,0:T(8,128)(2,1)S(1)} %add_convert_fusion), channel_id=1, source_target_pairs={{4,0},{8,4},{12,8},{5,1},{9,5},{13,9},{6,2},{10,6},{14,10},{7,3},{... | collective-permute-start | bytes 786440 | tf_op jit(solution)/shard_map/ppermute | solution.py:286
  82.1 8.3 %collective-permute-start.37 = (bf16[2,16,2048]{2,1,0:T(8,128)(2,1)S(1)}, bf16[2,16,2048]{2,1,0:T(8,128)(2,1)S(1)}, u32[]{:S(2)}, u32[]{:S(2)}) collective-permute-start(bf16[2,16,2048]{2,1,0:T(8,128)(2,1)S(1)} %get-tuple-element.84), channel_id=1, source_target_pairs={{0,32},{32,64},{64,96},{96,0},{1,33},{33,65},{65,97},{97,1},{2,34}... | collective-permute-start | bytes 393224 | tf_op jit(solution)/shard_map/ppermute | solution.py:248
  82.4 9.5 %collective-permute-start.38 = (bf16[2,16,2048]{2,1,0:T(8,128)(2,1)S(1)}, bf16[2,16,2048]{2,1,0:T(8,128)(2,1)S(1)}, u32[]{:S(2)}, u32[]{:S(2)}) collective-permute-start(bf16[2,16,2048]{2,1,0:T(8,128)(2,1)S(1)} %get-tuple-element.85), channel_id=1, source_target_pairs={{0,64},{32,96},{64,0},{96,32},{1,65},{33,97},{65,1},{97,33},{2,66}... | collective-permute-start | bytes 393224 | tf_op jit(solution)/shard_map/ppermute | solution.py:248
  84.5 7.4 %collective-permute-start.39 = (bf16[2,16,2048]{2,1,0:T(8,128)(2,1)S(1)}, bf16[2,16,2048]{2,1,0:T(8,128)(2,1)S(1)}, u32[]{:S(2)}, u32[]{:S(2)}) collective-permute-start(bf16[2,16,2048]{2,1,0:T(8,128)(2,1)S(1)} %get-tuple-element.86), channel_id=1, source_target_pairs={{0,96},{32,0},{64,32},{96,64},{1,97},{33,1},{65,33},{97,65},{2,98}... | collective-permute-start | bytes 393224 | tf_op jit(solution)/shard_map/ppermute | solution.py:248
  87.1 11.1 %collective-permute-start.13 = (bf16[256,128]{1,0:T(8,128)(2,1)S(1)}, bf16[256,128]{1,0:T(8,128)(2,1)S(1)}, u32[]{:S(2)}, u32[]{:S(2)}) collective-permute-start(bf16[256,128]{1,0:T(8,128)(2,1)S(1)} %get-tuple-element.64), channel_id=1, source_target_pairs={{0,3},{1,0},{2,1},{3,2},{4,7},{5,4},{6,5},{7,6},{8,11},{9,8},{10,9... | collective-permute-start | bytes 196616 | tf_op jit(solution)/shard_map/ppermute | solution.py:248
  87.4 10.8 %collective-permute-start.14 = (bf16[256,128]{1,0:T(8,128)(2,1)S(1)}, bf16[256,128]{1,0:T(8,128)(2,1)S(1)}, u32[]{:S(2)}, u32[]{:S(2)}) collective-permute-start(bf16[256,128]{1,0:T(8,128)(2,1)S(1)} %get-tuple-element.65), channel_id=1, source_target_pairs={{0,2},{1,3},{2,0},{3,1},{4,6},{5,7},{6,4},{7,5},{8,10},{9,11},{10,... | collective-permute-start | bytes 196616 | tf_op jit(solution)/shard_map/ppermute | solution.py:248
  90.4 8.3 %collective-permute-start.15 = (bf16[256,128]{1,0:T(8,128)(2,1)S(1)}, bf16[256,128]{1,0:T(8,128)(2,1)S(1)}, u32[]{:S(2)}, u32[]{:S(2)}) collective-permute-start(bf16[256,128]{1,0:T(8,128)(2,1)S(1)} %get-tuple-element.66), channel_id=1, source_target_pairs={{0,1},{1,2},{2,3},{3,0},{4,5},{5,6},{6,7},{7,4},{8,9},{9,10},{10,1... | collective-permute-start | bytes 196616 | tf_op jit(solution)/shard_map/ppermute | solution.py:248
  92.0 27.0 %collective-permute-start.40 = (bf16[4,2,16,2048]{3,2,1,0:T(8,128)(2,1)S(1)}, bf16[4,2,16,2048]{3,2,1,0:T(8,128)(2,1)S(1)}, u32[]{:S(2)}, u32[]{:S(2)}) collective-permute-start(bf16[4,2,16,2048]{3,2,1,0:T(8,128)(2,1)S(1)} %pad_maximum_fusion), channel_id=1, source_target_pairs={{0,128},{128,0},{1,129},{129,1},{2,130},{130,2},{3,131},{131,3},{4... | collective-permute-start | bytes 1572872 | tf_op jit(solution)/shard_map/ppermute | solution.py:248
  108.6 27.6 %collective-permute-start.23 = (bf16[4,2,16,1024]{3,2,1,0:T(8,128)(2,1)S(1)}, bf16[4,2,16,1024]{3,2,1,0:T(8,128)(2,1)S(1)}, u32[]{:S(2)}, u32[]{:S(2)}) collective-permute-start(bf16[4,2,16,1024]{3,2,1,0:T(8,128)(2,1)S(1)} %pad_maximum_fusion.1), channel_id=1, source_target_pairs={{0,128},{128,0},{1,129},{129,1},{2,130},{130,2},{3,131},{131,3},{4... | collective-permute-start | bytes 786440 | tf_op jit(solution)/shard_map/ppermute | solution.py:248
  110.7 7.0 %collective-permute-start.33 = (bf16[2,16,2048]{2,1,0:T(8,128)(2,1)S(1)}, bf16[2,16,2048]{2,1,0:T(8,128)(2,1)S(1)}, u32[]{:S(2)}, u32[]{:S(2)}) collective-permute-start(bf16[2,16,2048]{2,1,0:T(8,128)(2,1)S(1)} %get-tuple-element.78), channel_id=1, source_target_pairs={{0,96},{32,0},{64,32},{96,64},{1,97},{33,1},{65,33},{97,65},{2,98}... | collective-permute-start | bytes 393224 | tf_op jit(solution)/shard_map/ppermute | solution.py:248
  (24 other events, 109.8 us)

commit v3 on v2

v3 whole, which is shorter than its diff:
```python
import functools

import jax
import jax.numpy as jnp
from jax import lax
from jax.experimental import pallas as pl
from jax.experimental.pallas import tpu as pltpu
from jax.sharding import Mesh, PartitionSpec as P

HD = 128
QH = 16
KVH = 4
GROUP = QH // KVH
TOK = 128
CAP = 16
DOCS = 16
SLOTS = 4
BLK = SLOTS * TOK
QROWS = GROUP * TOK
QD_ROWS = 2 * QROWS + 16
KV_ROWS = 2 * TOK
FACTOR = HD ** (-0.5)
LOG2E = 1.4426950408889634
f32 = jnp.float32
bf16 = jnp.bfloat16
VMEM = pl.BlockSpec(memory_space=pltpu.VMEM)
SMEM = pl.BlockSpec(memory_space=pltpu.SMEM)
SMALL, LARGE, WHOLE = 12 * 2**20, 28 * 2**20, 56 * 2**20


def aligned(index, unit):
    return pl.ds(pl.multiple_of(index * unit, unit), unit)


def split_kv(at_ref, k_ref, v_ref, *outs):
    z = at_ref[1]
    for slot in range(SLOTS):
        head = aligned(lax.rem(z + slot, SLOTS), HD)
        outs[slot][:TOK, :] = k_ref[:, head]
        outs[slot][TOK:, :] = v_ref[:, head]


def split_qd(at_ref, q_ref, o_ref, g_ref, after_ref, *outs):
    z = at_ref[1]
    lane = lax.broadcasted_iota(jnp.int32, (TOK, HD), 1)
    for slot in range(SLOTS):
        dest = lax.rem(z + slot, SLOTS)
        terms = jnp.zeros((TOK, HD), f32)
        for h in range(GROUP):
            head = aligned(dest * GROUP + h, HD)
            grad = g_ref[:, head]
            outs[slot][h * TOK : (h + 1) * TOK, :] = q_ref[:, head]
            outs[slot][QROWS + h * TOK : QROWS + (h + 1) * TOK, :] = grad
            term = jnp.sum(
                grad.astype(f32) * o_ref[:, head].astype(f32), axis=1, keepdims=True
            )
            terms = jnp.where(lax.rem(lane, GROUP) == h, term, terms)
        high = terms.astype(bf16).astype(f32)
        mid = (terms - high).astype(bf16).astype(f32)
        low = terms - high - mid
        part = lane // GROUP
        packed = jnp.where(
            part == 0, high, jnp.where(part == 1, mid, jnp.where(part == 2, low, 0.0))
        )
        outs[slot][2 * QROWS :, :] = packed.T[:16, :].astype(bf16)


def dot(a, b, dims):
    return lax.dot_general(a, b, (dims, ((), ())), preferred_element_type=f32)


def attention_grads(at_ref, *refs):
    kv_refs, qd_refs = refs[:4], refs[4:8]
    dq_refs, dkv_refs = refs[8:12], refs[12:16]
    qd, kk, vv, kacc, vacc, dqs, delta = refs[16:]
    y, z = at_ref[0], at_ref[1]
    along_z = [lax.rem(z + SLOTS - s, SLOTS) for s in range(SLOTS)]
    along_y = [aligned(lax.rem(y + SLOTS - k, SLOTS), TOK) for k in range(4)]
    for s in range(SLOTS):
        qd[along_z[s]] = qd_refs[s][...]
        for k in range(4):
            kk[along_z[s], along_y[k], :] = kv_refs[k][s * KV_ROWS : s * KV_ROWS + TOK, :]
            vv[along_z[s], along_y[k], :] = kv_refs[k][s * KV_ROWS + TOK : (s + 1) * KV_ROWS, :]
    key_at = lax.broadcasted_iota(jnp.int32, (TOK, QROWS), 0)
    query_at = lax.rem(lax.broadcasted_iota(jnp.int32, (TOK, QROWS), 1), TOK)
    delta[...] = key_at - query_at

    for part in range(SLOTS):
        query = qd[part, :QROWS, :]
        grad = qd[part, QROWS : 2 * QROWS, :]
        terms3 = qd[part, 2 * QROWS :, :].astype(f32)
        term4 = terms3[0:4] + terms3[4:8] + terms3[8:12]
        term = jnp.concatenate([term4[h : h + 1] for h in range(GROUP)], axis=1)
        scores = [dot(kk[t], query, ((1,), (1,))) for t in range(part + 1)]
        scores[part] = jnp.concatenate(
            [
                jnp.where(
                    delta[...] <= (y - other) * TOK,
                    scores[part][other * TOK : (other + 1) * TOK],
                    -jnp.inf,
                )
                for other in range(SLOTS)
            ],
            axis=0,
        )
        top = functools.reduce(
            jnp.maximum, [jnp.max(score, axis=0, keepdims=True) for score in scores]
        )
        weights = [jnp.exp2((score - top) * (FACTOR * LOG2E)) for score in scores]
        inverse = 1.0 / sum(jnp.sum(weight, axis=0, keepdims=True) for weight in weights)
        dq = jnp.zeros((QROWS, HD), f32)
        for t in range(part + 1):
            attn = weights[t] * inverse
            grad_attn = dot(vv[t], grad, ((1,), (1,)))
            low = (attn * (grad_attn - term)).astype(bf16)
            value_part = dot(attn.astype(bf16), grad, ((1,), (0,)))
            key_part = dot(low, query, ((1,), (0,)))
            if t == part:
                vacc[t] = value_part
                kacc[t] = key_part
            else:
                vacc[t] += value_part
                kacc[t] += key_part
            dq = dq + dot(low, kk[t], ((0,), (0,)))
        dqs[part] = (dq * FACTOR).astype(bf16)

    for s in range(SLOTS):
        dq_refs[s][...] = dqs[along_z[s]]
        for k in range(4):
            keys = kacc[along_z[s], along_y[k], :]
            dkv_refs[k][s * KV_ROWS : s * KV_ROWS + TOK, :] = (keys * FACTOR).astype(bf16)
            values = vacc[along_z[s], along_y[k], :]
            dkv_refs[k][s * KV_ROWS + TOK : (s + 1) * KV_ROWS, :] = values.astype(bf16)


def sum_kv(at_ref, own_ref, one_ref, two_ref, three_ref, *outs):
    total = own_ref[...].astype(f32) + one_ref[...].astype(f32)
    total = (total + two_ref[...].astype(f32) + three_ref[...].astype(f32)).astype(bf16)
    for s in range(SLOTS):
        outs[s][...] = total[s * KV_ROWS : (s + 1) * KV_ROWS]


def pack(at_ref, sel_ref, *refs):
    z = at_ref[1]
    queries, kvs, out = refs[:4], refs[4:8], refs[8]
    sel = sel_ref[...]

    def put(rows, place_of):
        picked = dot(sel, rows, ((1,), (0,))).astype(bf16)
        out[:, :, aligned(place_of, HD)] = picked.reshape(DOCS, CAP, HD)

    for slot in range(SLOTS):
        group = lax.rem(z + slot, SLOTS)
        for h in range(GROUP):
            put(queries[slot][h * TOK : (h + 1) * TOK, :], group * GROUP + h)
        put(kvs[slot][:TOK, :], QH + group)
        put(kvs[slot][TOK:, :], QH + KVH + group)


ANY = pl.BlockSpec(memory_space=pl.ANY)


def call(kernel, ins, outs, scratch=(), out_specs=None, aliases=None, limit=SMALL):
    return pl.pallas_call(
        kernel,
        out_shape=outs,
        in_specs=[SMEM] + ([VMEM] * ins if isinstance(ins, int) else ins),
        out_specs=out_specs or [VMEM] * len(outs),
        scratch_shapes=list(scratch),
        input_output_aliases=aliases or {},
        compiler_params=pltpu.CompilerParams(vmem_limit_bytes=limit),
    )


def shaped(*shape, dtype=bf16):
    return jax.ShapeDtypeStruct(shape, dtype)


def selection(lens, owners, targets):
    before = jnp.arange(16)[:, None] < jnp.arange(16)[None, :]
    starts = jnp.sum(jnp.where(before, lens[:, None], 0), axis=0)
    owned = owners[None, :] == targets[:, None]
    start = jnp.sum(jnp.where(owned, starts[None, :], 0), axis=1)
    size = jnp.sum(jnp.where(owned, lens[None, :], 0), axis=1)
    slot = jnp.arange(CAP)
    row = jnp.where(slot[None, :] < size[:, None], start[:, None] + slot[None, :], -1)
    return (row.reshape(-1)[:, None] == jnp.arange(TOK)[None, :]).astype(bf16)


def body(queries, keys, values, outputs, out_grads, lengths, owners):
    y, z = lax.axis_index("y"), lax.axis_index("zl")
    at = jnp.stack([y, z]).astype(jnp.int32)

    def shift(a, axis, by):
        size = lax.axis_size(axis)
        return lax.ppermute(a, axis, [(i, (i + by) % size) for i in range(size)])

    kv = call(split_kv, 2, [shaped(KV_ROWS, HD)] * 4, limit=WHOLE)(at, keys[0], values[0])
    kv_own = jnp.concatenate([kv[0]] + [shift(kv[k], "zl", k) for k in (1, 2, 3)], axis=0)
    kv_all = [kv_own] + [shift(kv_own, "y", k) for k in (1, 2, 3)]
    qd = call(split_qd, [VMEM] * 3 + [ANY], [shaped(QD_ROWS, HD)] * 4, limit=WHOLE)(
        at, queries[0], outputs[0], out_grads[0], kv[1]
    )
    qd_all = [qd[0]] + [shift(qd[k], "zl", k) for k in (1, 2, 3)]

    sel = selection(lengths[0, 0], owners[0, 0], jnp.arange(DOCS))

    grads = call(
        attention_grads,
        8,
        [shaped(QROWS, HD)] * 4 + [shaped(4 * KV_ROWS, HD)] * 4,
        [
            pltpu.VMEM((SLOTS, QD_ROWS, HD), bf16),
            pltpu.VMEM((4, BLK, HD), bf16),
            pltpu.VMEM((4, BLK, HD), bf16),
            pltpu.VMEM((4, BLK, HD), f32),
            pltpu.VMEM((4, BLK, HD), f32),
            pltpu.VMEM((SLOTS, QROWS, HD), bf16),
            pltpu.VMEM((TOK, QROWS), jnp.int32),
        ],
        limit=LARGE,
    )(at, *kv_all, *qd_all)
    dq, dkv = grads[:4], grads[4:]
    dkv_parts = [dkv[0]] + [shift(dkv[k], "y", 4 - k) for k in (1, 2, 3)]

    dq_back = [dq[0]] + [shift(dq[k], "zl", 4 - k) for k in (1, 2, 3)]
    slots = call(sum_kv, 4, [shaped(KV_ROWS, HD)] * 4)(at, *dkv_parts)
    dkv_back = [slots[0]] + [shift(slots[k], "zl", 4 - k) for k in (1, 2, 3)]
    rows = call(pack, 9, shaped(DOCS, CAP, (QH + 2 * KVH) * HD), out_specs=VMEM)(
        at, sel, *dq_back, *dkv_back
    )
    returned = lax.all_to_all(rows, ("zh", "x", "c"), 0, 0, tiled=True)
    return returned[None, None]


def solution(mesh):
    split = Mesh(mesh.devices.reshape(2, 4, 2, 4, 4), ("zh", "x", "c", "zl", "y"))
    rows = P(("zh", "x", "c"), ("zl", "y"), None)
    return jax.shard_map(
        body,
        mesh=split,
        in_specs=(rows,) * 7,
        out_specs=P(("zh", "x", "c"), ("zl", "y"), None, None, None),
        check_vma=False,
    )
```

time: 138 us -> 126 us (0.913)
  the two profiles are of different devices: /device:TPU:119 before, /device:TPU:1 now
where the time goes in v3:
time: 126 us; the launch traced here: 124 us
  blocking collectives  46 us (37%)
  starting transfers between devices  36.7 us (29%)
  waiting for transfers between devices  20.7 us (16%)
  Pallas kernels  16.7 us (13%)
  local copies, waits for them, and re-layouts  2.23 us (2%)
    all_to_all x1, blocking collectives, body(): returned = lax.all_to_all(rows, ('zh', 'x', 'c'), 0, 0, tiled=True)  46 us
    ppermute x18, starting transfers between devices, shift(): return lax.ppermute(a, axis, [(i, (i + by) % size) for i in range(size)])  36.7 us
    ppermute x18, waiting for transfers between devices, shift(): return lax.ppermute(a, axis, [(i, (i + by) % size) for i in range(size)])  20.7 us
    pallas_call x1, Pallas kernels, body(): call(attention_grads, 8, [shaped(QROWS, HD)] * 4 + [shaped(4 * KV_ROWS, H...  10.3 us
    pallas_call x1, Pallas kernels, body(): call(split_qd, [VMEM] * 3 + [ANY], [shaped(QD_ROWS, HD)] * 4, limit=WHOLE)  2.85 us
  transfers between devices with their start and end apart: 18, of which 6 were waited for; matrix products, arithmetic and copies ran while one was open for 0% of the time, Pallas kernels for 3%

profile of v3, /device:TPU:1, one launch (start us, length us, event | category | flops | bytes accessed | tf_op | source)
XLA Modules:
  0.0 123.5 jit_solution(12180509550477399473)
XLA Ops:
  0.7 1.7 %shard_map.73 = (bf16[256,128]{1,0:T(8,128)(2,1)}, bf16[256,128]{1,0:T(8,128)(2,1)}, bf16[256,128]{1,0:T(8,128)(2,1)}, bf16[256,128]{1,0:T(8,128)(2,1)}) custom-call(s32[2]{0:T(128)} %pad_add_fusion.at_ref, bf16[128,512]{1,0:T(8,128)(2,1)} %bitcast.14, bf16[128,512]{1,0:T(8,128)(2,1)} %bitcast.15), custom_call_target="tpu_custom_call" | custom-call | tf_op jit(solution)/shard_map/pallas_call | solution.py:198
  2.4 2.5 %collective-permute-start = (bf16[256,128]{1,0:T(8,128)(2,1)}, bf16[256,128]{1,0:T(8,128)(2,1)S(1)}, u32[]{:S(2)}, u32[]{:S(2)}) collective-permute-start(bf16[256,128]{1,0:T(8,128)(2,1)} %get-tuple-element.26.after_ref), channel_id=1, source_target_pairs={{0,4},{4,8},{8,12},{12,0},{1,5},{5,9},{9,13},{13,1},{2,6},{6,10},{... | collective-permute-start | bytes 196616 | tf_op jit(solution)/shard_map/ppermute | solution.py:196
  4.9 3.0 %collective-permute-start.1 = (bf16[256,128]{1,0:T(8,128)(2,1)}, bf16[256,128]{1,0:T(8,128)(2,1)S(1)}, u32[]{:S(2)}, u32[]{:S(2)}) collective-permute-start(bf16[256,128]{1,0:T(8,128)(2,1)} %get-tuple-element.27), channel_id=1, source_target_pairs={{0,8},{4,12},{8,0},{12,4},{1,9},{5,13},{9,1},{13,5},{2,10},{6,14},... | collective-permute-start | bytes 196616 | tf_op jit(solution)/shard_map/ppermute | solution.py:196
  8.6 2.9 %shard_map.74 = (bf16[1040,128]{1,0:T(8,128)(2,1)}, bf16[1040,128]{1,0:T(8,128)(2,1)}, bf16[1040,128]{1,0:T(8,128)(2,1)}, bf16[1040,128]{1,0:T(8,128)(2,1)}) custom-call(s32[2]{0:T(128)} %pad_add_fusion.at_ref, bf16[128,2048]{1,0:T(8,128)(2,1)} %bitcast.11, bf16[128,2048]{1,0:T(8,128)(2,1)} %bitcast.12, bf16[128,2048]{1,0:T(8,128)(2,1)} %bitcast.13, ...), custom_call_target="tpu_custom_call" | custom-call | tf_op jit(solution)/shard_map/pallas_call | solution.py:201
  12.2 2.6 %collective-permute-start.8 = (bf16[1040,128]{1,0:T(8,128)(2,1)}, bf16[1040,128]{1,0:T(8,128)(2,1)S(1)}, u32[]{:S(2)}, u32[]{:S(2)}) collective-permute-start(bf16[1040,128]{1,0:T(8,128)(2,1)} %get-tuple-element.32), channel_id=1, source_target_pairs={{0,12},{4,0},{8,4},{12,8},{1,13},{5,1},{9,5},{13,9},{2,14},{6,2},{... | collective-permute-start | bytes 798728 | tf_op jit(solution)/shard_map/ppermute | solution.py:196
  14.9 1.4 %collective-permute-start.3 = (bf16[1024,128]{1,0:T(8,128)(2,1)S(1)}, bf16[1024,128]{1,0:T(8,128)(2,1)S(1)}, u32[]{:S(2)}, u32[]{:S(2)}) collective-permute-start(bf16[1024,128]{1,0:T(8,128)(2,1)S(1)} %constant_dynamic-update-slice_fusion.refs_0_), channel_id=1, source_target_pairs={{0,1},{1,2},{2,3},{3,0},{4,5},{5,6},{6,7},{7,4},{8,9},{9,10},{10,1... | collective-permute-start | bytes 786440 | tf_op jit(solution)/shard_map/ppermute | solution.py:196
  16.3 2.6 %collective-permute-start.4 = (bf16[1024,128]{1,0:T(8,128)(2,1)S(1)}, bf16[1024,128]{1,0:T(8,128)(2,1)S(1)}, u32[]{:S(2)}, u32[]{:S(2)}) collective-permute-start(bf16[1024,128]{1,0:T(8,128)(2,1)S(1)} %constant_dynamic-update-slice_fusion.refs_0_), channel_id=1, source_target_pairs={{0,2},{1,3},{2,0},{3,1},{4,6},{5,7},{6,4},{7,5},{8,10},{9,11},{10,... | collective-permute-start | bytes 786440 | tf_op jit(solution)/shard_map/ppermute | solution.py:196
  18.9 1.1 collective-permute-done.6.refs_5_
  20.0 2.7 %collective-permute-start.5 = (bf16[1024,128]{1,0:T(8,128)(2,1)S(1)}, bf16[1024,128]{1,0:T(8,128)(2,1)S(1)}, u32[]{:S(2)}, u32[]{:S(2)}) collective-permute-start(bf16[1024,128]{1,0:T(8,128)(2,1)S(1)} %constant_dynamic-update-slice_fusion.refs_0_), channel_id=1, source_target_pairs={{0,3},{1,0},{2,1},{3,2},{4,7},{5,4},{6,5},{7,6},{8,11},{9,8},{10,9... | collective-permute-start | bytes 786440 | tf_op jit(solution)/shard_map/ppermute | solution.py:196
  22.8 10.1 %collective-permute-done.7.refs_6_ = bf16[1040,128]{1,0:T(8,128)(2,1)S(1)} collective-permute-done((bf16[1040,128]{1,0:T(8,128)(2,1)}, bf16[1040,128]{1,0:T(8,128)(2,1)S(1)}, u32[]{:S(2)}, u32[]{:S(2)}) %collective-permute-start.7) | collective-permute-done | bytes 266272 | tf_op jit(solution)/shard_map/ppermute | solution.py:196
  32.9 0.9 copy-done
  33.9 10.3 %shard_map.75 = (bf16[512,128]{1,0:T(8,128)(2,1)S(1)}, bf16[512,128]{1,0:T(8,128)(2,1)S(1)}, bf16[512,128]{1,0:T(8,128)(2,1)S(1)}, bf16[512,128]{1,0:T(8,128)(2,...) custom-call(s32[2]{0:T(128)S(1)} %copy-done.1, ...), custom_call_target="tpu_custom_call" | custom-call | tf_op jit(solution)/shard_map/pallas_call | solution.py:208
  44.2 2.8 %collective-permute-start.12 = (bf16[1024,128]{1,0:T(8,128)(2,1)S(1)}, bf16[1024,128]{1,0:T(8,128)(2,1)S(1)}, u32[]{:S(2)}, u32[]{:S(2)}) collective-permute-start(bf16[1024,128]{1,0:T(8,128)(2,1)S(1)} %get-tuple-element.38), channel_id=1, source_target_pairs={{0,3},{1,0},{2,1},{3,2},{4,7},{5,4},{6,5},{7,6},{8,11},{9,8},{10,9... | collective-permute-start | bytes 786440 | tf_op jit(solution)/shard_map/ppermute | solution.py:196
  48.1 5.1 %collective-permute-start.10 = (bf16[512,128]{1,0:T(8,128)(2,1)S(1)}, bf16[512,128]{1,0:T(8,128)(2,1)S(1)}, u32[]{:S(2)}, u32[]{:S(2)}) collective-permute-start(bf16[512,128]{1,0:T(8,128)(2,1)S(1)} %get-tuple-element.35), channel_id=1, source_target_pairs={{0,8},{4,12},{8,0},{12,4},{1,9},{5,13},{9,1},{13,5},{2,10},{6,14},... | collective-permute-start | bytes 393224 | tf_op jit(solution)/shard_map/ppermute | solution.py:196
  53.4 1.2 collective-permute-start.11
  54.6 3.1 %collective-permute-start.9 = (bf16[512,128]{1,0:T(8,128)(2,1)S(1)}, bf16[512,128]{1,0:T(8,128)(2,1)S(1)}, u32[]{:S(2)}, u32[]{:S(2)}) collective-permute-start(bf16[512,128]{1,0:T(8,128)(2,1)S(1)} %get-tuple-element.34), channel_id=1, source_target_pairs={{0,12},{4,0},{8,4},{12,8},{1,13},{5,1},{9,5},{13,9},{2,14},{6,2},{... | collective-permute-start | bytes 393224 | tf_op jit(solution)/shard_map/ppermute | solution.py:196
  57.7 4.6 %collective-permute-done.14.three_ref = bf16[1024,128]{1,0:T(8,128)(2,1)S(1)} collective-permute-done((bf16[1024,128]{1,0:T(8,128)(2,1)S(1)}, bf16[1024,128]{1,0:T(8,128)(2,1)S(1)}, u32[]{:S(2)}, u32[]{:S(2)}) %collective-permute-start.14) | collective-permute-done | bytes 262176 | tf_op jit(solution)/shard_map/ppermute | solution.py:196
  63.0 4.7 %collective-permute-start.15 = (bf16[256,128]{1,0:T(8,128)(2,1)S(1)}, bf16[256,128]{1,0:T(8,128)(2,1)S(1)}, u32[]{:S(2)}, u32[]{:S(2)}) collective-permute-start(bf16[256,128]{1,0:T(8,128)(2,1)S(1)} %get-tuple-element.42), channel_id=1, source_target_pairs={{0,12},{4,0},{8,4},{12,8},{1,13},{5,1},{9,5},{13,9},{2,14},{6,2},{... | collective-permute-start | bytes 196616 | tf_op jit(solution)/shard_map/ppermute | solution.py:196
  67.7 2.6 %collective-permute-start.16 = (bf16[256,128]{1,0:T(8,128)(2,1)S(1)}, bf16[256,128]{1,0:T(8,128)(2,1)S(1)}, u32[]{:S(2)}, u32[]{:S(2)}) collective-permute-start(bf16[256,128]{1,0:T(8,128)(2,1)S(1)} %get-tuple-element.43), channel_id=1, source_target_pairs={{0,8},{4,12},{8,0},{12,4},{1,9},{5,13},{9,1},{13,5},{2,10},{6,14},... | collective-permute-start | bytes 196616 | tf_op jit(solution)/shard_map/ppermute | solution.py:196
  71.1 3.4 %collective-permute-done.16.refs_6_ = bf16[256,128]{1,0:T(8,128)(2,1)S(1)} collective-permute-done((bf16[256,128]{1,0:T(8,128)(2,1)S(1)}, bf16[256,128]{1,0:T(8,128)(2,1)S(1)}, u32[]{:S(2)}, u32[]{:S(2)}) %collective-permute-start.16) | collective-permute-done | bytes 65568 | tf_op jit(solution)/shard_map/ppermute | solution.py:196
  74.5 0.8 collective-permute-done.17.refs_7_
  75.3 1.1 shard_map.77
  76.4 46.0 %all_to_all.5 = bf16[16,16,3072]{2,1,0:T(8,128)(2,1)S(1)} all-to-all(bf16[16,16,3072]{2,1,0:T(8,128)(2,1)S(1)} %shard_map.77), channel_id=1, replica_groups=mesh['zh'=2,'x'=4,'c'=2,'zl'=4,'y'=4] {'zh','x','c'}, dimensions={0} | all-to-all | bytes 3145728 | tf_op jit(solution)/shard_map/all_to_all | solution.py:232
  122.4 1.1 copy.12
  (39 shorter events, 5.1 us)
Async XLA Ops:
  0.0 22.7 %copy-start.3 = (s32[1,1,16]{2,1,0:T(1,128)S(1)}, s32[1,1,16]{2,1,0:T(1,128)}, u32[]{:S(2)}) copy-start(s32[1,1,16]{2,1,0:T(1,128)} %param.12) | copy-start | bytes 196
  0.7 32.3 %copy-start.1 = (s32[2]{0:T(128)S(1)}, s32[2]{0:T(128)}, u32[]{:S(2)}) copy-start(s32[2]{0:T(128)} %pad_add_fusion.at_ref) | copy-start | bytes 28
  2.4 9.8 %copy-start.2 = (bf16[256,128]{1,0:T(8,128)(2,1)S(1)}, bf16[256,128]{1,0:T(8,128)(2,1)}, u32[]{:S(2)}) copy-start(bf16[256,128]{1,0:T(8,128)(2,1)} %get-tuple-element.25) | copy-start | bytes 196612
  2.4 9.8 %collective-permute-start = (bf16[256,128]{1,0:T(8,128)(2,1)}, bf16[256,128]{1,0:T(8,128)(2,1)S(1)}, u32[]{:S(2)}, u32[]{:S(2)}) collective-permute-start(bf16[256,128]{1,0:T(8,128)(2,1)} %get-tuple-element.26.after_ref), channel_id=1, source_target_pairs={{0,4},{4,8},{8,12},{12,0},{1,5},{5,9},{9,13},{13,1},{2,6},{6,10},{... | collective-permute-start | bytes 196616 | tf_op jit(solution)/shard_map/ppermute | solution.py:196
  4.9 10.0 %collective-permute-start.1 = (bf16[256,128]{1,0:T(8,128)(2,1)}, bf16[256,128]{1,0:T(8,128)(2,1)S(1)}, u32[]{:S(2)}, u32[]{:S(2)}) collective-permute-start(bf16[256,128]{1,0:T(8,128)(2,1)} %get-tuple-element.27), channel_id=1, source_target_pairs={{0,8},{4,12},{8,0},{12,4},{1,9},{5,13},{9,1},{13,5},{2,10},{6,14},... | collective-permute-start | bytes 196616 | tf_op jit(solution)/shard_map/ppermute | solution.py:196
  7.9 7.0 %collective-permute-start.2 = (bf16[256,128]{1,0:T(8,128)(2,1)}, bf16[256,128]{1,0:T(8,128)(2,1)S(1)}, u32[]{:S(2)}, u32[]{:S(2)}) collective-permute-start(bf16[256,128]{1,0:T(8,128)(2,1)} %get-tuple-element.28), channel_id=1, source_target_pairs={{0,12},{4,0},{8,4},{12,8},{1,13},{5,1},{9,5},{13,9},{2,14},{6,2},{... | collective-permute-start | bytes 196616 | tf_op jit(solution)/shard_map/ppermute | solution.py:196
  11.4 36.6 %copy-start.4 = (s32[1,1,16]{2,1,0:T(1,128)S(1)}, s32[1,1,16]{2,1,0:T(1,128)}, u32[]{:S(2)}) copy-start(s32[1,1,16]{2,1,0:T(1,128)} %param.13) | copy-start | bytes 196
  11.4 8.5 %collective-permute-start.6 = (bf16[1040,128]{1,0:T(8,128)(2,1)}, bf16[1040,128]{1,0:T(8,128)(2,1)S(1)}, u32[]{:S(2)}, u32[]{:S(2)}) collective-permute-start(bf16[1040,128]{1,0:T(8,128)(2,1)} %get-tuple-element.30), channel_id=1, source_target_pairs={{0,4},{4,8},{8,12},{12,0},{1,5},{5,9},{9,13},{13,1},{2,6},{6,10},{... | collective-permute-start | bytes 798728 | tf_op jit(solution)/shard_map/ppermute | solution.py:196
  12.2 20.7 %collective-permute-start.7 = (bf16[1040,128]{1,0:T(8,128)(2,1)}, bf16[1040,128]{1,0:T(8,128)(2,1)S(1)}, u32[]{:S(2)}, u32[]{:S(2)}) collective-permute-start(bf16[1040,128]{1,0:T(8,128)(2,1)} %get-tuple-element.31), channel_id=1, source_target_pairs={{0,8},{4,12},{8,0},{12,4},{1,9},{5,13},{9,1},{13,5},{2,10},{6,14},... | collective-permute-start | bytes 798728 | tf_op jit(solution)/shard_map/ppermute | solution.py:196
  12.2 20.7 %collective-permute-start.8 = (bf16[1040,128]{1,0:T(8,128)(2,1)}, bf16[1040,128]{1,0:T(8,128)(2,1)S(1)}, u32[]{:S(2)}, u32[]{:S(2)}) collective-permute-start(bf16[1040,128]{1,0:T(8,128)(2,1)} %get-tuple-element.32), channel_id=1, source_target_pairs={{0,12},{4,0},{8,4},{12,8},{1,13},{5,1},{9,5},{13,9},{2,14},{6,2},{... | collective-permute-start | bytes 798728 | tf_op jit(solution)/shard_map/ppermute | solution.py:196
  14.9 18.0 %collective-permute-start.3 = (bf16[1024,128]{1,0:T(8,128)(2,1)S(1)}, bf16[1024,128]{1,0:T(8,128)(2,1)S(1)}, u32[]{:S(2)}, u32[]{:S(2)}) collective-permute-start(bf16[1024,128]{1,0:T(8,128)(2,1)S(1)} %constant_dynamic-update-slice_fusion.refs_0_), channel_id=1, source_target_pairs={{0,1},{1,2},{2,3},{3,0},{4,5},{5,6},{6,7},{7,4},{8,9},{9,10},{10,1... | collective-permute-start | bytes 786440 | tf_op jit(solution)/shard_map/ppermute | solution.py:196
  16.3 16.6 %collective-permute-start.4 = (bf16[1024,128]{1,0:T(8,128)(2,1)S(1)}, bf16[1024,128]{1,0:T(8,128)(2,1)S(1)}, u32[]{:S(2)}, u32[]{:S(2)}) collective-permute-start(bf16[1024,128]{1,0:T(8,128)(2,1)S(1)} %constant_dynamic-update-slice_fusion.refs_0_), channel_id=1, source_target_pairs={{0,2},{1,3},{2,0},{3,1},{4,6},{5,7},{6,4},{7,5},{8,10},{9,11},{10,... | collective-permute-start | bytes 786440 | tf_op jit(solution)/shard_map/ppermute | solution.py:196
  20.0 12.9 %collective-permute-start.5 = (bf16[1024,128]{1,0:T(8,128)(2,1)S(1)}, bf16[1024,128]{1,0:T(8,128)(2,1)S(1)}, u32[]{:S(2)}, u32[]{:S(2)}) collective-permute-start(bf16[1024,128]{1,0:T(8,128)(2,1)S(1)} %constant_dynamic-update-slice_fusion.refs_0_), channel_id=1, source_target_pairs={{0,3},{1,0},{2,1},{3,2},{4,7},{5,4},{6,5},{7,6},{8,11},{9,8},{10,9... | collective-permute-start | bytes 786440 | tf_op jit(solution)/shard_map/ppermute | solution.py:196
  32.9 1.0 copy-start
  44.2 10.4 %collective-permute-start.12 = (bf16[1024,128]{1,0:T(8,128)(2,1)S(1)}, bf16[1024,128]{1,0:T(8,128)(2,1)S(1)}, u32[]{:S(2)}, u32[]{:S(2)}) collective-permute-start(bf16[1024,128]{1,0:T(8,128)(2,1)S(1)} %get-tuple-element.38), channel_id=1, source_target_pairs={{0,3},{1,0},{2,1},{3,2},{4,7},{5,4},{6,5},{7,6},{8,11},{9,8},{10,9... | collective-permute-start | bytes 786440 | tf_op jit(solution)/shard_map/ppermute | solution.py:196
  47.0 10.7 %collective-permute-start.13 = (bf16[1024,128]{1,0:T(8,128)(2,1)S(1)}, bf16[1024,128]{1,0:T(8,128)(2,1)S(1)}, u32[]{:S(2)}, u32[]{:S(2)}) collective-permute-start(bf16[1024,128]{1,0:T(8,128)(2,1)S(1)} %get-tuple-element.39), channel_id=1, source_target_pairs={{0,2},{1,3},{2,0},{3,1},{4,6},{5,7},{6,4},{7,5},{8,10},{9,11},{10,... | collective-permute-start | bytes 786440 | tf_op jit(solution)/shard_map/ppermute | solution.py:196
  47.3 15.0 %collective-permute-start.14 = (bf16[1024,128]{1,0:T(8,128)(2,1)S(1)}, bf16[1024,128]{1,0:T(8,128)(2,1)S(1)}, u32[]{:S(2)}, u32[]{:S(2)}) collective-permute-start(bf16[1024,128]{1,0:T(8,128)(2,1)S(1)} %get-tuple-element.40), channel_id=1, source_target_pairs={{0,1},{1,2},{2,3},{3,0},{4,5},{5,6},{6,7},{7,4},{8,9},{9,10},{10,1... | collective-permute-start | bytes 786440 | tf_op jit(solution)/shard_map/ppermute | solution.py:196
  48.1 22.1 %collective-permute-start.10 = (bf16[512,128]{1,0:T(8,128)(2,1)S(1)}, bf16[512,128]{1,0:T(8,128)(2,1)S(1)}, u32[]{:S(2)}, u32[]{:S(2)}) collective-permute-start(bf16[512,128]{1,0:T(8,128)(2,1)S(1)} %get-tuple-element.35), channel_id=1, source_target_pairs={{0,8},{4,12},{8,0},{12,4},{1,9},{5,13},{9,1},{13,5},{2,10},{6,14},... | collective-permute-start | bytes 393224 | tf_op jit(solution)/shard_map/ppermute | solution.py:196
  53.4 16.9 %collective-permute-start.11 = (bf16[512,128]{1,0:T(8,128)(2,1)S(1)}, bf16[512,128]{1,0:T(8,128)(2,1)S(1)}, u32[]{:S(2)}, u32[]{:S(2)}) collective-permute-start(bf16[512,128]{1,0:T(8,128)(2,1)S(1)} %get-tuple-element.36), channel_id=1, source_target_pairs={{0,4},{4,8},{8,12},{12,0},{1,5},{5,9},{9,13},{13,1},{2,6},{6,10},{... | collective-permute-start | bytes 393224 | tf_op jit(solution)/shard_map/ppermute | solution.py:196
  54.6 15.8 %collective-permute-start.9 = (bf16[512,128]{1,0:T(8,128)(2,1)S(1)}, bf16[512,128]{1,0:T(8,128)(2,1)S(1)}, u32[]{:S(2)}, u32[]{:S(2)}) collective-permute-start(bf16[512,128]{1,0:T(8,128)(2,1)S(1)} %get-tuple-element.34), channel_id=1, source_target_pairs={{0,12},{4,0},{8,4},{12,8},{1,13},{5,1},{9,5},{13,9},{2,14},{6,2},{... | collective-permute-start | bytes 393224 | tf_op jit(solution)/shard_map/ppermute | solution.py:196
  63.0 8.1 %collective-permute-start.15 = (bf16[256,128]{1,0:T(8,128)(2,1)S(1)}, bf16[256,128]{1,0:T(8,128)(2,1)S(1)}, u32[]{:S(2)}, u32[]{:S(2)}) collective-permute-start(bf16[256,128]{1,0:T(8,128)(2,1)S(1)} %get-tuple-element.42), channel_id=1, source_target_pairs={{0,12},{4,0},{8,4},{12,8},{1,13},{5,1},{9,5},{13,9},{2,14},{6,2},{... | collective-permute-start | bytes 196616 | tf_op jit(solution)/shard_map/ppermute | solution.py:196
  67.7 6.8 %collective-permute-start.16 = (bf16[256,128]{1,0:T(8,128)(2,1)S(1)}, bf16[256,128]{1,0:T(8,128)(2,1)S(1)}, u32[]{:S(2)}, u32[]{:S(2)}) collective-permute-start(bf16[256,128]{1,0:T(8,128)(2,1)S(1)} %get-tuple-element.43), channel_id=1, source_target_pairs={{0,8},{4,12},{8,0},{12,4},{1,9},{5,13},{9,1},{13,5},{2,10},{6,14},... | collective-permute-start | bytes 196616 | tf_op jit(solution)/shard_map/ppermute | solution.py:196
  70.2 5.0 %collective-permute-start.17 = (bf16[256,128]{1,0:T(8,128)(2,1)S(1)}, bf16[256,128]{1,0:T(8,128)(2,1)S(1)}, u32[]{:S(2)}, u32[]{:S(2)}) collective-permute-start(bf16[256,128]{1,0:T(8,128)(2,1)S(1)} %get-tuple-element.44), channel_id=1, source_target_pairs={{0,4},{4,8},{8,12},{12,0},{1,5},{5,9},{9,13},{13,1},{2,6},{6,10},{... | collective-permute-start | bytes 196616 | tf_op jit(solution)/shard_map/ppermute | solution.py:196

commit v4 on v3

--- a/solution.py
+++ b/solution.py
@@ -14,6 +14,7 @@
 TOK = 128
 CAP = 16
 DOCS = 16
+CODE_ROW = 12
 SLOTS = 4
 BLK = SLOTS * TOK
 QROWS = GROUP * TOK
@@ -25,7 +26,7 @@
 bf16 = jnp.bfloat16
 VMEM = pl.BlockSpec(memory_space=pltpu.VMEM)
 SMEM = pl.BlockSpec(memory_space=pltpu.SMEM)
-SMALL, LARGE, WHOLE = 12 * 2**20, 28 * 2**20, 56 * 2**20
+SMALL, LARGE, WHOLE = 12 * 2**20, 20 * 2**20, 56 * 2**20
 
 
 def aligned(index, unit):
@@ -40,9 +41,17 @@
         outs[slot][TOK:, :] = v_ref[:, head]
 
 
-def split_qd(at_ref, q_ref, o_ref, g_ref, after_ref, *outs):
+def split_qd(at_ref, lens_ref, owners_ref, q_ref, o_ref, g_ref, after_ref, *outs):
     z = at_ref[1]
     lane = lax.broadcasted_iota(jnp.int32, (TOK, HD), 1)
+    position = lax.broadcasted_iota(jnp.int32, (16, TOK), 1)
+    code = jnp.zeros((16, TOK), jnp.int32)
+    start = 0
+    for child in range(16):
+        code = jnp.where(position >= start, owners_ref[child] * CAP + position - start, code)
+        start = start + lens_ref[child]
+    row = lax.broadcasted_iota(jnp.int32, (16, TOK), 0)
+    code = jnp.where(row == CODE_ROW, code, 0).astype(f32)
     for slot in range(SLOTS):
         dest = lax.rem(z + slot, SLOTS)
         terms = jnp.zeros((TOK, HD), f32)
@@ -62,7 +71,7 @@
         packed = jnp.where(
             part == 0, high, jnp.where(part == 1, mid, jnp.where(part == 2, low, 0.0))
         )
-        outs[slot][2 * QROWS :, :] = packed.T[:16, :].astype(bf16)
+        outs[slot][2 * QROWS :, :] = (packed.T[:16, :] + code).astype(bf16)
 
 
 def dot(a, b, dims):
@@ -71,8 +80,8 @@
 
 def attention_grads(at_ref, *refs):
     kv_refs, qd_refs = refs[:4], refs[4:8]
-    dq_refs, dkv_refs = refs[8:12], refs[12:16]
-    qd, kk, vv, kacc, vacc, dqs, delta = refs[16:]
+    dq_ref, code_ref, dkv_refs = refs[8], refs[9], refs[10:14]
+    qd, kk, vv, kacc, vacc, delta = refs[14:]
     y, z = at_ref[0], at_ref[1]
     along_z = [lax.rem(z + SLOTS - s, SLOTS) for s in range(SLOTS)]
     along_y = [aligned(lax.rem(y + SLOTS - k, SLOTS), TOK) for k in range(4)]
@@ -122,39 +131,59 @@
                 vacc[t] += value_part
                 kacc[t] += key_part
             dq = dq + dot(low, kk[t], ((0,), (0,)))
-        dqs[part] = (dq * FACTOR).astype(bf16)
-
-    for s in range(SLOTS):
-        dq_refs[s][...] = dqs[along_z[s]]
+        dq_ref[part] = (dq * FACTOR).astype(bf16)
+        code_ref[part] = qd[part, 2 * QROWS :, :]
+
+    for t in range(SLOTS):
         for k in range(4):
-            keys = kacc[along_z[s], along_y[k], :]
-            dkv_refs[k][s * KV_ROWS : s * KV_ROWS + TOK, :] = (keys * FACTOR).astype(bf16)
-            values = vacc[along_z[s], along_y[k], :]
-            dkv_refs[k][s * KV_ROWS + TOK : (s + 1) * KV_ROWS, :] = values.astype(bf16)
-
-
-def sum_kv(at_ref, own_ref, one_ref, two_ref, three_ref, *outs):
+            keys = kacc[t, along_y[k], :]
+            dkv_refs[k][t * KV_ROWS : t * KV_ROWS + TOK, :] = (keys * FACTOR).astype(bf16)
+            values = vacc[t, along_y[k], :]
+            dkv_refs[k][t * KV_ROWS + TOK : (t + 1) * KV_ROWS, :] = values.astype(bf16)
+
+
+def pick(code_ref, t, heads, out_ref):
+    slot_code = lax.broadcasted_iota(jnp.int32, (DOCS * CAP, TOK), 0)
+    code = code_ref[t].astype(f32)[CODE_ROW : CODE_ROW + 1].astype(jnp.int32)
+    sel = jnp.where(slot_code == code, 1.0, 0.0).astype(bf16)
+    for place, rows in enumerate(heads):
+        picked = dot(sel, rows, ((1,), (0,))).astype(bf16)
+        out_ref[:, t, :, place * HD : (place + 1) * HD] = picked.reshape(DOCS, CAP, HD)
+
+
+def pack_query(at_ref, dq_ref, code_ref, out_ref):
+    for t in range(SLOTS):
+        pick(code_ref, t, [dq_ref[t, h * TOK : (h + 1) * TOK, :] for h in range(GROUP)], out_ref)
+
+
+def pack_kv(at_ref, code_ref, own_ref, one_ref, two_ref, three_ref, out_ref):
     total = own_ref[...].astype(f32) + one_ref[...].astype(f32)
     total = (total + two_ref[...].astype(f32) + three_ref[...].astype(f32)).astype(bf16)
-    for s in range(SLOTS):
-        outs[s][...] = total[s * KV_ROWS : (s + 1) * KV_ROWS]
-
-
-def pack(at_ref, sel_ref, *refs):
-    z = at_ref[1]
-    queries, kvs, out = refs[:4], refs[4:8], refs[8]
-    sel = sel_ref[...]
-
-    def put(rows, place_of):
-        picked = dot(sel, rows, ((1,), (0,))).astype(bf16)
-        out[:, :, aligned(place_of, HD)] = picked.reshape(DOCS, CAP, HD)
-
-    for slot in range(SLOTS):
-        group = lax.rem(z + slot, SLOTS)
-        for h in range(GROUP):
-            put(queries[slot][h * TOK : (h + 1) * TOK, :], group * GROUP + h)
-        put(kvs[slot][:TOK, :], QH + group)
-        put(kvs[slot][TOK:, :], QH + KVH + group)
+    for t in range(SLOTS):
+        first = t * KV_ROWS
+        heads = [total[first : first + TOK], total[first + TOK : first + KV_ROWS]]
+        pick(code_ref, t, heads, out_ref)
+
+
+def place(at_ref, query_ref, kv_ref, out, sem):
+    copies = []
+    for group in range(SLOTS):
+        for source, first, width, to in (
+            (query_ref, 0, QROWS, group * GROUP * HD),
+            (kv_ref, 0, HD, (QH + group) * HD),
+            (kv_ref, HD, HD, (QH + KVH + group) * HD),
+        ):
+            copies.append(
+                pltpu.make_async_copy(
+                    source.at[:, group, :, pl.ds(first, width)],
+                    out.at[:, :, pl.ds(to, width)],
+                    sem.at[len(copies)],
+                )
+            )
+    for copy in copies:
+        copy.start()
+    for copy in copies:
+        copy.wait()
 
 
 ANY = pl.BlockSpec(memory_space=pl.ANY)
@@ -176,17 +205,6 @@
     return jax.ShapeDtypeStruct(shape, dtype)
 
 
-def selection(lens, owners, targets):
-    before = jnp.arange(16)[:, None] < jnp.arange(16)[None, :]
-    starts = jnp.sum(jnp.where(before, lens[:, None], 0), axis=0)
-    owned = owners[None, :] == targets[:, None]
-    start = jnp.sum(jnp.where(owned, starts[None, :], 0), axis=1)
-    size = jnp.sum(jnp.where(owned, lens[None, :], 0), axis=1)
-    slot = jnp.arange(CAP)
-    row = jnp.where(slot[None, :] < size[:, None], start[:, None] + slot[None, :], -1)
-    return (row.reshape(-1)[:, None] == jnp.arange(TOK)[None, :]).astype(bf16)
-
-
 def body(queries, keys, values, outputs, out_grads, lengths, owners):
     y, z = lax.axis_index("y"), lax.axis_index("zl")
     at = jnp.stack([y, z]).astype(jnp.int32)
@@ -198,38 +216,44 @@
     kv = call(split_kv, 2, [shaped(KV_ROWS, HD)] * 4, limit=WHOLE)(at, keys[0], values[0])
     kv_own = jnp.concatenate([kv[0]] + [shift(kv[k], "zl", k) for k in (1, 2, 3)], axis=0)
     kv_all = [kv_own] + [shift(kv_own, "y", k) for k in (1, 2, 3)]
-    qd = call(split_qd, [VMEM] * 3 + [ANY], [shaped(QD_ROWS, HD)] * 4, limit=WHOLE)(
-        at, queries[0], outputs[0], out_grads[0], kv[1]
+    qd = call(split_qd, [SMEM] * 2 + [VMEM] * 3 + [ANY], [shaped(QD_ROWS, HD)] * 4, limit=WHOLE)(
+        at, lengths[0, 0], owners[0, 0], queries[0], outputs[0], out_grads[0], kv[1]
     )
     qd_all = [qd[0]] + [shift(qd[k], "zl", k) for k in (1, 2, 3)]
 
-    sel = selection(lengths[0, 0], owners[0, 0], jnp.arange(DOCS))
-
-    grads = call(
+    dq, codes, *dkv = call(
         attention_grads,
         8,
-        [shaped(QROWS, HD)] * 4 + [shaped(4 * KV_ROWS, HD)] * 4,
+        [shaped(SLOTS, QROWS, HD), shaped(SLOTS, 16, HD)] + [shaped(4 * KV_ROWS, HD)] * 4,
         [
             pltpu.VMEM((SLOTS, QD_ROWS, HD), bf16),
             pltpu.VMEM((4, BLK, HD), bf16),
             pltpu.VMEM((4, BLK, HD), bf16),
             pltpu.VMEM((4, BLK, HD), f32),
             pltpu.VMEM((4, BLK, HD), f32),
-            pltpu.VMEM((SLOTS, QROWS, HD), bf16),
             pltpu.VMEM((TOK, QROWS), jnp.int32),
         ],
         limit=LARGE,
     )(at, *kv_all, *qd_all)
-    dq, dkv = grads[:4], grads[4:]
     dkv_parts = [dkv[0]] + [shift(dkv[k], "y", 4 - k) for k in (1, 2, 3)]
 
-    dq_back = [dq[0]] + [shift(dq[k], "zl", 4 - k) for k in (1, 2, 3)]
-    slots = call(sum_kv, 4, [shaped(KV_ROWS, HD)] * 4)(at, *dkv_parts)
-    dkv_back = [slots[0]] + [shift(slots[k], "zl", 4 - k) for k in (1, 2, 3)]
-    rows = call(pack, 9, shaped(DOCS, CAP, (QH + 2 * KVH) * HD), out_specs=VMEM)(
-        at, sel, *dq_back, *dkv_back
-    )
-    returned = lax.all_to_all(rows, ("zh", "x", "c"), 0, 0, tiled=True)
+    def to_owners(kernel, operands, heads):
+        shape = (DOCS, SLOTS, CAP, heads * HD)
+        rows = call(kernel, len(operands), shaped(*shape), out_specs=VMEM)(at, *operands)
+        rows = rows.reshape(DOCS * SLOTS, CAP, heads * HD)
+        rows = lax.all_to_all(rows, ("zh", "x", "c", "zl"), 0, 0, tiled=True)
+        return rows.reshape(shape)
+
+    query_rows = to_owners(pack_query, [dq, codes], GROUP)
+    query_rows, *dkv_parts = lax.optimization_barrier((query_rows, *dkv_parts))
+    kv_rows = to_owners(pack_kv, [codes, *dkv_parts], 2)
+    returned = call(
+        place,
+        2,
+        shaped(DOCS, CAP, (QH + 2 * KVH) * HD),
+        [pltpu.SemaphoreType.DMA((3 * SLOTS,))],
+        ANY,
+    )(at, query_rows, kv_rows)
     return returned[None, None]
 
 

time: 126 us -> 118 us (0.937); the launches traced: 124 us -> 117 us
  blocking collectives: 46 us -> 23.4 us
  waiting for transfers between devices: 20.7 us -> 39.6 us
  starting transfers between devices: 36.7 us -> 33 us
  Pallas kernels: 16.7 us -> 19.6 us
    all_to_all x1, blocking collectives: 46 us -> 23.4 us  [to_owners(): rows = lax.all_to_all(rows, ('zh', 'x', 'c', 'zl'), 0, 0, tiled=True)]
    ppermute x18 -> x12, starting transfers between devices: 36.7 us -> 16.2 us  [shift(): return lax.ppermute(a, axis, [(i, (i + by) % size) for i in range(size)])]
    all_to_all x0 -> x1, starting transfers between devices: none -> 16.8 us  [to_owners(): rows = lax.all_to_all(rows, ('zh', 'x', 'c', 'zl'), 0, 0, tiled=True)]
    all_to_all x0 -> x1, waiting for transfers between devices: none -> 11.6 us  [to_owners(): rows = lax.all_to_all(rows, ('zh', 'x', 'c', 'zl'), 0, 0, tiled=True)]
    ppermute x18 -> x12, waiting for transfers between devices: 20.7 us -> 27.9 us  [shift(): return lax.ppermute(a, axis, [(i, (i + by) % size) for i in range(size)])]
    pallas_call x4 -> x5, Pallas kernels: 14.9 us -> 17.8 us  [the longest x1 10.4 us: body(): call(attention_grads, 8, [shaped(SLOTS, QROWS, HD), shaped(SLOTS, 16, HD)...]
  transfers between devices with their start and end apart: 18 -> 13, of which waited for: 6 -> 6; matrix products, arithmetic and copies ran while one was open for 0% -> 0% of each run, Pallas kernels for 3% -> 2%
where the time goes in v4:
time: 118 us; the launch traced here: 117 us
  waiting for transfers between devices  39.6 us (34%)
  starting transfers between devices  33 us (28%)
  blocking collectives  23.4 us (20%)
  Pallas kernels  19.6 us (17%)
    ppermute x12, waiting for transfers between devices, shift(): return lax.ppermute(a, axis, [(i, (i + by) % size) for i in range(size)])  27.9 us
    all_to_all x1, blocking collectives, to_owners(): rows = lax.all_to_all(rows, ('zh', 'x', 'c', 'zl'), 0, 0, tiled=True)  23.4 us
    all_to_all x1, starting transfers between devices, to_owners(): rows = lax.all_to_all(rows, ('zh', 'x', 'c', 'zl'), 0, 0, tiled=True)  16.8 us
    ppermute x12, starting transfers between devices, shift(): return lax.ppermute(a, axis, [(i, (i + by) % size) for i in range(size)])  16.2 us
    all_to_all x1, waiting for transfers between devices, to_owners(): rows = lax.all_to_all(rows, ('zh', 'x', 'c', 'zl'), 0, 0, tiled=True)  11.6 us
    pallas_call x1, Pallas kernels, body(): call(attention_grads, 8, [shaped(SLOTS, QROWS, HD), shaped(SLOTS, 16, HD)...  10.4 us
    pallas_call x1, Pallas kernels, body(): call(split_qd, [SMEM] * 2 + [VMEM] * 3 + [ANY], [shaped(QD_ROWS, HD)] * 4...  2.88 us
    pallas_call x2, Pallas kernels, to_owners(): call(kernel, len(operands), shaped(*shape), out_specs=VMEM)(at, *operands)  2.79 us
  transfers between devices with their start and end apart: 13, of which 6 were waited for; matrix products, arithmetic and copies ran while one was open for 0% of the time, Pallas kernels for 2%

profile of v4, /device:TPU:1, one launch (start us, length us, event | category | flops | bytes accessed | tf_op | source)
XLA Modules:
  0.0 117.4 jit_solution(17652629773748023871)
XLA Ops:
  0.0 0.6 pad_add_fusion.at_ref
  0.7 1.7 %shard_map.73 = (bf16[256,128]{1,0:T(8,128)(2,1)}, bf16[256,128]{1,0:T(8,128)(2,1)}, bf16[256,128]{1,0:T(8,128)(2,1)}, bf16[256,128]{1,0:T(8,128)(2,1)}) custom-call(s32[2]{0:T(128)} %pad_add_fusion.at_ref, bf16[128,512]{1,0:T(8,128)(2,1)} %bitcast.20, bf16[128,512]{1,0:T(8,128)(2,1)} %bitcast.21), custom_call_target="tpu_custom_call" | custom-call | tf_op jit(solution)/shard_map/pallas_call | solution.py:216
  2.4 3.8 %collective-permute-start.1 = (bf16[256,128]{1,0:T(8,128)(2,1)}, bf16[256,128]{1,0:T(8,128)(2,1)S(1)}, u32[]{:S(2)}, u32[]{:S(2)}) collective-permute-start(bf16[256,128]{1,0:T(8,128)(2,1)} %get-tuple-element.26), channel_id=1, source_target_pairs={{0,8},{4,12},{8,0},{12,4},{1,9},{5,13},{9,1},{13,5},{2,10},{6,14},... | collective-permute-start | bytes 196616 | tf_op jit(solution)/shard_map/ppermute | solution.py:214
  6.2 1.4 %collective-permute-start.2 = (bf16[256,128]{1,0:T(8,128)(2,1)}, bf16[256,128]{1,0:T(8,128)(2,1)S(1)}, u32[]{:S(2)}, u32[]{:S(2)}) collective-permute-start(bf16[256,128]{1,0:T(8,128)(2,1)} %get-tuple-element.27), channel_id=1, source_target_pairs={{0,12},{4,0},{8,4},{12,8},{1,13},{5,1},{9,5},{13,9},{2,14},{6,2},{... | collective-permute-start | bytes 196616 | tf_op jit(solution)/shard_map/ppermute | solution.py:214
  7.9 2.9 %shard_map.74 = (bf16[1040,128]{1,0:T(8,128)(2,1)}, bf16[1040,128]{1,0:T(8,128)(2,1)}, bf16[1040,128]{1,0:T(8,128)(2,1)}, bf16[1040,128]{1,0:T(8,128)(2,1)}) custom-call(s32[2]{0:T(128)} %pad_add_fusion.at_ref, s32[16]{0:T(128)} %bitcast.22, s32[16]{0:T(128)} %bitcast.23, bf16[128,2048]{1,0:T(8,128)(2,1)} %bitcast.17, bf16[128,2048]{1,0:T(8,128)(2,1)} %bitcast.18, ...), custom_call_target="tpu_custom_call" | custom-call | tf_op jit(solution)/shard_map/pallas_call | solution.py:219
  10.7 1.5 %collective-permute-start.6 = (bf16[1040,128]{1,0:T(8,128)(2,1)}, bf16[1040,128]{1,0:T(8,128)(2,1)S(1)}, u32[]{:S(2)}, u32[]{:S(2)}) collective-permute-start(bf16[1040,128]{1,0:T(8,128)(2,1)} %get-tuple-element.29), channel_id=1, source_target_pairs={{0,4},{4,8},{8,12},{12,0},{1,5},{5,9},{9,13},{13,1},{2,6},{6,10},{... | collective-permute-start | bytes 798728 | tf_op jit(solution)/shard_map/ppermute | solution.py:214
  12.2 1.9 %collective-permute-start.7 = (bf16[1040,128]{1,0:T(8,128)(2,1)}, bf16[1040,128]{1,0:T(8,128)(2,1)S(1)}, u32[]{:S(2)}, u32[]{:S(2)}) collective-permute-start(bf16[1040,128]{1,0:T(8,128)(2,1)} %get-tuple-element.30), channel_id=1, source_target_pairs={{0,8},{4,12},{8,0},{12,4},{1,9},{5,13},{9,1},{13,5},{2,10},{6,14},... | collective-permute-start | bytes 798728 | tf_op jit(solution)/shard_map/ppermute | solution.py:214
  14.5 2.8 %collective-permute-start.5 = (bf16[1024,128]{1,0:T(8,128)(2,1)S(1)}, bf16[1024,128]{1,0:T(8,128)(2,1)S(1)}, u32[]{:S(2)}, u32[]{:S(2)}) collective-permute-start(bf16[1024,128]{1,0:T(8,128)(2,1)S(1)} %constant_dynamic-update-slice_fusion.refs_0_), channel_id=1, source_target_pairs={{0,3},{1,0},{2,1},{3,2},{4,7},{5,4},{6,5},{7,6},{8,11},{9,8},{10,9... | collective-permute-start | bytes 786440 | tf_op jit(solution)/shard_map/ppermute | solution.py:214
  17.6 1.7 %collective-permute-done.6.refs_5_ = bf16[1040,128]{1,0:T(8,128)(2,1)S(1)} collective-permute-done((bf16[1040,128]{1,0:T(8,128)(2,1)}, bf16[1040,128]{1,0:T(8,128)(2,1)S(1)}, u32[]{:S(2)}, u32[]{:S(2)}) %collective-permute-start.6) | collective-permute-done | bytes 266272 | tf_op jit(solution)/shard_map/ppermute | solution.py:214
  19.3 1.3 %collective-permute-start.3 = (bf16[1024,128]{1,0:T(8,128)(2,1)S(1)}, bf16[1024,128]{1,0:T(8,128)(2,1)S(1)}, u32[]{:S(2)}, u32[]{:S(2)}) collective-permute-start(bf16[1024,128]{1,0:T(8,128)(2,1)S(1)} %constant_dynamic-update-slice_fusion.refs_0_), channel_id=1, source_target_pairs={{0,1},{1,2},{2,3},{3,0},{4,5},{5,6},{6,7},{7,4},{8,9},{9,10},{10,1... | collective-permute-start | bytes 786440 | tf_op jit(solution)/shard_map/ppermute | solution.py:214
  20.6 11.9 %collective-permute-done.7.refs_6_ = bf16[1040,128]{1,0:T(8,128)(2,1)S(1)} collective-permute-done((bf16[1040,128]{1,0:T(8,128)(2,1)}, bf16[1040,128]{1,0:T(8,128)(2,1)S(1)}, u32[]{:S(2)}, u32[]{:S(2)}) %collective-permute-start.7) | collective-permute-done | bytes 266272 | tf_op jit(solution)/shard_map/ppermute | solution.py:214
  32.6 0.9 copy-done
  33.5 10.4 %shard_map.75 = (bf16[4,512,128]{2,1,0:T(8,128)(2,1)S(1)}, bf16[4,16,128]{2,1,0:T(8,128)(2,1)S(1)}, bf16[1024,128]{1,0:T(8,128)(2,1)S(1)}, bf16[1024,128]{1,0:T(...) custom-call(s32[2]{0:T(128)S(1)} %copy-done.1, ...), custom_call_target="tpu_custom_call" | custom-call | tf_op jit(solution)/shard_map/pallas_call | solution.py:224
  43.9 1.9 %shard_map.76 = bf16[16,4,16,512]{3,2,1,0:T(8,128)(2,1)} custom-call(s32[2]{0:T(128)S(1)} %copy-done.1, bf16[4,512,128]{2,1,0:T(8,128)(2,1)S(1)} %get-tuple-element.32.dq_ref, bf16[4,16,128]{2,1,0:T(8,128)(2,1)S(1)} %get-tuple-element.33.code_ref), custom_call_target="tpu_custom_call" | custom-call | tf_op jit(solution)/shard_map/pallas_call | solution.py:242
  45.8 16.8 %all-to-all-start = ((bf16[64,16,512]{2,1,0:T(8,128)(2,1)}), bf16[64,16,512]{2,1,0:T(8,128)(2,1)S(1)}, u32[]{:S(2)}, u32[]{:S(2)}) async-start(bf16[64,16,512]{2,1,0:T(8,128)(2,1)} %bitcast.9), calls=%async_computation | async-start | bytes 2097152 | tf_op jit(solution)/shard_map/all_to_all | solution.py:244
  62.7 1.6 %collective-permute-start.9 = (bf16[1024,128]{1,0:T(8,128)(2,1)S(1)}, bf16[1024,128]{1,0:T(8,128)(2,1)S(1)}, u32[]{:S(2)}, u32[]{:S(2)}) collective-permute-start(bf16[1024,128]{1,0:T(8,128)(2,1)S(1)} %get-tuple-element.35), channel_id=1, source_target_pairs={{0,3},{1,0},{2,1},{3,2},{4,7},{5,4},{6,5},{7,6},{8,11},{9,8},{10,9... | collective-permute-start | bytes 786440 | tf_op jit(solution)/shard_map/ppermute | solution.py:214
  64.6 0.7 collective-permute-start.11
  65.3 4.9 %collective-permute-done.9.one_ref = bf16[1024,128]{1,0:T(8,128)(2,1)S(1)} collective-permute-done((bf16[1024,128]{1,0:T(8,128)(2,1)S(1)}, bf16[1024,128]{1,0:T(8,128)(2,1)S(1)}, u32[]{:S(2)}, u32[]{:S(2)}) %collective-permute-start.9) | collective-permute-done | bytes 262176 | tf_op jit(solution)/shard_map/ppermute | solution.py:214
  70.2 2.8 %collective-permute-done.10.two_ref = bf16[1024,128]{1,0:T(8,128)(2,1)S(1)} collective-permute-done((bf16[1024,128]{1,0:T(8,128)(2,1)S(1)}, bf16[1024,128]{1,0:T(8,128)(2,1)S(1)}, u32[]{:S(2)}, u32[]{:S(2)}) %collective-permute-start.10) | collective-permute-done | bytes 262176 | tf_op jit(solution)/shard_map/ppermute | solution.py:214
  72.9 6.7 %collective-permute-done.11.three_ref = bf16[1024,128]{1,0:T(8,128)(2,1)S(1)} collective-permute-done((bf16[1024,128]{1,0:T(8,128)(2,1)S(1)}, bf16[1024,128]{1,0:T(8,128)(2,1)S(1)}, u32[]{:S(2)}, u32[]{:S(2)}) %collective-permute-start.11) | collective-permute-done | bytes 262176 | tf_op jit(solution)/shard_map/ppermute | solution.py:214
  79.6 11.6 %all-to-all-done = bf16[64,16,512]{2,1,0:T(8,128)(2,1)S(1)} async-done(((bf16[64,16,512]{2,1,0:T(8,128)(2,1)}), bf16[64,16,512]{2,1,0:T(8,128)(2,1)S(1)}, u32[]{:S(2)}, u32[]{:S(2)}) %all-to-all-start) | async-done | bytes 1048608 | tf_op jit(solution)/shard_map/all_to_all | solution.py:244
  91.3 0.9 shard_map.77
  92.1 23.4 %all_to_all.10 = bf16[64,16,256]{2,1,0:T(8,128)(2,1)S(1)} all-to-all(bf16[64,16,256]{2,1,0:T(8,128)(2,1)S(1)} %bitcast.15), channel_id=1, replica_groups=mesh['zh'=2,'x'=4,'c'=2,'zl'=4,'y'=4] {'zh','x','c','zl'}, dimensions={0} | all-to-all | bytes 1048576 | tf_op jit(solution)/shard_map/all_to_all | solution.py:244
  115.5 1.8 %shard_map.78 = bf16[16,16,3072]{2,1,0:T(8,128)(2,1)} custom-call(s32[2]{0:T(128)S(1)} %copy-done.1, bf16[16,4,16,512]{3,2,1,0:T(8,128)(2,1)S(1)} %bitcast.14, bf16[16,4,16,256]{3,2,1,0:T(8,128)(2,1)S(1)} %bitcast.16), custom_call_target="tpu_custom_call" | custom-call | tf_op jit(solution)/shard_map/pallas_call | solution.py:250
  (20 shorter events, 1.3 us)
Async XLA Ops:
  0.6 31.9 %copy-start.1 = (s32[2]{0:T(128)S(1)}, s32[2]{0:T(128)}, u32[]{:S(2)}) copy-start(s32[2]{0:T(128)} %pad_add_fusion.at_ref) | copy-start | bytes 28
  2.4 11.7 %copy-start.2 = (bf16[256,128]{1,0:T(8,128)(2,1)S(1)}, bf16[256,128]{1,0:T(8,128)(2,1)}, u32[]{:S(2)}) copy-start(bf16[256,128]{1,0:T(8,128)(2,1)} %get-tuple-element.24) | copy-start | bytes 196612
  2.4 12.0 %collective-permute-start.1 = (bf16[256,128]{1,0:T(8,128)(2,1)}, bf16[256,128]{1,0:T(8,128)(2,1)S(1)}, u32[]{:S(2)}, u32[]{:S(2)}) collective-permute-start(bf16[256,128]{1,0:T(8,128)(2,1)} %get-tuple-element.26), channel_id=1, source_target_pairs={{0,8},{4,12},{8,0},{12,4},{1,9},{5,13},{9,1},{13,5},{2,10},{6,14},... | collective-permute-start | bytes 196616 | tf_op jit(solution)/shard_map/ppermute | solution.py:214
  6.2 8.2 %collective-permute-start.2 = (bf16[256,128]{1,0:T(8,128)(2,1)}, bf16[256,128]{1,0:T(8,128)(2,1)S(1)}, u32[]{:S(2)}, u32[]{:S(2)}) collective-permute-start(bf16[256,128]{1,0:T(8,128)(2,1)} %get-tuple-element.27), channel_id=1, source_target_pairs={{0,12},{4,0},{8,4},{12,8},{1,13},{5,1},{9,5},{13,9},{2,14},{6,2},{... | collective-permute-start | bytes 196616 | tf_op jit(solution)/shard_map/ppermute | solution.py:214
  7.7 6.4 %collective-permute-start = (bf16[256,128]{1,0:T(8,128)(2,1)}, bf16[256,128]{1,0:T(8,128)(2,1)S(1)}, u32[]{:S(2)}, u32[]{:S(2)}) collective-permute-start(bf16[256,128]{1,0:T(8,128)(2,1)} %get-tuple-element.25.after_ref), channel_id=1, source_target_pairs={{0,4},{4,8},{8,12},{12,0},{1,5},{5,9},{9,13},{13,1},{2,6},{6,10},{... | collective-permute-start | bytes 196616 | tf_op jit(solution)/shard_map/ppermute | solution.py:214
  10.7 8.6 %collective-permute-start.6 = (bf16[1040,128]{1,0:T(8,128)(2,1)}, bf16[1040,128]{1,0:T(8,128)(2,1)S(1)}, u32[]{:S(2)}, u32[]{:S(2)}) collective-permute-start(bf16[1040,128]{1,0:T(8,128)(2,1)} %get-tuple-element.29), channel_id=1, source_target_pairs={{0,4},{4,8},{8,12},{12,0},{1,5},{5,9},{9,13},{13,1},{2,6},{6,10},{... | collective-permute-start | bytes 798728 | tf_op jit(solution)/shard_map/ppermute | solution.py:214
  12.2 20.3 %collective-permute-start.7 = (bf16[1040,128]{1,0:T(8,128)(2,1)}, bf16[1040,128]{1,0:T(8,128)(2,1)S(1)}, u32[]{:S(2)}, u32[]{:S(2)}) collective-permute-start(bf16[1040,128]{1,0:T(8,128)(2,1)} %get-tuple-element.30), channel_id=1, source_target_pairs={{0,8},{4,12},{8,0},{12,4},{1,9},{5,13},{9,1},{13,5},{2,10},{6,14},... | collective-permute-start | bytes 798728 | tf_op jit(solution)/shard_map/ppermute | solution.py:214
  14.1 18.4 %collective-permute-start.8 = (bf16[1040,128]{1,0:T(8,128)(2,1)}, bf16[1040,128]{1,0:T(8,128)(2,1)S(1)}, u32[]{:S(2)}, u32[]{:S(2)}) collective-permute-start(bf16[1040,128]{1,0:T(8,128)(2,1)} %get-tuple-element.31), channel_id=1, source_target_pairs={{0,12},{4,0},{8,4},{12,8},{1,13},{5,1},{9,5},{13,9},{2,14},{6,2},{... | collective-permute-start | bytes 798728 | tf_op jit(solution)/shard_map/ppermute | solution.py:214
  14.5 18.1 %collective-permute-start.5 = (bf16[1024,128]{1,0:T(8,128)(2,1)S(1)}, bf16[1024,128]{1,0:T(8,128)(2,1)S(1)}, u32[]{:S(2)}, u32[]{:S(2)}) collective-permute-start(bf16[1024,128]{1,0:T(8,128)(2,1)S(1)} %constant_dynamic-update-slice_fusion.refs_0_), channel_id=1, source_target_pairs={{0,3},{1,0},{2,1},{3,2},{4,7},{5,4},{6,5},{7,6},{8,11},{9,8},{10,9... | collective-permute-start | bytes 786440 | tf_op jit(solution)/shard_map/ppermute | solution.py:214
  17.3 15.3 %collective-permute-start.4 = (bf16[1024,128]{1,0:T(8,128)(2,1)S(1)}, bf16[1024,128]{1,0:T(8,128)(2,1)S(1)}, u32[]{:S(2)}, u32[]{:S(2)}) collective-permute-start(bf16[1024,128]{1,0:T(8,128)(2,1)S(1)} %constant_dynamic-update-slice_fusion.refs_0_), channel_id=1, source_target_pairs={{0,2},{1,3},{2,0},{3,1},{4,6},{5,7},{6,4},{7,5},{8,10},{9,11},{10,... | collective-permute-start | bytes 786440 | tf_op jit(solution)/shard_map/ppermute | solution.py:214
  19.3 13.2 %collective-permute-start.3 = (bf16[1024,128]{1,0:T(8,128)(2,1)S(1)}, bf16[1024,128]{1,0:T(8,128)(2,1)S(1)}, u32[]{:S(2)}, u32[]{:S(2)}) collective-permute-start(bf16[1024,128]{1,0:T(8,128)(2,1)S(1)} %constant_dynamic-update-slice_fusion.refs_0_), channel_id=1, source_target_pairs={{0,1},{1,2},{2,3},{3,0},{4,5},{5,6},{6,7},{7,4},{8,9},{9,10},{10,1... | collective-permute-start | bytes 786440 | tf_op jit(solution)/shard_map/ppermute | solution.py:214
  32.6 1.0 copy-start
  45.8 45.4 %all-to-all-start = ((bf16[64,16,512]{2,1,0:T(8,128)(2,1)}), bf16[64,16,512]{2,1,0:T(8,128)(2,1)S(1)}, u32[]{:S(2)}, u32[]{:S(2)}) async-start(bf16[64,16,512]{2,1,0:T(8,128)(2,1)} %bitcast.9), calls=%async_computation | async-start | bytes 2097152 | tf_op jit(solution)/shard_map/all_to_all | solution.py:244
  62.7 7.5 %collective-permute-start.9 = (bf16[1024,128]{1,0:T(8,128)(2,1)S(1)}, bf16[1024,128]{1,0:T(8,128)(2,1)S(1)}, u32[]{:S(2)}, u32[]{:S(2)}) collective-permute-start(bf16[1024,128]{1,0:T(8,128)(2,1)S(1)} %get-tuple-element.35), channel_id=1, source_target_pairs={{0,3},{1,0},{2,1},{3,2},{4,7},{5,4},{6,5},{7,6},{8,11},{9,8},{10,9... | collective-permute-start | bytes 786440 | tf_op jit(solution)/shard_map/ppermute | solution.py:214
  64.3 8.7 %collective-permute-start.10 = (bf16[1024,128]{1,0:T(8,128)(2,1)S(1)}, bf16[1024,128]{1,0:T(8,128)(2,1)S(1)}, u32[]{:S(2)}, u32[]{:S(2)}) collective-permute-start(bf16[1024,128]{1,0:T(8,128)(2,1)S(1)} %get-tuple-element.36), channel_id=1, source_target_pairs={{0,2},{1,3},{2,0},{3,1},{4,6},{5,7},{6,4},{7,5},{8,10},{9,11},{10,... | collective-permute-start | bytes 786440 | tf_op jit(solution)/shard_map/ppermute | solution.py:214
  64.6 15.0 %collective-permute-start.11 = (bf16[1024,128]{1,0:T(8,128)(2,1)S(1)}, bf16[1024,128]{1,0:T(8,128)(2,1)S(1)}, u32[]{:S(2)}, u32[]{:S(2)}) collective-permute-start(bf16[1024,128]{1,0:T(8,128)(2,1)S(1)} %get-tuple-element.37), channel_id=1, source_target_pairs={{0,1},{1,2},{2,3},{3,0},{4,5},{5,6},{6,7},{7,4},{8,9},{9,10},{10,1... | collective-permute-start | bytes 786440 | tf_op jit(solution)/shard_map/ppermute | solution.py:214

commit v5 on v4

--- a/solution.py
+++ b/solution.py
@@ -33,16 +33,16 @@
     return pl.ds(pl.multiple_of(index * unit, unit), unit)
 
 
-def split_kv(at_ref, k_ref, v_ref, *outs):
-    z = at_ref[1]
+def split_kv(k_ref, v_ref, *outs):
+    z = lax.axis_index("zl")
     for slot in range(SLOTS):
         head = aligned(lax.rem(z + slot, SLOTS), HD)
         outs[slot][:TOK, :] = k_ref[:, head]
         outs[slot][TOK:, :] = v_ref[:, head]
 
 
-def split_qd(at_ref, lens_ref, owners_ref, q_ref, o_ref, g_ref, after_ref, *outs):
-    z = at_ref[1]
+def split_qd(lens_ref, owners_ref, q_ref, o_ref, g_ref, after_ref, *outs):
+    z = lax.axis_index("zl")
     lane = lax.broadcasted_iota(jnp.int32, (TOK, HD), 1)
     position = lax.broadcasted_iota(jnp.int32, (16, TOK), 1)
     code = jnp.zeros((16, TOK), jnp.int32)
@@ -78,11 +78,11 @@
     return lax.dot_general(a, b, (dims, ((), ())), preferred_element_type=f32)
 
 
-def attention_grads(at_ref, *refs):
+def attention_grads(*refs):
     kv_refs, qd_refs = refs[:4], refs[4:8]
     dq_ref, code_ref, dkv_refs = refs[8], refs[9], refs[10:14]
     qd, kk, vv, kacc, vacc, delta = refs[14:]
-    y, z = at_ref[0], at_ref[1]
+    y, z = lax.axis_index("y"), lax.axis_index("zl")
     along_z = [lax.rem(z + SLOTS - s, SLOTS) for s in range(SLOTS)]
     along_y = [aligned(lax.rem(y + SLOTS - k, SLOTS), TOK) for k in range(4)]
     for s in range(SLOTS):
@@ -151,12 +151,12 @@
         out_ref[:, t, :, place * HD : (place + 1) * HD] = picked.reshape(DOCS, CAP, HD)
 
 
-def pack_query(at_ref, dq_ref, code_ref, out_ref):
+def pack_query(dq_ref, code_ref, out_ref):
     for t in range(SLOTS):
         pick(code_ref, t, [dq_ref[t, h * TOK : (h + 1) * TOK, :] for h in range(GROUP)], out_ref)
 
 
-def pack_kv(at_ref, code_ref, own_ref, one_ref, two_ref, three_ref, out_ref):
+def pack_kv(code_ref, own_ref, one_ref, two_ref, three_ref, out_ref):
     total = own_ref[...].astype(f32) + one_ref[...].astype(f32)
     total = (total + two_ref[...].astype(f32) + three_ref[...].astype(f32)).astype(bf16)
     for t in range(SLOTS):
@@ -165,7 +165,7 @@
         pick(code_ref, t, heads, out_ref)
 
 
-def place(at_ref, query_ref, kv_ref, out, sem):
+def place(query_ref, kv_ref, out, sem):
     copies = []
     for group in range(SLOTS):
         for source, first, width, to in (
@@ -193,7 +193,7 @@
     return pl.pallas_call(
         kernel,
         out_shape=outs,
-        in_specs=[SMEM] + ([VMEM] * ins if isinstance(ins, int) else ins),
+        in_specs=[VMEM] * ins if isinstance(ins, int) else ins,
         out_specs=out_specs or [VMEM] * len(outs),
         scratch_shapes=list(scratch),
         input_output_aliases=aliases or {},
@@ -206,18 +206,15 @@
 
 
 def body(queries, keys, values, outputs, out_grads, lengths, owners):
-    y, z = lax.axis_index("y"), lax.axis_index("zl")
-    at = jnp.stack([y, z]).astype(jnp.int32)
-
     def shift(a, axis, by):
         size = lax.axis_size(axis)
         return lax.ppermute(a, axis, [(i, (i + by) % size) for i in range(size)])
 
-    kv = call(split_kv, 2, [shaped(KV_ROWS, HD)] * 4, limit=WHOLE)(at, keys[0], values[0])
+    kv = call(split_kv, 2, [shaped(KV_ROWS, HD)] * 4, limit=WHOLE)(keys[0], values[0])
     kv_own = jnp.concatenate([kv[0]] + [shift(kv[k], "zl", k) for k in (1, 2, 3)], axis=0)
     kv_all = [kv_own] + [shift(kv_own, "y", k) for k in (1, 2, 3)]
     qd = call(split_qd, [SMEM] * 2 + [VMEM] * 3 + [ANY], [shaped(QD_ROWS, HD)] * 4, limit=WHOLE)(
-        at, lengths[0, 0], owners[0, 0], queries[0], outputs[0], out_grads[0], kv[1]
+        lengths[0, 0], owners[0, 0], queries[0], outputs[0], out_grads[0], kv[1]
     )
     qd_all = [qd[0]] + [shift(qd[k], "zl", k) for k in (1, 2, 3)]
 
@@ -234,12 +231,12 @@
             pltpu.VMEM((TOK, QROWS), jnp.int32),
         ],
         limit=LARGE,
-    )(at, *kv_all, *qd_all)
+    )(*kv_all, *qd_all)
     dkv_parts = [dkv[0]] + [shift(dkv[k], "y", 4 - k) for k in (1, 2, 3)]
 
     def to_owners(kernel, operands, heads):
         shape = (DOCS, SLOTS, CAP, heads * HD)
-        rows = call(kernel, len(operands), shaped(*shape), out_specs=VMEM)(at, *operands)
+        rows = call(kernel, len(operands), shaped(*shape), out_specs=VMEM)(*operands)
         rows = rows.reshape(DOCS * SLOTS, CAP, heads * HD)
         rows = lax.all_to_all(rows, ("zh", "x", "c", "zl"), 0, 0, tiled=True)
         return rows.reshape(shape)
@@ -253,7 +250,7 @@
         shaped(DOCS, CAP, (QH + 2 * KVH) * HD),
         [pltpu.SemaphoreType.DMA((3 * SLOTS,))],
         ANY,
-    )(at, query_rows, kv_rows)
+    )(query_rows, kv_rows)
     return returned[None, None]
 
 

time: 118 us -> 115 us (0.975)
  Pallas kernels: 19.6 us -> 17.4 us
  transfers between devices with their start and end apart: 13 -> 13, of which waited for: 6 -> 6; matrix products, arithmetic and copies ran while one was open for 0% -> 0% of each run, Pallas kernels for 2% -> 3%
where the time goes in v5:
time: 115 us
  waiting for transfers between devices  39.6 us (34%)
  starting transfers between devices  33 us (29%)
  blocking collectives  23.4 us (20%)
  Pallas kernels  17.4 us (15%)
    ppermute x12, waiting for transfers between devices, shift(): return lax.ppermute(a, axis, [(i, (i + by) % size) for i in range(size)])  27.9 us
    all_to_all x1, blocking collectives, to_owners(): rows = lax.all_to_all(rows, ('zh', 'x', 'c', 'zl'), 0, 0, tiled=True)  23.4 us
    all_to_all x1, starting transfers between devices, to_owners(): rows = lax.all_to_all(rows, ('zh', 'x', 'c', 'zl'), 0, 0, tiled=True)  16.8 us
    ppermute x12, starting transfers between devices, shift(): return lax.ppermute(a, axis, [(i, (i + by) % size) for i in range(size)])  16.2 us
    all_to_all x1, waiting for transfers between devices, to_owners(): rows = lax.all_to_all(rows, ('zh', 'x', 'c', 'zl'), 0, 0, tiled=True)  11.6 us
    pallas_call x1, Pallas kernels, body(): call(attention_grads, 8, [shaped(SLOTS, QROWS, HD), shaped(SLOTS, 16, HD)...  9.84 us
    pallas_call x1, Pallas kernels, body(): call(split_qd, [SMEM] * 2 + [VMEM] * 3 + [ANY], [shaped(QD_ROWS, HD)] * 4...  2.89 us
  transfers between devices with their start and end apart: 13, of which 6 were waited for; matrix products, arithmetic and copies ran while one was open for 0% of the time, Pallas kernels for 3%

profile of v5, /device:TPU:1, one launch (start us, length us, event | category | flops | bytes accessed | tf_op | source)
XLA Modules:
  0.0 114.6 jit_solution(7409920110011819376)
XLA Ops:
  0.0 1.7 %shard_map.73 = (bf16[256,128]{1,0:T(8,128)(2,1)}, bf16[256,128]{1,0:T(8,128)(2,1)}, bf16[256,128]{1,0:T(8,128)(2,1)}, bf16[256,128]{1,0:T(8,128)(2,1)}) custom-call(bf16[128,512]{1,0:T(8,128)(2,1)} %bitcast.18, bf16[128,512]{1,0:T(8,128)(2,1)} %bitcast.19), custom_call_target="tpu_custom_call" | custom-call | tf_op jit(solution)/shard_map/pallas_call | solution.py:213
  1.7 3.8 %collective-permute-start.1 = (bf16[256,128]{1,0:T(8,128)(2,1)}, bf16[256,128]{1,0:T(8,128)(2,1)S(1)}, u32[]{:S(2)}, u32[]{:S(2)}) collective-permute-start(bf16[256,128]{1,0:T(8,128)(2,1)} %get-tuple-element.26), channel_id=1, source_target_pairs={{0,8},{4,12},{8,0},{12,4},{1,9},{5,13},{9,1},{13,5},{2,10},{6,14},... | collective-permute-start | bytes 196616 | tf_op jit(solution)/shard_map/ppermute | solution.py:211
  5.5 1.4 %collective-permute-start.2 = (bf16[256,128]{1,0:T(8,128)(2,1)}, bf16[256,128]{1,0:T(8,128)(2,1)S(1)}, u32[]{:S(2)}, u32[]{:S(2)}) collective-permute-start(bf16[256,128]{1,0:T(8,128)(2,1)} %get-tuple-element.27), channel_id=1, source_target_pairs={{0,12},{4,0},{8,4},{12,8},{1,13},{5,1},{9,5},{13,9},{2,14},{6,2},{... | collective-permute-start | bytes 196616 | tf_op jit(solution)/shard_map/ppermute | solution.py:211
  7.2 2.9 %shard_map.74 = (bf16[1040,128]{1,0:T(8,128)(2,1)}, bf16[1040,128]{1,0:T(8,128)(2,1)}, bf16[1040,128]{1,0:T(8,128)(2,1)}, bf16[1040,128]{1,0:T(8,128)(2,1)}) custom-call(s32[16]{0:T(128)} %bitcast.20, s32[16]{0:T(128)} %bitcast.21, bf16[128,2048]{1,0:T(8,128)(2,1)} %bitcast.15, bf16[128,2048]{1,0:T(8,128)(2,1)} %bitcast.16, bf16[128,2048]{1,0:T(8,128)(2,1)} %bitcast.17, ...), custom_call_target="tpu_custom_call" | custom-call | tf_op jit(solution)/shard_map/pallas_call | solution.py:216
  10.1 1.5 %collective-permute-start.6 = (bf16[1040,128]{1,0:T(8,128)(2,1)}, bf16[1040,128]{1,0:T(8,128)(2,1)S(1)}, u32[]{:S(2)}, u32[]{:S(2)}) collective-permute-start(bf16[1040,128]{1,0:T(8,128)(2,1)} %get-tuple-element.29), channel_id=1, source_target_pairs={{0,4},{4,8},{8,12},{12,0},{1,5},{5,9},{9,13},{13,1},{2,6},{6,10},{... | collective-permute-start | bytes 798728 | tf_op jit(solution)/shard_map/ppermute | solution.py:211
  11.5 1.9 %collective-permute-start.7 = (bf16[1040,128]{1,0:T(8,128)(2,1)}, bf16[1040,128]{1,0:T(8,128)(2,1)S(1)}, u32[]{:S(2)}, u32[]{:S(2)}) collective-permute-start(bf16[1040,128]{1,0:T(8,128)(2,1)} %get-tuple-element.30), channel_id=1, source_target_pairs={{0,8},{4,12},{8,0},{12,4},{1,9},{5,13},{9,1},{13,5},{2,10},{6,14},... | collective-permute-start | bytes 798728 | tf_op jit(solution)/shard_map/ppermute | solution.py:211
  13.8 2.8 %collective-permute-start.5 = (bf16[1024,128]{1,0:T(8,128)(2,1)S(1)}, bf16[1024,128]{1,0:T(8,128)(2,1)S(1)}, u32[]{:S(2)}, u32[]{:S(2)}) collective-permute-start(bf16[1024,128]{1,0:T(8,128)(2,1)S(1)} %constant_dynamic-update-slice_fusion.refs_0_), channel_id=1, source_target_pairs={{0,3},{1,0},{2,1},{3,2},{4,7},{5,4},{6,5},{7,6},{8,11},{9,8},{10,9... | collective-permute-start | bytes 786440 | tf_op jit(solution)/shard_map/ppermute | solution.py:211
  16.6 0.3 collective-permute-start.4
  16.9 1.7 %collective-permute-done.6.refs_5_ = bf16[1040,128]{1,0:T(8,128)(2,1)S(1)} collective-permute-done((bf16[1040,128]{1,0:T(8,128)(2,1)}, bf16[1040,128]{1,0:T(8,128)(2,1)S(1)}, u32[]{:S(2)}, u32[]{:S(2)}) %collective-permute-start.6) | collective-permute-done | bytes 266272 | tf_op jit(solution)/shard_map/ppermute | solution.py:211
  18.7 1.3 %collective-permute-start.3 = (bf16[1024,128]{1,0:T(8,128)(2,1)S(1)}, bf16[1024,128]{1,0:T(8,128)(2,1)S(1)}, u32[]{:S(2)}, u32[]{:S(2)}) collective-permute-start(bf16[1024,128]{1,0:T(8,128)(2,1)S(1)} %constant_dynamic-update-slice_fusion.refs_0_), channel_id=1, source_target_pairs={{0,1},{1,2},{2,3},{3,0},{4,5},{5,6},{6,7},{7,4},{8,9},{9,10},{10,1... | collective-permute-start | bytes 786440 | tf_op jit(solution)/shard_map/ppermute | solution.py:211
  19.9 11.9 %collective-permute-done.7.refs_6_ = bf16[1040,128]{1,0:T(8,128)(2,1)S(1)} collective-permute-done((bf16[1040,128]{1,0:T(8,128)(2,1)}, bf16[1040,128]{1,0:T(8,128)(2,1)S(1)}, u32[]{:S(2)}, u32[]{:S(2)}) %collective-permute-start.7) | collective-permute-done | bytes 266272 | tf_op jit(solution)/shard_map/ppermute | solution.py:211
  31.9 0.9 copy-done
  32.8 9.8 %shard_map.75 = (bf16[4,512,128]{2,1,0:T(8,128)(2,1)S(1)}, bf16[4,16,128]{2,1,0:T(8,128)(2,1)S(1)}, bf16[1024,128]{1,0:T(8,128)(2,1)S(1)}, bf16[1024,128]{1,0:T(...) custom-call(bf16[1024,128]{1,0:T(8,128)(2,1)S(1)} %constant_dynamic-update-slice_fusion.refs_0_, ...), custom_call_target="tpu_custom_call" | custom-call | tf_op jit(solution)/shard_map/pallas_call | solution.py:221
  42.7 1.4 %shard_map.76 = bf16[16,4,16,512]{3,2,1,0:T(8,128)(2,1)} custom-call(bf16[4,512,128]{2,1,0:T(8,128)(2,1)S(1)} %get-tuple-element.32.dq_ref, bf16[4,16,128]{2,1,0:T(8,128)(2,1)S(1)} %get-tuple-element.33.code_ref), custom_call_target="tpu_custom_call" | custom-call | tf_op jit(solution)/shard_map/pallas_call | solution.py:239
  44.1 16.8 %all-to-all-start = ((bf16[64,16,512]{2,1,0:T(8,128)(2,1)}), bf16[64,16,512]{2,1,0:T(8,128)(2,1)S(1)}, u32[]{:S(2)}, u32[]{:S(2)}) async-start(bf16[64,16,512]{2,1,0:T(8,128)(2,1)} %bitcast.7), calls=%async_computation | async-start | bytes 2097152 | tf_op jit(solution)/shard_map/all_to_all | solution.py:241
  60.9 1.6 %collective-permute-start.9 = (bf16[1024,128]{1,0:T(8,128)(2,1)S(1)}, bf16[1024,128]{1,0:T(8,128)(2,1)S(1)}, u32[]{:S(2)}, u32[]{:S(2)}) collective-permute-start(bf16[1024,128]{1,0:T(8,128)(2,1)S(1)} %get-tuple-element.35), channel_id=1, source_target_pairs={{0,3},{1,0},{2,1},{3,2},{4,7},{5,4},{6,5},{7,6},{8,11},{9,8},{10,9... | collective-permute-start | bytes 786440 | tf_op jit(solution)/shard_map/ppermute | solution.py:211
  62.5 0.3 collective-permute-start.10
  62.9 0.7 collective-permute-start.11
  63.5 4.9 %collective-permute-done.9.one_ref = bf16[1024,128]{1,0:T(8,128)(2,1)S(1)} collective-permute-done((bf16[1024,128]{1,0:T(8,128)(2,1)S(1)}, bf16[1024,128]{1,0:T(8,128)(2,1)S(1)}, u32[]{:S(2)}, u32[]{:S(2)}) %collective-permute-start.9) | collective-permute-done | bytes 262176 | tf_op jit(solution)/shard_map/ppermute | solution.py:211
  68.4 2.7 %collective-permute-done.10.two_ref = bf16[1024,128]{1,0:T(8,128)(2,1)S(1)} collective-permute-done((bf16[1024,128]{1,0:T(8,128)(2,1)S(1)}, bf16[1024,128]{1,0:T(8,128)(2,1)S(1)}, u32[]{:S(2)}, u32[]{:S(2)}) %collective-permute-start.10) | collective-permute-done | bytes 262176 | tf_op jit(solution)/shard_map/ppermute | solution.py:211
  71.2 6.7 %collective-permute-done.11.three_ref = bf16[1024,128]{1,0:T(8,128)(2,1)S(1)} collective-permute-done((bf16[1024,128]{1,0:T(8,128)(2,1)S(1)}, bf16[1024,128]{1,0:T(8,128)(2,1)S(1)}, u32[]{:S(2)}, u32[]{:S(2)}) %collective-permute-start.11) | collective-permute-done | bytes 262176 | tf_op jit(solution)/shard_map/ppermute | solution.py:211
  77.9 11.6 %all-to-all-done = bf16[64,16,512]{2,1,0:T(8,128)(2,1)S(1)} async-done(((bf16[64,16,512]{2,1,0:T(8,128)(2,1)}), bf16[64,16,512]{2,1,0:T(8,128)(2,1)S(1)}, u32[]{:S(2)}, u32[]{:S(2)}) %all-to-all-start) | async-done | bytes 1048608 | tf_op jit(solution)/shard_map/all_to_all | solution.py:241
  89.8 23.4 %all_to_all.10 = bf16[64,16,256]{2,1,0:T(8,128)(2,1)S(1)} all-to-all(bf16[64,16,256]{2,1,0:T(8,128)(2,1)S(1)} %bitcast.13), channel_id=1, replica_groups=mesh['zh'=2,'x'=4,'c'=2,'zl'=4,'y'=4] {'zh','x','c','zl'}, dimensions={0} | all-to-all | bytes 1048576 | tf_op jit(solution)/shard_map/all_to_all | solution.py:241
  113.2 1.2 %shard_map.78 = bf16[16,16,3072]{2,1,0:T(8,128)(2,1)} custom-call(bf16[16,4,16,512]{3,2,1,0:T(8,128)(2,1)S(1)} %bitcast.12, bf16[16,4,16,256]{3,2,1,0:T(8,128)(2,1)S(1)} %bitcast.14), custom_call_target="tpu_custom_call" | custom-call | tf_op jit(solution)/shard_map/pallas_call | solution.py:247
  (17 shorter events, 0.9 us)
Async XLA Ops:
  1.7 11.7 %copy-start.1 = (bf16[256,128]{1,0:T(8,128)(2,1)S(1)}, bf16[256,128]{1,0:T(8,128)(2,1)}, u32[]{:S(2)}) copy-start(bf16[256,128]{1,0:T(8,128)(2,1)} %get-tuple-element.24) | copy-start | bytes 196612
  1.7 12.0 %collective-permute-start.1 = (bf16[256,128]{1,0:T(8,128)(2,1)}, bf16[256,128]{1,0:T(8,128)(2,1)S(1)}, u32[]{:S(2)}, u32[]{:S(2)}) collective-permute-start(bf16[256,128]{1,0:T(8,128)(2,1)} %get-tuple-element.26), channel_id=1, source_target_pairs={{0,8},{4,12},{8,0},{12,4},{1,9},{5,13},{9,1},{13,5},{2,10},{6,14},... | collective-permute-start | bytes 196616 | tf_op jit(solution)/shard_map/ppermute | solution.py:211
  5.5 8.2 %collective-permute-start.2 = (bf16[256,128]{1,0:T(8,128)(2,1)}, bf16[256,128]{1,0:T(8,128)(2,1)S(1)}, u32[]{:S(2)}, u32[]{:S(2)}) collective-permute-start(bf16[256,128]{1,0:T(8,128)(2,1)} %get-tuple-element.27), channel_id=1, source_target_pairs={{0,12},{4,0},{8,4},{12,8},{1,13},{5,1},{9,5},{13,9},{2,14},{6,2},{... | collective-permute-start | bytes 196616 | tf_op jit(solution)/shard_map/ppermute | solution.py:211
  7.0 6.4 %collective-permute-start = (bf16[256,128]{1,0:T(8,128)(2,1)}, bf16[256,128]{1,0:T(8,128)(2,1)S(1)}, u32[]{:S(2)}, u32[]{:S(2)}) collective-permute-start(bf16[256,128]{1,0:T(8,128)(2,1)} %get-tuple-element.25.after_ref), channel_id=1, source_target_pairs={{0,4},{4,8},{8,12},{12,0},{1,5},{5,9},{9,13},{13,1},{2,6},{6,10},{... | collective-permute-start | bytes 196616 | tf_op jit(solution)/shard_map/ppermute | solution.py:211
  10.1 8.6 %collective-permute-start.6 = (bf16[1040,128]{1,0:T(8,128)(2,1)}, bf16[1040,128]{1,0:T(8,128)(2,1)S(1)}, u32[]{:S(2)}, u32[]{:S(2)}) collective-permute-start(bf16[1040,128]{1,0:T(8,128)(2,1)} %get-tuple-element.29), channel_id=1, source_target_pairs={{0,4},{4,8},{8,12},{12,0},{1,5},{5,9},{9,13},{13,1},{2,6},{6,10},{... | collective-permute-start | bytes 798728 | tf_op jit(solution)/shard_map/ppermute | solution.py:211
  11.5 20.3 %collective-permute-start.7 = (bf16[1040,128]{1,0:T(8,128)(2,1)}, bf16[1040,128]{1,0:T(8,128)(2,1)S(1)}, u32[]{:S(2)}, u32[]{:S(2)}) collective-permute-start(bf16[1040,128]{1,0:T(8,128)(2,1)} %get-tuple-element.30), channel_id=1, source_target_pairs={{0,8},{4,12},{8,0},{12,4},{1,9},{5,13},{9,1},{13,5},{2,10},{6,14},... | collective-permute-start | bytes 798728 | tf_op jit(solution)/shard_map/ppermute | solution.py:211
  13.4 18.4 %collective-permute-start.8 = (bf16[1040,128]{1,0:T(8,128)(2,1)}, bf16[1040,128]{1,0:T(8,128)(2,1)S(1)}, u32[]{:S(2)}, u32[]{:S(2)}) collective-permute-start(bf16[1040,128]{1,0:T(8,128)(2,1)} %get-tuple-element.31), channel_id=1, source_target_pairs={{0,12},{4,0},{8,4},{12,8},{1,13},{5,1},{9,5},{13,9},{2,14},{6,2},{... | collective-permute-start | bytes 798728 | tf_op jit(solution)/shard_map/ppermute | solution.py:211
  13.8 18.1 %collective-permute-start.5 = (bf16[1024,128]{1,0:T(8,128)(2,1)S(1)}, bf16[1024,128]{1,0:T(8,128)(2,1)S(1)}, u32[]{:S(2)}, u32[]{:S(2)}) collective-permute-start(bf16[1024,128]{1,0:T(8,128)(2,1)S(1)} %constant_dynamic-update-slice_fusion.refs_0_), channel_id=1, source_target_pairs={{0,3},{1,0},{2,1},{3,2},{4,7},{5,4},{6,5},{7,6},{8,11},{9,8},{10,9... | collective-permute-start | bytes 786440 | tf_op jit(solution)/shard_map/ppermute | solution.py:211
  16.6 15.3 %collective-permute-start.4 = (bf16[1024,128]{1,0:T(8,128)(2,1)S(1)}, bf16[1024,128]{1,0:T(8,128)(2,1)S(1)}, u32[]{:S(2)}, u32[]{:S(2)}) collective-permute-start(bf16[1024,128]{1,0:T(8,128)(2,1)S(1)} %constant_dynamic-update-slice_fusion.refs_0_), channel_id=1, source_target_pairs={{0,2},{1,3},{2,0},{3,1},{4,6},{5,7},{6,4},{7,5},{8,10},{9,11},{10,... | collective-permute-start | bytes 786440 | tf_op jit(solution)/shard_map/ppermute | solution.py:211
  18.7 13.2 %collective-permute-start.3 = (bf16[1024,128]{1,0:T(8,128)(2,1)S(1)}, bf16[1024,128]{1,0:T(8,128)(2,1)S(1)}, u32[]{:S(2)}, u32[]{:S(2)}) collective-permute-start(bf16[1024,128]{1,0:T(8,128)(2,1)S(1)} %constant_dynamic-update-slice_fusion.refs_0_), channel_id=1, source_target_pairs={{0,1},{1,2},{2,3},{3,0},{4,5},{5,6},{6,7},{7,4},{8,9},{9,10},{10,1... | collective-permute-start | bytes 786440 | tf_op jit(solution)/shard_map/ppermute | solution.py:211
  31.9 1.0 copy-start
  44.1 45.4 %all-to-all-start = ((bf16[64,16,512]{2,1,0:T(8,128)(2,1)}), bf16[64,16,512]{2,1,0:T(8,128)(2,1)S(1)}, u32[]{:S(2)}, u32[]{:S(2)}) async-start(bf16[64,16,512]{2,1,0:T(8,128)(2,1)} %bitcast.7), calls=%async_computation | async-start | bytes 2097152 | tf_op jit(solution)/shard_map/all_to_all | solution.py:241
  60.9 7.5 %collective-permute-start.9 = (bf16[1024,128]{1,0:T(8,128)(2,1)S(1)}, bf16[1024,128]{1,0:T(8,128)(2,1)S(1)}, u32[]{:S(2)}, u32[]{:S(2)}) collective-permute-start(bf16[1024,128]{1,0:T(8,128)(2,1)S(1)} %get-tuple-element.35), channel_id=1, source_target_pairs={{0,3},{1,0},{2,1},{3,2},{4,7},{5,4},{6,5},{7,6},{8,11},{9,8},{10,9... | collective-permute-start | bytes 786440 | tf_op jit(solution)/shard_map/ppermute | solution.py:211
  62.5 8.7 %collective-permute-start.10 = (bf16[1024,128]{1,0:T(8,128)(2,1)S(1)}, bf16[1024,128]{1,0:T(8,128)(2,1)S(1)}, u32[]{:S(2)}, u32[]{:S(2)}) collective-permute-start(bf16[1024,128]{1,0:T(8,128)(2,1)S(1)} %get-tuple-element.36), channel_id=1, source_target_pairs={{0,2},{1,3},{2,0},{3,1},{4,6},{5,7},{6,4},{7,5},{8,10},{9,11},{10,... | collective-permute-start | bytes 786440 | tf_op jit(solution)/shard_map/ppermute | solution.py:211
  62.9 15.0 %collective-permute-start.11 = (bf16[1024,128]{1,0:T(8,128)(2,1)S(1)}, bf16[1024,128]{1,0:T(8,128)(2,1)S(1)}, u32[]{:S(2)}, u32[]{:S(2)}) collective-permute-start(bf16[1024,128]{1,0:T(8,128)(2,1)S(1)} %get-tuple-element.37), channel_id=1, source_target_pairs={{0,1},{1,2},{2,3},{3,0},{4,5},{5,6},{6,7},{7,4},{8,9},{9,10},{10,1... | collective-permute-start | bytes 786440 | tf_op jit(solution)/shard_map/ppermute | solution.py:211

commit v6 on v5

--- a/solution.py
+++ b/solution.py
@@ -76,6 +76,10 @@
 
 def dot(a, b, dims):
     return lax.dot_general(a, b, (dims, ((), ())), preferred_element_type=f32)
+
+
+def move(in_ref, out_ref):
+    out_ref[...] = in_ref[...]
 
 
 def attention_grads(*refs):
@@ -212,11 +216,13 @@
 
     kv = call(split_kv, 2, [shaped(KV_ROWS, HD)] * 4, limit=WHOLE)(keys[0], values[0])
     kv_own = jnp.concatenate([kv[0]] + [shift(kv[k], "zl", k) for k in (1, 2, 3)], axis=0)
-    kv_all = [kv_own] + [shift(kv_own, "y", k) for k in (1, 2, 3)]
     qd = call(split_qd, [SMEM] * 2 + [VMEM] * 3 + [ANY], [shaped(QD_ROWS, HD)] * 4, limit=WHOLE)(
         lengths[0, 0], owners[0, 0], queries[0], outputs[0], out_grads[0], kv[1]
     )
-    qd_all = [qd[0]] + [shift(qd[k], "zl", k) for k in (1, 2, 3)]
+    own = call(move, 1, shaped(QD_ROWS, HD), out_specs=VMEM)(qd[0])
+    own, kv_late = lax.optimization_barrier((own, kv_own))
+    kv_all = [kv_own] + [shift(kv_late if k == 1 else kv_own, "y", k) for k in (1, 2, 3)]
+    qd_all = [own] + [shift(qd[k], "zl", k) for k in (1, 2, 3)]
 
     dq, codes, *dkv = call(
         attention_grads,

time: 115 us -> 114 us (level)
  no operation moved by 1% of the time
where the time goes in v6:
time: 114 us
  waiting for transfers between devices  38.5 us (34%)
  starting transfers between devices  33.1 us (29%)
  blocking collectives  23.4 us (21%)
  Pallas kernels  17.4 us (15%)
    ppermute x12, waiting for transfers between devices, shift(): return lax.ppermute(a, axis, [(i, (i + by) % size) for i in range(size)])  26.9 us
    all_to_all x1, blocking collectives, to_owners(): rows = lax.all_to_all(rows, ('zh', 'x', 'c', 'zl'), 0, 0, tiled=True)  23.4 us
    all_to_all x1, starting transfers between devices, to_owners(): rows = lax.all_to_all(rows, ('zh', 'x', 'c', 'zl'), 0, 0, tiled=True)  16.9 us
    ppermute x12, starting transfers between devices, shift(): return lax.ppermute(a, axis, [(i, (i + by) % size) for i in range(size)])  16.2 us
    all_to_all x1, waiting for transfers between devices, to_owners(): rows = lax.all_to_all(rows, ('zh', 'x', 'c', 'zl'), 0, 0, tiled=True)  11.6 us
    pallas_call x1, Pallas kernels, body(): call(attention_grads, 8, [shaped(SLOTS, QROWS, HD), shaped(SLOTS, 16, HD)...  9.84 us
    pallas_call x1, Pallas kernels, body(): call(split_qd, [SMEM] * 2 + [VMEM] * 3 + [ANY], [shaped(QD_ROWS, HD)] * 4...  2.89 us
  transfers between devices with their start and end apart: 13, of which 6 were waited for; matrix products, arithmetic and copies ran while one was open for 0% of the time, Pallas kernels for 3%

profile of v6, /device:TPU:1, one launch (start us, length us, event | category | flops | bytes accessed | tf_op | source)
XLA Modules:
  0.0 113.7 jit_solution(435812163500463775)
XLA Ops:
  0.0 1.7 %shard_map.73 = (bf16[256,128]{1,0:T(8,128)(2,1)}, bf16[256,128]{1,0:T(8,128)(2,1)}, bf16[256,128]{1,0:T(8,128)(2,1)}, bf16[256,128]{1,0:T(8,128)(2,1)}) custom-call(bf16[128,512]{1,0:T(8,128)(2,1)} %bitcast.18, bf16[128,512]{1,0:T(8,128)(2,1)} %bitcast.19), custom_call_target="tpu_custom_call" | custom-call | tf_op jit(solution)/shard_map/pallas_call | solution.py:217
  1.7 3.8 %collective-permute-start.1 = (bf16[256,128]{1,0:T(8,128)(2,1)}, bf16[256,128]{1,0:T(8,128)(2,1)S(1)}, u32[]{:S(2)}, u32[]{:S(2)}) collective-permute-start(bf16[256,128]{1,0:T(8,128)(2,1)} %get-tuple-element.28), channel_id=1, source_target_pairs={{0,8},{4,12},{8,0},{12,4},{1,9},{5,13},{9,1},{13,5},{2,10},{6,14},... | collective-permute-start | bytes 196616 | tf_op jit(solution)/shard_map/ppermute | solution.py:215
  5.5 1.4 %collective-permute-start.2 = (bf16[256,128]{1,0:T(8,128)(2,1)}, bf16[256,128]{1,0:T(8,128)(2,1)S(1)}, u32[]{:S(2)}, u32[]{:S(2)}) collective-permute-start(bf16[256,128]{1,0:T(8,128)(2,1)} %get-tuple-element.29), channel_id=1, source_target_pairs={{0,12},{4,0},{8,4},{12,8},{1,13},{5,1},{9,5},{13,9},{2,14},{6,2},{... | collective-permute-start | bytes 196616 | tf_op jit(solution)/shard_map/ppermute | solution.py:215
  7.2 2.9 %shard_map.74 = (bf16[1040,128]{1,0:T(8,128)(2,1)}, bf16[1040,128]{1,0:T(8,128)(2,1)}, bf16[1040,128]{1,0:T(8,128)(2,1)}, bf16[1040,128]{1,0:T(8,128)(2,1)}) custom-call(s32[16]{0:T(128)} %bitcast.20, s32[16]{0:T(128)} %bitcast.21, bf16[128,2048]{1,0:T(8,128)(2,1)} %bitcast.15, bf16[128,2048]{1,0:T(8,128)(2,1)} %bitcast.16, bf16[128,2048]{1,0:T(8,128)(2,1)} %bitcast.17, ...), custom_call_target="tpu_custom_call" | custom-call | tf_op jit(solution)/shard_map/pallas_call | solution.py:219
  10.1 1.5 %collective-permute-start.6 = (bf16[1040,128]{1,0:T(8,128)(2,1)}, bf16[1040,128]{1,0:T(8,128)(2,1)S(1)}, u32[]{:S(2)}, u32[]{:S(2)}) collective-permute-start(bf16[1040,128]{1,0:T(8,128)(2,1)} %get-tuple-element.33), channel_id=1, source_target_pairs={{0,4},{4,8},{8,12},{12,0},{1,5},{5,9},{9,13},{13,1},{2,6},{6,10},{... | collective-permute-start | bytes 798728 | tf_op jit(solution)/shard_map/ppermute | solution.py:215
  11.5 1.9 %collective-permute-start.7 = (bf16[1040,128]{1,0:T(8,128)(2,1)}, bf16[1040,128]{1,0:T(8,128)(2,1)S(1)}, u32[]{:S(2)}, u32[]{:S(2)}) collective-permute-start(bf16[1040,128]{1,0:T(8,128)(2,1)} %get-tuple-element.34), channel_id=1, source_target_pairs={{0,8},{4,12},{8,0},{12,4},{1,9},{5,13},{9,1},{13,5},{2,10},{6,14},... | collective-permute-start | bytes 798728 | tf_op jit(solution)/shard_map/ppermute | solution.py:215
  13.4 0.9 copy-done
  14.8 2.8 %collective-permute-start.5 = (bf16[1024,128]{1,0:T(8,128)(2,1)S(1)}, bf16[1024,128]{1,0:T(8,128)(2,1)S(1)}, u32[]{:S(2)}, u32[]{:S(2)}) collective-permute-start(bf16[1024,128]{1,0:T(8,128)(2,1)S(1)} %constant_dynamic-update-slice_fusion.refs_0_), channel_id=1, source_target_pairs={{0,3},{1,0},{2,1},{3,2},{4,7},{5,4},{6,5},{7,6},{8,11},{9,8},{10,9... | collective-permute-start | bytes 786440 | tf_op jit(solution)/shard_map/ppermute | solution.py:215
  17.6 0.3 collective-permute-start.4
  17.9 0.7 collective-permute-done.6.refs_5_
  18.7 1.3 %collective-permute-start.3 = (bf16[1024,128]{1,0:T(8,128)(2,1)S(1)}, bf16[1024,128]{1,0:T(8,128)(2,1)S(1)}, u32[]{:S(2)}, u32[]{:S(2)}) collective-permute-start(bf16[1024,128]{1,0:T(8,128)(2,1)S(1)} %constant_dynamic-update-slice_fusion.refs_0_), channel_id=1, source_target_pairs={{0,1},{1,2},{2,3},{3,0},{4,5},{5,6},{6,7},{7,4},{8,9},{9,10},{10,1... | collective-permute-start | bytes 786440 | tf_op jit(solution)/shard_map/ppermute | solution.py:215
  19.9 11.8 %collective-permute-done.7.refs_6_ = bf16[1040,128]{1,0:T(8,128)(2,1)S(1)} collective-permute-done((bf16[1040,128]{1,0:T(8,128)(2,1)}, bf16[1040,128]{1,0:T(8,128)(2,1)S(1)}, u32[]{:S(2)}, u32[]{:S(2)}) %collective-permute-start.7) | collective-permute-done | bytes 266272 | tf_op jit(solution)/shard_map/ppermute | solution.py:215
  31.8 9.8 %shard_map.76 = (bf16[4,512,128]{2,1,0:T(8,128)(2,1)S(1)}, bf16[4,16,128]{2,1,0:T(8,128)(2,1)S(1)}, bf16[1024,128]{1,0:T(8,128)(2,1)S(1)}, bf16[1024,128]{1,0:T(...) custom-call(bf16[1024,128]{1,0:T(8,128)(2,1)S(1)} %constant_dynamic-update-slice_fusion.refs_0_, ...), custom_call_target="tpu_custom_call" | custom-call | tf_op jit(solution)/shard_map/pallas_call | solution.py:227
  41.7 1.4 %shard_map.77 = bf16[16,4,16,512]{3,2,1,0:T(8,128)(2,1)} custom-call(bf16[4,512,128]{2,1,0:T(8,128)(2,1)S(1)} %get-tuple-element.36.dq_ref, bf16[4,16,128]{2,1,0:T(8,128)(2,1)S(1)} %get-tuple-element.37.code_ref), custom_call_target="tpu_custom_call" | custom-call | tf_op jit(solution)/shard_map/pallas_call | solution.py:245
  43.1 16.9 %all-to-all-start = ((bf16[64,16,512]{2,1,0:T(8,128)(2,1)}), bf16[64,16,512]{2,1,0:T(8,128)(2,1)S(1)}, u32[]{:S(2)}, u32[]{:S(2)}) async-start(bf16[64,16,512]{2,1,0:T(8,128)(2,1)} %bitcast.7), calls=%async_computation | async-start | bytes 2097152 | tf_op jit(solution)/shard_map/all_to_all | solution.py:247
  60.0 1.6 %collective-permute-start.9 = (bf16[1024,128]{1,0:T(8,128)(2,1)S(1)}, bf16[1024,128]{1,0:T(8,128)(2,1)S(1)}, u32[]{:S(2)}, u32[]{:S(2)}) collective-permute-start(bf16[1024,128]{1,0:T(8,128)(2,1)S(1)} %get-tuple-element.39), channel_id=1, source_target_pairs={{0,3},{1,0},{2,1},{3,2},{4,7},{5,4},{6,5},{7,6},{8,11},{9,8},{10,9... | collective-permute-start | bytes 786440 | tf_op jit(solution)/shard_map/ppermute | solution.py:215
  61.6 0.3 collective-permute-start.10
  61.9 0.7 collective-permute-start.11
  62.6 4.9 %collective-permute-done.9.one_ref = bf16[1024,128]{1,0:T(8,128)(2,1)S(1)} collective-permute-done((bf16[1024,128]{1,0:T(8,128)(2,1)S(1)}, bf16[1024,128]{1,0:T(8,128)(2,1)S(1)}, u32[]{:S(2)}, u32[]{:S(2)}) %collective-permute-start.9) | collective-permute-done | bytes 262176 | tf_op jit(solution)/shard_map/ppermute | solution.py:215
  67.5 2.7 %collective-permute-done.10.two_ref = bf16[1024,128]{1,0:T(8,128)(2,1)S(1)} collective-permute-done((bf16[1024,128]{1,0:T(8,128)(2,1)S(1)}, bf16[1024,128]{1,0:T(8,128)(2,1)S(1)}, u32[]{:S(2)}, u32[]{:S(2)}) %collective-permute-start.10) | collective-permute-done | bytes 262176 | tf_op jit(solution)/shard_map/ppermute | solution.py:215
  70.2 6.7 %collective-permute-done.11.three_ref = bf16[1024,128]{1,0:T(8,128)(2,1)S(1)} collective-permute-done((bf16[1024,128]{1,0:T(8,128)(2,1)S(1)}, bf16[1024,128]{1,0:T(8,128)(2,1)S(1)}, u32[]{:S(2)}, u32[]{:S(2)}) %collective-permute-start.11) | collective-permute-done | bytes 262176 | tf_op jit(solution)/shard_map/ppermute | solution.py:215
  76.9 11.6 %all-to-all-done = bf16[64,16,512]{2,1,0:T(8,128)(2,1)S(1)} async-done(((bf16[64,16,512]{2,1,0:T(8,128)(2,1)}), bf16[64,16,512]{2,1,0:T(8,128)(2,1)S(1)}, u32[]{:S(2)}, u32[]{:S(2)}) %all-to-all-start) | async-done | bytes 1048608 | tf_op jit(solution)/shard_map/all_to_all | solution.py:247
  88.9 23.4 %all_to_all.10 = bf16[64,16,256]{2,1,0:T(8,128)(2,1)S(1)} all-to-all(bf16[64,16,256]{2,1,0:T(8,128)(2,1)S(1)} %bitcast.13), channel_id=1, replica_groups=mesh['zh'=2,'x'=4,'c'=2,'zl'=4,'y'=4] {'zh','x','c','zl'}, dimensions={0} | all-to-all | bytes 1048576 | tf_op jit(solution)/shard_map/all_to_all | solution.py:247
  112.3 1.2 %shard_map.79 = bf16[16,16,3072]{2,1,0:T(8,128)(2,1)} custom-call(bf16[16,4,16,512]{3,2,1,0:T(8,128)(2,1)S(1)} %bitcast.12, bf16[16,4,16,256]{3,2,1,0:T(8,128)(2,1)S(1)} %bitcast.14), custom_call_target="tpu_custom_call" | custom-call | tf_op jit(solution)/shard_map/pallas_call | solution.py:253
  (18 shorter events, 0.9 us)
Async XLA Ops:
  1.7 12.7 %copy-start.1 = (bf16[256,128]{1,0:T(8,128)(2,1)S(1)}, bf16[256,128]{1,0:T(8,128)(2,1)}, u32[]{:S(2)}) copy-start(bf16[256,128]{1,0:T(8,128)(2,1)} %get-tuple-element.26) | copy-start | bytes 196612
  1.7 13.0 %collective-permute-start.1 = (bf16[256,128]{1,0:T(8,128)(2,1)}, bf16[256,128]{1,0:T(8,128)(2,1)S(1)}, u32[]{:S(2)}, u32[]{:S(2)}) collective-permute-start(bf16[256,128]{1,0:T(8,128)(2,1)} %get-tuple-element.28), channel_id=1, source_target_pairs={{0,8},{4,12},{8,0},{12,4},{1,9},{5,13},{9,1},{13,5},{2,10},{6,14},... | collective-permute-start | bytes 196616 | tf_op jit(solution)/shard_map/ppermute | solution.py:215
  5.5 9.2 %collective-permute-start.2 = (bf16[256,128]{1,0:T(8,128)(2,1)}, bf16[256,128]{1,0:T(8,128)(2,1)S(1)}, u32[]{:S(2)}, u32[]{:S(2)}) collective-permute-start(bf16[256,128]{1,0:T(8,128)(2,1)} %get-tuple-element.29), channel_id=1, source_target_pairs={{0,12},{4,0},{8,4},{12,8},{1,13},{5,1},{9,5},{13,9},{2,14},{6,2},{... | collective-permute-start | bytes 196616 | tf_op jit(solution)/shard_map/ppermute | solution.py:215
  7.0 7.4 %collective-permute-start = (bf16[256,128]{1,0:T(8,128)(2,1)}, bf16[256,128]{1,0:T(8,128)(2,1)S(1)}, u32[]{:S(2)}, u32[]{:S(2)}) collective-permute-start(bf16[256,128]{1,0:T(8,128)(2,1)} %get-tuple-element.27.after_ref), channel_id=1, source_target_pairs={{0,4},{4,8},{8,12},{12,0},{1,5},{5,9},{9,13},{13,1},{2,6},{6,10},{... | collective-permute-start | bytes 196616 | tf_op jit(solution)/shard_map/ppermute | solution.py:215
  10.1 8.6 %collective-permute-start.6 = (bf16[1040,128]{1,0:T(8,128)(2,1)}, bf16[1040,128]{1,0:T(8,128)(2,1)S(1)}, u32[]{:S(2)}, u32[]{:S(2)}) collective-permute-start(bf16[1040,128]{1,0:T(8,128)(2,1)} %get-tuple-element.33), channel_id=1, source_target_pairs={{0,4},{4,8},{8,12},{12,0},{1,5},{5,9},{9,13},{13,1},{2,6},{6,10},{... | collective-permute-start | bytes 798728 | tf_op jit(solution)/shard_map/ppermute | solution.py:215
  11.5 20.3 %collective-permute-start.7 = (bf16[1040,128]{1,0:T(8,128)(2,1)}, bf16[1040,128]{1,0:T(8,128)(2,1)S(1)}, u32[]{:S(2)}, u32[]{:S(2)}) collective-permute-start(bf16[1040,128]{1,0:T(8,128)(2,1)} %get-tuple-element.34), channel_id=1, source_target_pairs={{0,8},{4,12},{8,0},{12,4},{1,9},{5,13},{9,1},{13,5},{2,10},{6,14},... | collective-permute-start | bytes 798728 | tf_op jit(solution)/shard_map/ppermute | solution.py:215
  13.4 1.0 copy-start
  14.4 17.4 %collective-permute-start.8 = (bf16[1040,128]{1,0:T(8,128)(2,1)}, bf16[1040,128]{1,0:T(8,128)(2,1)S(1)}, u32[]{:S(2)}, u32[]{:S(2)}) collective-permute-start(bf16[1040,128]{1,0:T(8,128)(2,1)} %get-tuple-element.35), channel_id=1, source_target_pairs={{0,12},{4,0},{8,4},{12,8},{1,13},{5,1},{9,5},{13,9},{2,14},{6,2},{... | collective-permute-start | bytes 798728 | tf_op jit(solution)/shard_map/ppermute | solution.py:215
  14.8 17.0 %collective-permute-start.5 = (bf16[1024,128]{1,0:T(8,128)(2,1)S(1)}, bf16[1024,128]{1,0:T(8,128)(2,1)S(1)}, u32[]{:S(2)}, u32[]{:S(2)}) collective-permute-start(bf16[1024,128]{1,0:T(8,128)(2,1)S(1)} %constant_dynamic-update-slice_fusion.refs_0_), channel_id=1, source_target_pairs={{0,3},{1,0},{2,1},{3,2},{4,7},{5,4},{6,5},{7,6},{8,11},{9,8},{10,9... | collective-permute-start | bytes 786440 | tf_op jit(solution)/shard_map/ppermute | solution.py:215
  17.6 14.2 %collective-permute-start.4 = (bf16[1024,128]{1,0:T(8,128)(2,1)S(1)}, bf16[1024,128]{1,0:T(8,128)(2,1)S(1)}, u32[]{:S(2)}, u32[]{:S(2)}) collective-permute-start(bf16[1024,128]{1,0:T(8,128)(2,1)S(1)} %constant_dynamic-update-slice_fusion.refs_0_), channel_id=1, source_target_pairs={{0,2},{1,3},{2,0},{3,1},{4,6},{5,7},{6,4},{7,5},{8,10},{9,11},{10,... | collective-permute-start | bytes 786440 | tf_op jit(solution)/shard_map/ppermute | solution.py:215
  18.7 13.2 %collective-permute-start.3 = (bf16[1024,128]{1,0:T(8,128)(2,1)S(1)}, bf16[1024,128]{1,0:T(8,128)(2,1)S(1)}, u32[]{:S(2)}, u32[]{:S(2)}) collective-permute-start(bf16[1024,128]{1,0:T(8,128)(2,1)S(1)} %constant_dynamic-update-slice_fusion.refs_0_), channel_id=1, source_target_pairs={{0,1},{1,2},{2,3},{3,0},{4,5},{5,6},{6,7},{7,4},{8,9},{9,10},{10,1... | collective-permute-start | bytes 786440 | tf_op jit(solution)/shard_map/ppermute | solution.py:215
  43.1 45.5 %all-to-all-start = ((bf16[64,16,512]{2,1,0:T(8,128)(2,1)}), bf16[64,16,512]{2,1,0:T(8,128)(2,1)S(1)}, u32[]{:S(2)}, u32[]{:S(2)}) async-start(bf16[64,16,512]{2,1,0:T(8,128)(2,1)} %bitcast.7), calls=%async_computation | async-start | bytes 2097152 | tf_op jit(solution)/shard_map/all_to_all | solution.py:247
  60.0 7.5 %collective-permute-start.9 = (bf16[1024,128]{1,0:T(8,128)(2,1)S(1)}, bf16[1024,128]{1,0:T(8,128)(2,1)S(1)}, u32[]{:S(2)}, u32[]{:S(2)}) collective-permute-start(bf16[1024,128]{1,0:T(8,128)(2,1)S(1)} %get-tuple-element.39), channel_id=1, source_target_pairs={{0,3},{1,0},{2,1},{3,2},{4,7},{5,4},{6,5},{7,6},{8,11},{9,8},{10,9... | collective-permute-start | bytes 786440 | tf_op jit(solution)/shard_map/ppermute | solution.py:215
  61.6 8.7 %collective-permute-start.10 = (bf16[1024,128]{1,0:T(8,128)(2,1)S(1)}, bf16[1024,128]{1,0:T(8,128)(2,1)S(1)}, u32[]{:S(2)}, u32[]{:S(2)}) collective-permute-start(bf16[1024,128]{1,0:T(8,128)(2,1)S(1)} %get-tuple-element.40), channel_id=1, source_target_pairs={{0,2},{1,3},{2,0},{3,1},{4,6},{5,7},{6,4},{7,5},{8,10},{9,11},{10,... | collective-permute-start | bytes 786440 | tf_op jit(solution)/shard_map/ppermute | solution.py:215
  61.9 15.0 %collective-permute-start.11 = (bf16[1024,128]{1,0:T(8,128)(2,1)S(1)}, bf16[1024,128]{1,0:T(8,128)(2,1)S(1)}, u32[]{:S(2)}, u32[]{:S(2)}) collective-permute-start(bf16[1024,128]{1,0:T(8,128)(2,1)S(1)} %get-tuple-element.41), channel_id=1, source_target_pairs={{0,1},{1,2},{2,3},{3,0},{4,5},{5,6},{6,7},{7,4},{8,9},{9,10},{10,1... | collective-permute-start | bytes 786440 | tf_op jit(solution)/shard_map/ppermute | solution.py:215
